TPU v7x, 32 devices: a whole 2x2x4 slice. The times are simulated.
32 devices in a mesh: dp: 4 (over y, core), fsdp: 8 (over z, x).
Axes of the slice: x: 2, y: 2, z: 4, core: 2. Of those that a mesh axis runs over, the one named last changes fastest.
Arguments:
- decoder_in: bfloat16 [16384, 768], P(('dp', 'fsdp')), may hold values from -6 to 6
- encoder_out: bfloat16 [256, 512, 768], P(('dp', 'fsdp')), may hold values from -6 to 6
- decoder_lengths: int32 [32, 8], P(('dp', 'fsdp')), may hold values from 1 to 128, 512 in all within a row
- encoder_lengths: int32 [256], P(('dp', 'fsdp')), may hold values from 1 to 512, as said below
- norm_gains: float32 [3, 768], P(None, 'fsdp'), may hold values from 0.25 to 1.75
- rel_table: float32 [32, 12], P('dp'), may hold values from -4 to 4
- query_self: float32 [768, 768], P('dp', 'fsdp'), may hold values from -0.109375 to 0.109375
- key_self: float32 [768, 768], P('dp', 'fsdp'), may hold values from -0.109375 to 0.109375
- value_self: float32 [768, 768], P('dp', 'fsdp'), may hold values from -0.21875 to 0.21875
- out_self: float32 [768, 768], P('dp', 'fsdp'), may hold values from -0.4375 to 0.4375
- query_cross: float32 [768, 768], P('dp', 'fsdp'), may hold values from -0.109375 to 0.109375
- key_cross: float32 [768, 768], P('dp', 'fsdp'), may hold values from -0.109375 to 0.109375
- value_cross: float32 [768, 768], P('dp', 'fsdp'), may hold values from -0.21875 to 0.21875
- out_cross: float32 [768, 768], P('dp', 'fsdp'), may hold values from -0.4375 to 0.4375
- feed_in: float32 [768, 3072], P('dp', 'fsdp'), may hold values from -0.21875 to 0.21875
- feed_out: float32 [3072, 768], P('dp', 'fsdp'), may hold values from -0.21875 to 0.21875
- upstream: bfloat16 [16384, 768], P(('dp', 'fsdp')), may hold values from -12 to 12
Outputs:
- decoder_out: bfloat16 [16384, 768], P(('dp', 'fsdp'))
- decoder_gradient: bfloat16 [16384, 768], P(('dp', 'fsdp'))
- encoder_gradient: bfloat16 [256, 512, 768], P(('dp', 'fsdp'))
- gains_gradient: float32 [3, 768], P(None, 'fsdp')
- table_gradient: float32 [32, 12], P('dp')
- query_self_gradient: float32 [768, 768], P('dp', 'fsdp')
- key_self_gradient: float32 [768, 768], P('dp', 'fsdp')
- value_self_gradient: float32 [768, 768], P('dp', 'fsdp')
- out_self_gradient: float32 [768, 768], P('dp', 'fsdp')
- query_cross_gradient: float32 [768, 768], P('dp', 'fsdp')
- key_cross_gradient: float32 [768, 768], P('dp', 'fsdp')
- value_cross_gradient: float32 [768, 768], P('dp', 'fsdp')
- out_cross_gradient: float32 [768, 768], P('dp', 'fsdp')
- feed_in_gradient: float32 [768, 3072], P('dp', 'fsdp')
- feed_out_gradient: float32 [3072, 768], P('dp', 'fsdp')
Inputs may be any that keep to these rules, and one draw needn't show every extreme that they name: `decoder_lengths`: in each row the 8 lengths sum to 512. `encoder_lengths`: in every row one of its 8 examples has all 512 encoder positions valid.
All inputs are finite; a program needn't handle non-finite values.
Results may differ from a plain program's by a relative error of at most 0.025.
The roundings to bfloat16 on the way count: a program that leaves them out, or rounds other values in their place, can miss the bound.
Values may be sent and summed in bfloat16 or wider, within the bound.
A program may use at most 512 MiB of HBM per device.

v0:
```python
from functools import partial
import math

import jax
import jax.numpy as jnp
from jax import lax
from jax.sharding import PartitionSpec as P

HEADS = 12
HEAD_DIM = 64
BUCKETS = 32
MAX_DIST = 128


epsilon = 1e-06


def rms_norm(hidden, gain_row):
    factor = lax.rsqrt(jnp.mean(hidden * hidden, axis=-1, keepdims=True) + epsilon)
    return hidden * factor * gain_row


def bucket_of(distance):
    half_count = BUCKETS // 2
    counted = jnp.zeros_like(distance)
    for section_index in range(1, half_count):
        edge_at = int(
            math.ceil(half_count * (MAX_DIST / half_count) ** (section_index / half_count))
        )
        counted = counted + (distance >= edge_at).astype(jnp.int32)
    return jnp.where(distance < half_count, distance, half_count + counted)


def bias_build(table_full, length):
    distance = jnp.arange(length, dtype=jnp.int32)
    one_hot = (
        bucket_of(distance)[:, None] == jnp.arange(BUCKETS, dtype=jnp.int32)[None, :]
    ).astype(jnp.float32)
    by_distance = jnp.dot(
        one_hot, table_full, precision=lax.Precision.HIGHEST, preferred_element_type=jnp.float32
    ).T
    head_count = by_distance.shape[0]
    widened = jnp.concatenate(
        [by_distance[:, ::-1], jnp.zeros((head_count, length), jnp.float32)], axis=1
    )
    repeated = jnp.tile(widened, (1, length))[:, : length * (2 * length - 1)]
    return repeated.reshape(head_count, length, 2 * length - 1)[:, :, length - 1 :]


def project(source, matrix):
    return jnp.dot(source, matrix, preferred_element_type=jnp.float32)


def back_project(delta_rows, matrix):
    return jnp.einsum("ti,di->td", delta_rows, matrix, preferred_element_type=jnp.float32)


def outer_sum(left_rows, right_rows):
    return jnp.einsum("ti,tj->ij", left_rows, right_rows, preferred_element_type=jnp.float32)


def score_block(query_rows, key_rows):
    return jnp.einsum("qhd,khd->hqk", query_rows, key_rows, preferred_element_type=jnp.float32)


def softmax_parts(scores, visible):
    shown_keys = visible[None, :, :]
    any_shown = jnp.any(shown_keys, axis=-1, keepdims=True)
    row_max = jnp.max(jnp.where(shown_keys, scores, -jnp.inf), axis=-1, keepdims=True)
    row_max = jnp.where(any_shown, row_max, 0.0)
    raised = jnp.where(shown_keys, jnp.exp(scores - row_max), 0.0)
    row_total = jnp.where(any_shown, jnp.sum(raised, axis=-1, keepdims=True), 1.0)
    return (raised / row_total, row_max, row_total)


def probs_again(scores, visible, row_max, row_total):
    return jnp.where(visible[None, :, :], jnp.exp(scores - row_max), 0.0) / row_total


def mix_values(attention, value_rows):
    return jnp.einsum(
        "hqk,khd->qhd",
        attention.astype(jnp.bfloat16),
        value_rows,
        preferred_element_type=jnp.float32,
    )


def attention_back(query_rows, key_rows, value_rows, attention, delta_rows):
    delta_attention = jnp.einsum(
        "qhd,khd->hqk", delta_rows, value_rows, preferred_element_type=jnp.float32
    )
    delta_values = jnp.einsum(
        "hqk,qhd->khd",
        attention.astype(jnp.bfloat16),
        delta_rows,
        preferred_element_type=jnp.float32,
    )
    delta_scores = attention * (
        delta_attention - jnp.sum(delta_attention * attention, axis=-1, keepdims=True)
    )
    low_scores = delta_scores.astype(jnp.bfloat16)
    delta_queries = jnp.einsum(
        "hqk,khd->qhd", low_scores, key_rows, preferred_element_type=jnp.float32
    )
    delta_keys = jnp.einsum(
        "hqk,qhd->khd", low_scores, query_rows, preferred_element_type=jnp.float32
    )
    return (delta_queries, delta_keys, delta_values, delta_scores)


def forward_pass(decoder_rows, encoder_flat, segment, valid_keys, gains_full, table_full, matrices):
    (
        query_self,
        key_self,
        value_self,
        out_self,
        query_cross,
        key_cross,
        value_cross,
        out_cross,
        feed_in,
        feed_out,
    ) = matrices
    row_count, length = segment.shape
    example_count, key_length = (valid_keys.shape[1], valid_keys.shape[2])
    inner_width = HEADS * HEAD_DIM
    places = jnp.arange(length, dtype=jnp.int32)
    causal = places[:, None] >= places[None, :]
    bias_full = bias_build(table_full, length)
    normed_one = rms_norm(decoder_rows, gains_full[0]).astype(jnp.bfloat16)
    queries_one = (
        project(normed_one, query_self)
        .astype(jnp.bfloat16)
        .reshape(row_count, length, HEADS, HEAD_DIM)
    )
    keys_one = (
        project(normed_one, key_self)
        .astype(jnp.bfloat16)
        .reshape(row_count, length, HEADS, HEAD_DIM)
    )
    values_one = (
        project(normed_one, value_self)
        .astype(jnp.bfloat16)
        .reshape(row_count, length, HEADS, HEAD_DIM)
    )

    def self_row(row_item):
        query_rows, key_rows, value_rows, seg_row = row_item
        visible = causal & (seg_row[:, None] == seg_row[None, :])
        attention, row_max, row_total = softmax_parts(
            score_block(query_rows, key_rows) + bias_full, visible
        )
        return (mix_values(attention, value_rows), row_max, row_total)

    attended, self_max, self_total = lax.map(self_row, (queries_one, keys_one, values_one, segment))
    attended_one = attended.reshape(row_count * length, inner_width).astype(jnp.bfloat16)
    hidden_one = decoder_rows + project(attended_one, out_self)
    normed_two = rms_norm(hidden_one, gains_full[1]).astype(jnp.bfloat16)
    queries_two = (
        project(normed_two, query_cross)
        .astype(jnp.bfloat16)
        .reshape(row_count, length, HEADS, HEAD_DIM)
    )
    keys_two = (
        project(encoder_flat, key_cross)
        .astype(jnp.bfloat16)
        .reshape(row_count, example_count, key_length, HEADS, HEAD_DIM)
    )
    values_two = (
        project(encoder_flat, value_cross)
        .astype(jnp.bfloat16)
        .reshape(row_count, example_count, key_length, HEADS, HEAD_DIM)
    )

    def cross_row(row_item):
        query_rows, key_blocks, value_blocks, seg_row, valid_row = row_item
        attended_row = jnp.zeros((length, HEADS, HEAD_DIM), jnp.float32)
        maxima = []
        totals = []
        for example in range(example_count):
            visible = (seg_row == example)[:, None] & valid_row[example][None, :]
            attention, row_max, row_total = softmax_parts(
                score_block(query_rows, key_blocks[example]), visible
            )
            attended_row = attended_row + mix_values(attention, value_blocks[example])
            maxima.append(row_max)
            totals.append(row_total)
        return (attended_row, jnp.stack(maxima), jnp.stack(totals))

    attended, cross_max, cross_total = lax.map(
        cross_row, (queries_two, keys_two, values_two, segment, valid_keys)
    )
    attended_two = attended.reshape(row_count * length, inner_width).astype(jnp.bfloat16)
    hidden_two = hidden_one + project(attended_two, out_cross)
    normed_three = rms_norm(hidden_two, gains_full[2]).astype(jnp.bfloat16)
    pre_act = project(normed_three, feed_in)
    active = jax.nn.gelu(pre_act, approximate=True).astype(jnp.bfloat16)
    output = hidden_two + project(active, feed_out)
    return (
        hidden_one,
        hidden_two,
        normed_one,
        normed_two,
        normed_three,
        queries_one,
        keys_one,
        values_one,
        self_max,
        self_total,
        attended_one,
        queries_two,
        keys_two,
        values_two,
        cross_max,
        cross_total,
        attended_two,
        pre_act,
        active,
        bias_full,
        output,
    )


def backward_pass(
    saved,
    decoder_rows,
    encoder_flat,
    segment,
    valid_keys,
    gains_full,
    table_full,
    matrices,
    upstream,
):
    (
        hidden_one,
        hidden_two,
        normed_one,
        normed_two,
        normed_three,
        queries_one,
        keys_one,
        values_one,
        self_max,
        self_total,
        attended_one,
        queries_two,
        keys_two,
        values_two,
        cross_max,
        cross_total,
        attended_two,
        pre_act,
        active,
        bias_full,
        output,
    ) = saved
    (
        query_self,
        key_self,
        value_self,
        out_self,
        query_cross,
        key_cross,
        value_cross,
        out_cross,
        feed_in,
        feed_out,
    ) = matrices
    row_count, length = segment.shape
    example_count = valid_keys.shape[1]
    inner_width = HEADS * HEAD_DIM
    places = jnp.arange(length, dtype=jnp.int32)
    causal = places[:, None] >= places[None, :]
    delta_hidden = upstream.astype(jnp.float32)
    feed_out_delta = outer_sum(active, upstream)
    delta_active = back_project(upstream, feed_out)
    gelu_pull = jax.vjp(partial(jax.nn.gelu, approximate=True), pre_act)[1]
    delta_pre = gelu_pull(delta_active)[0].astype(jnp.bfloat16)
    feed_in_delta = outer_sum(normed_three, delta_pre)
    delta_normed = back_project(delta_pre, feed_in)
    delta_input, gain_three = jax.vjp(rms_norm, hidden_two, gains_full[2])[1](delta_normed)
    delta_hidden = delta_hidden + delta_input
    branch_low = delta_hidden.astype(jnp.bfloat16)
    out_cross_delta = outer_sum(attended_two, branch_low)
    delta_attended = (
        back_project(branch_low, out_cross)
        .astype(jnp.bfloat16)
        .reshape(row_count, length, HEADS, HEAD_DIM)
    )

    def cross_back(row_item):
        query_rows, key_blocks, value_blocks, seg_row, valid_row, maxima, totals, delta_rows = (
            row_item
        )
        delta_queries = jnp.zeros(query_rows.shape, jnp.float32)
        key_deltas = []
        value_deltas = []
        for example in range(example_count):
            visible = (seg_row == example)[:, None] & valid_row[example][None, :]
            attention = probs_again(
                score_block(query_rows, key_blocks[example]),
                visible,
                maxima[example],
                totals[example],
            )
            query_part, key_part, value_part, unused_scores = attention_back(
                query_rows, key_blocks[example], value_blocks[example], attention, delta_rows
            )
            delta_queries = delta_queries + query_part
            key_deltas.append(key_part)
            value_deltas.append(value_part)
        return (delta_queries, jnp.stack(key_deltas), jnp.stack(value_deltas))

    delta_queries, delta_keys, delta_values = lax.map(
        cross_back,
        (
            queries_two,
            keys_two,
            values_two,
            segment,
            valid_keys,
            cross_max,
            cross_total,
            delta_attended,
        ),
    )
    queries_low = delta_queries.reshape(-1, inner_width).astype(jnp.bfloat16)
    keys_low = delta_keys.reshape(-1, inner_width).astype(jnp.bfloat16)
    values_low = delta_values.reshape(-1, inner_width).astype(jnp.bfloat16)
    query_cross_delta = outer_sum(normed_two, queries_low)
    key_cross_delta = outer_sum(encoder_flat, keys_low)
    value_cross_delta = outer_sum(encoder_flat, values_low)
    encoder_delta = back_project(keys_low, key_cross) + back_project(values_low, value_cross)
    delta_normed = back_project(queries_low, query_cross)
    delta_input, gain_two = jax.vjp(rms_norm, hidden_one, gains_full[1])[1](delta_normed)
    delta_hidden = delta_hidden + delta_input
    branch_low = delta_hidden.astype(jnp.bfloat16)
    out_self_delta = outer_sum(attended_one, branch_low)
    delta_attended = (
        back_project(branch_low, out_self)
        .astype(jnp.bfloat16)
        .reshape(row_count, length, HEADS, HEAD_DIM)
    )

    def self_back(bias_sum, row_item):
        query_rows, key_rows, value_rows, seg_row, row_max, row_total, delta_rows = row_item
        visible = causal & (seg_row[:, None] == seg_row[None, :])
        attention = probs_again(
            score_block(query_rows, key_rows) + bias_full, visible, row_max, row_total
        )
        query_part, key_part, value_part, score_part = attention_back(
            query_rows, key_rows, value_rows, attention, delta_rows
        )
        return (bias_sum + score_part, (query_part, key_part, value_part))

    bias_sum, self_deltas = lax.scan(
        self_back,
        jnp.zeros(bias_full.shape, jnp.float32),
        (queries_one, keys_one, values_one, segment, self_max, self_total, delta_attended),
    )
    table_delta = jax.vjp(partial(bias_build, length=length), table_full)[1](bias_sum)[0]
    queries_low = self_deltas[0].reshape(-1, inner_width).astype(jnp.bfloat16)
    keys_low = self_deltas[1].reshape(-1, inner_width).astype(jnp.bfloat16)
    values_low = self_deltas[2].reshape(-1, inner_width).astype(jnp.bfloat16)
    query_self_delta = outer_sum(normed_one, queries_low)
    key_self_delta = outer_sum(normed_one, keys_low)
    value_self_delta = outer_sum(normed_one, values_low)
    delta_normed = (
        back_project(queries_low, query_self)
        + back_project(keys_low, key_self)
        + back_project(values_low, value_self)
    )
    delta_input, gain_one = jax.vjp(rms_norm, decoder_rows, gains_full[0])[1](delta_normed)
    decoder_delta = delta_hidden + delta_input
    gains_delta = jnp.stack([gain_one, gain_two, gain_three])
    weight_deltas = (
        query_self_delta,
        key_self_delta,
        value_self_delta,
        out_self_delta,
        query_cross_delta,
        key_cross_delta,
        value_cross_delta,
        out_cross_delta,
        feed_in_delta,
        feed_out_delta,
    )
    return (decoder_delta, encoder_delta, gains_delta, table_delta, weight_deltas)


def body(
    decoder_in,
    encoder_out,
    decoder_lengths,
    encoder_lengths,
    norm_gains,
    rel_table,
    query_self,
    key_self,
    value_self,
    out_self,
    query_cross,
    key_cross,
    value_cross,
    out_cross,
    feed_in,
    feed_out,
    upstream,
):
    row_count, example_count = decoder_lengths.shape
    length = decoder_in.shape[0] // row_count
    key_length = encoder_out.shape[1]
    places = jnp.arange(length, dtype=jnp.int32)
    seg_ends = jnp.cumsum(decoder_lengths, axis=1, dtype=jnp.int32)
    segment = jnp.sum((places[None, :, None] >= seg_ends[:, None, :]).astype(jnp.int32), axis=-1)
    valid_keys = (
        jnp.arange(key_length, dtype=jnp.int32)[None, :] < encoder_lengths[:, None]
    ).reshape(row_count, example_count, key_length)
    decoder_rows = decoder_in.astype(jnp.float32)
    encoder_flat = encoder_out.reshape(-1, encoder_out.shape[2])
    shards = (
        query_self,
        key_self,
        value_self,
        out_self,
        query_cross,
        key_cross,
        value_cross,
        out_cross,
        feed_in,
        feed_out,
    )
    lowered = [shard_part.astype(jnp.bfloat16) for shard_part in shards]
    gains_low = norm_gains.astype(jnp.bfloat16)
    table_low = rel_table.astype(jnp.bfloat16)
    columns = (
        lax.all_gather(lowered[0], "fsdp", axis=1, tiled=True),
        lax.all_gather(lowered[1], "fsdp", axis=1, tiled=True),
        lax.all_gather(lowered[2], "fsdp", axis=1, tiled=True),
        lax.all_gather(lowered[3], "fsdp", axis=1, tiled=True),
        lax.all_gather(lowered[4], "fsdp", axis=1, tiled=True),
        lax.all_gather(lowered[5], "fsdp", axis=1, tiled=True),
        lax.all_gather(lowered[6], "fsdp", axis=1, tiled=True),
        lax.all_gather(lowered[7], "fsdp", axis=1, tiled=True),
        lax.all_gather(lowered[8], "fsdp", axis=1, tiled=True),
        lax.all_gather(lowered[9], "fsdp", axis=1, tiled=True),
        lax.all_gather(gains_low, "fsdp", axis=1, tiled=True),
    )
    gathered = (
        lax.all_gather(columns[0], "dp", axis=0, tiled=True),
        lax.all_gather(columns[1], "dp", axis=0, tiled=True),
        lax.all_gather(columns[2], "dp", axis=0, tiled=True),
        lax.all_gather(columns[3], "dp", axis=0, tiled=True),
        lax.all_gather(columns[4], "dp", axis=0, tiled=True),
        lax.all_gather(columns[5], "dp", axis=0, tiled=True),
        lax.all_gather(columns[6], "dp", axis=0, tiled=True),
        lax.all_gather(columns[7], "dp", axis=0, tiled=True),
        lax.all_gather(columns[8], "dp", axis=0, tiled=True),
        lax.all_gather(columns[9], "dp", axis=0, tiled=True),
        lax.all_gather(table_low, "dp", axis=0, tiled=True),
    )
    matrices = tuple(gathered[:10])
    gains_full = columns[10].astype(jnp.float32)
    table_full = gathered[10].astype(jnp.float32)
    saved = forward_pass(
        decoder_rows, encoder_flat, segment, valid_keys, gains_full, table_full, matrices
    )
    decoder_out = saved[-1].astype(jnp.bfloat16)
    columns_again = (
        lax.all_gather(lowered[0], "fsdp", axis=1, tiled=True),
        lax.all_gather(lowered[1], "fsdp", axis=1, tiled=True),
        lax.all_gather(lowered[2], "fsdp", axis=1, tiled=True),
        lax.all_gather(lowered[3], "fsdp", axis=1, tiled=True),
        lax.all_gather(lowered[4], "fsdp", axis=1, tiled=True),
        lax.all_gather(lowered[5], "fsdp", axis=1, tiled=True),
        lax.all_gather(lowered[6], "fsdp", axis=1, tiled=True),
        lax.all_gather(lowered[7], "fsdp", axis=1, tiled=True),
        lax.all_gather(lowered[8], "fsdp", axis=1, tiled=True),
        lax.all_gather(lowered[9], "fsdp", axis=1, tiled=True),
        lax.all_gather(gains_low, "fsdp", axis=1, tiled=True),
    )
    rows_again = (
        lax.all_gather(columns_again[0], "dp", axis=0, tiled=True),
        lax.all_gather(columns_again[1], "dp", axis=0, tiled=True),
        lax.all_gather(columns_again[2], "dp", axis=0, tiled=True),
        lax.all_gather(columns_again[3], "dp", axis=0, tiled=True),
        lax.all_gather(columns_again[4], "dp", axis=0, tiled=True),
        lax.all_gather(columns_again[5], "dp", axis=0, tiled=True),
        lax.all_gather(columns_again[6], "dp", axis=0, tiled=True),
        lax.all_gather(columns_again[7], "dp", axis=0, tiled=True),
        lax.all_gather(columns_again[8], "dp", axis=0, tiled=True),
        lax.all_gather(columns_again[9], "dp", axis=0, tiled=True),
        lax.all_gather(table_low, "dp", axis=0, tiled=True),
    )
    matrices_back = tuple(rows_again[:10])
    gains_back = columns_again[10].astype(jnp.float32)
    table_back = rows_again[10].astype(jnp.float32)
    saved_back = forward_pass(
        decoder_rows, encoder_flat, segment, valid_keys, gains_back, table_back, matrices_back
    )
    decoder_delta, encoder_delta, gains_delta, table_delta, weight_deltas = backward_pass(
        saved_back,
        decoder_rows,
        encoder_flat,
        segment,
        valid_keys,
        gains_back,
        table_back,
        matrices_back,
        upstream,
    )
    row_sums = (
        lax.psum_scatter(
            weight_deltas[0].astype(jnp.bfloat16), "dp", scatter_dimension=0, tiled=True
        ).astype(jnp.float32),
        lax.psum_scatter(
            weight_deltas[1].astype(jnp.bfloat16), "dp", scatter_dimension=0, tiled=True
        ).astype(jnp.float32),
        lax.psum_scatter(
            weight_deltas[2].astype(jnp.bfloat16), "dp", scatter_dimension=0, tiled=True
        ).astype(jnp.float32),
        lax.psum_scatter(
            weight_deltas[3].astype(jnp.bfloat16), "dp", scatter_dimension=0, tiled=True
        ).astype(jnp.float32),
        lax.psum_scatter(
            weight_deltas[4].astype(jnp.bfloat16), "dp", scatter_dimension=0, tiled=True
        ).astype(jnp.float32),
        lax.psum_scatter(
            weight_deltas[5].astype(jnp.bfloat16), "dp", scatter_dimension=0, tiled=True
        ).astype(jnp.float32),
        lax.psum_scatter(
            weight_deltas[6].astype(jnp.bfloat16), "dp", scatter_dimension=0, tiled=True
        ).astype(jnp.float32),
        lax.psum_scatter(
            weight_deltas[7].astype(jnp.bfloat16), "dp", scatter_dimension=0, tiled=True
        ).astype(jnp.float32),
        lax.psum_scatter(
            weight_deltas[8].astype(jnp.bfloat16), "dp", scatter_dimension=0, tiled=True
        ).astype(jnp.float32),
        lax.psum_scatter(
            weight_deltas[9].astype(jnp.bfloat16), "dp", scatter_dimension=0, tiled=True
        ).astype(jnp.float32),
        lax.psum_scatter(
            table_delta.astype(jnp.bfloat16), "dp", scatter_dimension=0, tiled=True
        ).astype(jnp.float32),
    )
    gains_partial = lax.psum(gains_delta, "dp")
    summed = (
        lax.psum_scatter(row_sums[0], "fsdp", scatter_dimension=1, tiled=True),
        lax.psum_scatter(row_sums[1], "fsdp", scatter_dimension=1, tiled=True),
        lax.psum_scatter(row_sums[2], "fsdp", scatter_dimension=1, tiled=True),
        lax.psum_scatter(row_sums[3], "fsdp", scatter_dimension=1, tiled=True),
        lax.psum_scatter(row_sums[4], "fsdp", scatter_dimension=1, tiled=True),
        lax.psum_scatter(row_sums[5], "fsdp", scatter_dimension=1, tiled=True),
        lax.psum_scatter(row_sums[6], "fsdp", scatter_dimension=1, tiled=True),
        lax.psum_scatter(row_sums[7], "fsdp", scatter_dimension=1, tiled=True),
        lax.psum_scatter(row_sums[8], "fsdp", scatter_dimension=1, tiled=True),
        lax.psum_scatter(row_sums[9], "fsdp", scatter_dimension=1, tiled=True),
        lax.psum_scatter(gains_partial, "fsdp", scatter_dimension=1, tiled=True),
    )
    gains_part = summed[10]
    table_part = lax.psum(row_sums[10], "fsdp")
    return (
        decoder_out,
        decoder_delta.astype(jnp.bfloat16),
        encoder_delta.astype(jnp.bfloat16).reshape(encoder_out.shape),
        gains_part,
        table_part,
        summed[0],
        summed[1],
        summed[2],
        summed[3],
        summed[4],
        summed[5],
        summed[6],
        summed[7],
        summed[8],
        summed[9],
    )


def solution(mesh):
    return jax.shard_map(
        body,
        mesh=mesh,
        in_specs=(
            P(("dp", "fsdp"), None),
            P(("dp", "fsdp"), None, None),
            P(("dp", "fsdp"), None),
            P(("dp", "fsdp")),
            P(None, "fsdp"),
            P("dp", None),
            P("dp", "fsdp"),
            P("dp", "fsdp"),
            P("dp", "fsdp"),
            P("dp", "fsdp"),
            P("dp", "fsdp"),
            P("dp", "fsdp"),
            P("dp", "fsdp"),
            P("dp", "fsdp"),
            P("dp", "fsdp"),
            P("dp", "fsdp"),
            P(("dp", "fsdp"), None),
        ),
        out_specs=(
            P(("dp", "fsdp"), None),
            P(("dp", "fsdp"), None),
            P(("dp", "fsdp"), None, None),
            P(None, "fsdp"),
            P("dp", None),
            P("dp", "fsdp"),
            P("dp", "fsdp"),
            P("dp", "fsdp"),
            P("dp", "fsdp"),
            P("dp", "fsdp"),
            P("dp", "fsdp"),
            P("dp", "fsdp"),
            P("dp", "fsdp"),
            P("dp", "fsdp"),
            P("dp", "fsdp"),
        ),
        check_vma=False,
    )
```

profile of v0, /device:TPU:1, one launch (start us, length us, event | category | flops | bytes accessed | tf_op | source)
XLA Modules:
  0.0 1960.6 jit_solution(18029440314685146357)
XLA Ops:
  8.4 26.2 %all_gather.91 = bf16[192,768]{0,1:T(8,128)(2,1)S(1)} all-gather(bf16[192,96]{0,1:T(8,128)(2,1)S(1)} %copy.355), channel_id=1, replica_groups=mesh['dp'=4,'fsdp'=8] {'fsdp'}, dimensions={1}, use_global_device_ids=true | all-gather | bytes 331776 | tf_op jit(solution)/shard_map/all_gather | solution.py:439
  36.5 24.8 %all_gather.93 = bf16[192,768]{0,1:T(8,128)(2,1)S(1)} all-gather(bf16[192,96]{0,1:T(8,128)(2,1)S(1)} %copy.358), channel_id=1, replica_groups=mesh['dp'=4,'fsdp'=8] {'fsdp'}, dimensions={1}, use_global_device_ids=true | all-gather | bytes 331776 | tf_op jit(solution)/shard_map/all_gather | solution.py:440
  63.3 24.9 %all_gather.89 = bf16[192,768]{0,1:T(8,128)(2,1)S(1)} all-gather(bf16[192,96]{0,1:T(8,128)(2,1)S(1)} %copy.352), channel_id=1, replica_groups=mesh['dp'=4,'fsdp'=8] {'fsdp'}, dimensions={1}, use_global_device_ids=true | all-gather | bytes 331776 | tf_op jit(solution)/shard_map/all_gather | solution.py:441
  90.2 24.6 %all_gather.102 = bf16[192,768]{0,1:T(8,128)(2,1)S(1)} all-gather(bf16[192,96]{0,1:T(8,128)(2,1)S(1)} %copy.370), channel_id=1, replica_groups=mesh['dp'=4,'fsdp'=8] {'fsdp'}, dimensions={1}, use_global_device_ids=true | all-gather | bytes 331776 | tf_op jit(solution)/shard_map/all_gather | solution.py:444
  115.8 24.7 %all_gather.98 = bf16[192,768]{0,1:T(8,128)(2,1)S(1)} all-gather(bf16[192,96]{0,1:T(8,128)(2,1)S(1)} %copy.365), channel_id=1, replica_groups=mesh['dp'=4,'fsdp'=8] {'fsdp'}, dimensions={1}, use_global_device_ids=true | all-gather | bytes 331776 | tf_op jit(solution)/shard_map/all_gather | solution.py:445
  141.6 25.4 %all_gather.96 = bf16[192,768]{0,1:T(8,128)(2,1)S(1)} all-gather(bf16[192,96]{0,1:T(8,128)(2,1)S(1)} %copy.363), channel_id=1, replica_groups=mesh['dp'=4,'fsdp'=8] {'fsdp'}, dimensions={1}, use_global_device_ids=true | all-gather | bytes 331776 | tf_op jit(solution)/shard_map/all_gather | solution.py:442
  168.1 25.1 %all_gather.100 = bf16[192,768]{0,1:T(8,128)(2,1)S(1)} all-gather(bf16[192,96]{0,1:T(8,128)(2,1)S(1)} %copy.367), channel_id=1, replica_groups=mesh['dp'=4,'fsdp'=8] {'fsdp'}, dimensions={1}, use_global_device_ids=true | all-gather | bytes 331776 | tf_op jit(solution)/shard_map/all_gather | solution.py:443
  195.8 25.7 %all_gather.104 = bf16[192,768]{0,1:T(8,128)(2,1)S(1)} all-gather(bf16[192,96]{0,1:T(8,128)(2,1)S(1)} %copy.380), channel_id=1, replica_groups=mesh['dp'=4,'fsdp'=8] {'fsdp'}, dimensions={1}, use_global_device_ids=true | all-gather | bytes 331776 | tf_op jit(solution)/shard_map/all_gather | solution.py:446
  232.3 53.5 %all_gather.95 = bf16[32,12]{1,0:T(8,128)(2,1)S(1)} all-gather(bf16[8,12]{1,0:T(8,128)(2,1)S(1)} %convert_element_type.573), channel_id=1, replica_groups=mesh['dp'=4,'fsdp'=8] {'dp'}, dimensions={0}, use_global_device_ids=true | all-gather | bytes 960 | tf_op jit(solution)/shard_map/all_gather | solution.py:462
  285.9 17.3 all-gather
  304.5 11.6 tile.4
  316.1 11.0 pad.12
  327.1 39.7 %copy.475 = f32[2,8,512,1024]{3,1,2,0:T(8,128)} copy(f32[2,8,512,1024]{3,2,1,0:T(8,128)S(1)} %bitcast.306) | data formatting | bytes 67108864
  366.8 22.6 %slice.328 = f32[12,523776]{1,0:T(8,128)} slice(f32[12,524288]{1,0:T(8,128)} %bitcast.307), slice={[0:12], [0:523776]} | slice | bytes 50282496 | tf_op jit(solution)/shard_map/slice | solution.py:46
  389.4 41.8 %reshape.1326 = f32[12,512,1023]{2,1,0:T(8,128)} reshape(f32[12,523776]{1,0:T(8,128)} %slice.328) | data formatting | bytes 50282496 | tf_op jit(solution)/shard_map/reshape | solution.py:47
  431.2 13.3 slice.329
  444.5 12.6 copy.473
  586.2 8.7 fusion.47
  628.3 8.4 fusion.148
  636.8 19.1 all-gather.32.cloned.1.call-done
  655.8 12.5 fusion.24
  677.3 8.9 bitcast_dynamic-update-slice_fusion.7
  686.3 11.2 multiply_reduce_fusion.1
  697.6 12.0 multiply_reduce_fusion.7
  709.7 8.9 multiply_reduce_fusion.8
  718.7 8.6 multiply_reduce_fusion.6
  727.3 11.2 multiply_reduce_fusion.5
  738.6 11.6 multiply_reduce_fusion.4
  750.2 8.6 multiply_reduce_fusion.3
  759.0 9.0 multiply_reduce_fusion.2
  793.2 10.7 multiply_convert_fusion.6
  807.1 10.8 multiply_convert_fusion.7
  823.1 10.9 multiply_convert_fusion.5
  839.4 10.8 multiply_convert_fusion.4
  855.5 10.8 multiply_convert_fusion.3
  871.6 11.0 multiply_convert_fusion.2
  887.8 10.7 multiply_convert_fusion.1
  921.9 8.7 bitcast_dynamic-update-slice_fusion.2
  938.3 8.9 bitcast_dynamic-update-slice_fusion.1
  957.1 9.5 multiply_reduce_fusion
  966.6 9.9 subtract_multiply_fusion
  1010.6 9.2 fusion.94
  1083.5 8.3 convolution_convert_fusion.2
  1128.6 47.8 %reduce-scatter.62.cloned.1.call-done = bf16[768,768]{1,0:T(8,128)(2,1)} async-done(((bf16[3072,768]{1,0:T(8,128)(2,1)}), bf16[768,768]{1,0:T(8,128)(2,1)}) %reduce-scatter.62.cloned.1.call-update) | async-done | bytes 1179664 | tf_op jit(solution)/shard_map/reduce_scatter | solution.py:542
  1180.6 12.8 copy.474
  1193.4 15.6 pad.7.clone
  1209.0 38.2 %reshape.1332 = f32[12,523776]{1,0:T(8,128)} reshape(f32[12,512,1023]{2,1,0:T(8,128)} %pad.7.clone) | data formatting | bytes 50282496 | tf_op jit(solution)/shard_map/transpose(jvp())/reshape | solution.py:47
  1247.2 12.0 pad.8
  1259.2 35.8 %copy.478 = f32[2,8,512,1024]{3,2,1,0:T(8,128)} copy(f32[2,8,512,1024]{3,1,2,0:T(8,128)S(1)} %bitcast.305) | data formatting | bytes 67108864
  1295.1 9.2 slice_reduce_fusion
  1311.0 18.0 psum.15
  1335.0 9.5 add_convert_fusion.3
  1344.5 8.2 fusion.158
  1352.7 10.2 add_convert_fusion
  1363.7 10.5 psum.16
  1375.8 44.1 %reduce-scatter.70.cloned.1.call-done = f32[96,192]{1,0:T(8,128)} async-done(((f32[768,192]{1,0:T(8,128)}), f32[96,192]{1,0:T(8,128)}) %reduce-scatter.70.cloned.1.call-update) | async-done | bytes 73744
  1421.5 63.0 %reduce-scatter.72.cloned.1.call-done = f32[96,192]{1,0:T(8,128)} async-done(((f32[768,192]{1,0:T(8,128)}), f32[96,192]{1,0:T(8,128)}) %reduce-scatter.72.cloned.1.call-update) | async-done | bytes 73744
  1486.1 63.3 %reduce-scatter.68.cloned.1.call-done = f32[96,192]{1,0:T(8,128)} async-done(((f32[768,192]{1,0:T(8,128)}), f32[96,192]{1,0:T(8,128)}) %reduce-scatter.68.cloned.1.call-update) | async-done | bytes 73744
  1551.1 63.0 %reduce-scatter.66.cloned.1.call-done = f32[96,192]{1,0:T(8,128)} async-done(((f32[768,192]{1,0:T(8,128)}), f32[96,192]{1,0:T(8,128)}) %reduce-scatter.66.cloned.1.call-update) | async-done | bytes 73744
  1615.8 63.4 %reduce-scatter.64.cloned.1.call-done = f32[96,192]{1,0:T(8,128)} async-done(((f32[768,192]{1,0:T(8,128)}), f32[96,192]{1,0:T(8,128)}) %reduce-scatter.64.cloned.1.call-update) | async-done | bytes 73744
  1680.8 62.9 %reduce-scatter.54.cloned.1.call-done = f32[192,96]{0,1:T(8,128)} async-done(((f32[192,768]{0,1:T(8,128)}), f32[192,96]{0,1:T(8,128)}) %reduce-scatter.54.cloned.1.call-update) | async-done | bytes 73744 | tf_op jit(solution)/shard_map/reduce_scatter | solution.py:557
  1745.3 63.5 %reduce-scatter.52.cloned.1.call-done = f32[192,96]{0,1:T(8,128)} async-done(((f32[192,768]{0,1:T(8,128)}), f32[192,96]{0,1:T(8,128)}) %reduce-scatter.52.cloned.1.call-update) | async-done | bytes 73744 | tf_op jit(solution)/shard_map/reduce_scatter | solution.py:556
  1810.4 71.2 %reduce-scatter.80.cloned.1.call-done = f32[96,768]{1,0:T(8,128)} async-done(((f32[768,768]{1,0:T(8,128)}), f32[96,768]{1,0:T(8,128)}) %reduce-scatter.80.cloned.1.call-update) | async-done | bytes 294928
  1881.6 72.0 %reduce-scatter.60.cloned.1.call-done = f32[192,384]{1,0:T(8,128)} async-done(((f32[192,3072]{1,0:T(8,128)}), f32[192,384]{1,0:T(8,128)}) %reduce-scatter.60.cloned.1.call-update) | async-done | bytes 294928 | tf_op jit(solution)/shard_map/reduce_scatter | solution.py:559
  (838 shorter events, 453.5 us)
Async XLA Ops:
  7.2 108.5 %copy-start.159 = (f32[192,96]{1,0:T(8,128)S(1)}, f32[192,96]{1,0:T(8,128)}, u32[]{:S(2)}) copy-start(f32[192,96]{1,0:T(8,128)} %param.29) | copy-start | bytes 221188
  7.2 134.3 %copy-start.160 = (f32[192,96]{1,0:T(8,128)S(1)}, f32[192,96]{1,0:T(8,128)}, u32[]{:S(2)}) copy-start(f32[192,96]{1,0:T(8,128)} %param.26) | copy-start | bytes 221188
  7.2 160.8 %copy-start.161 = (f32[192,96]{1,0:T(8,128)S(1)}, f32[192,96]{1,0:T(8,128)}, u32[]{:S(2)}) copy-start(f32[192,96]{1,0:T(8,128)} %param.27) | copy-start | bytes 221188
  7.2 187.0 %copy-start.130 = (f32[768,96]{0,1:T(8,128)S(1)}, f32[768,96]{0,1:T(8,128)}, u32[]{:S(2)}) copy-start(f32[768,96]{0,1:T(8,128)} %param.32) | copy-start | bytes 884740
  7.2 187.7 %copy-start.131 = (f32[192,384]{1,0:T(8,128)S(1)}, f32[192,384]{1,0:T(8,128)}, u32[]{:S(2)}) copy-start(f32[192,384]{1,0:T(8,128)} %param.31) | copy-start | bytes 884740
  7.2 188.5 %copy-start.162 = (f32[192,96]{1,0:T(8,128)S(1)}, f32[192,96]{1,0:T(8,128)}, u32[]{:S(2)}) copy-start(f32[192,96]{1,0:T(8,128)} %param.30) | copy-start | bytes 221188
  7.2 449.9 %all-gather.16.cloned.1.call-start = ((), (), s32[]{:S(2)}) async-start(), calls=%async_computation.22 | async-start | bytes 1474560 | tf_op jit(solution)/shard_map/all_gather | solution.py:452
  35.5 187.0 %copy-start.205 = (s32[1,8]{1,0:T(1,128)S(1)}, s32[1,8]{1,0:T(1,128)}, u32[]{:S(2)}) copy-start(s32[1,8]{1,0:T(1,128)} %param.19) | copy-start | bytes 100
  35.5 187.8 %copy-start.200 = (s32[8]{0:T(128)S(1)}, s32[8]{0:T(128)}, u32[]{:S(2)}) copy-start(s32[8]{0:T(128)} %param.20) | copy-start | bytes 100
  35.5 424.0 %all-gather.18.cloned.1.call-start = ((), (), s32[]{:S(2)}) async-start(), calls=%async_computation.23 | async-start | bytes 1474560 | tf_op jit(solution)/shard_map/all_gather | solution.py:453
  62.2 400.0 %all-gather.14.cloned.1.call-start = ((), (), s32[]{:S(2)}) async-start(), calls=%async_computation.21 | async-start | bytes 1474560 | tf_op jit(solution)/shard_map/all_gather | solution.py:454
  88.2 143.8 %copy-start.197 = (f32[3,96]{1,0:T(4,128)S(1)}, f32[3,96]{1,0:T(4,128)}, u32[]{:S(2)}) copy-start(f32[3,96]{1,0:T(4,128)} %param.21) | copy-start | bytes 3460
  88.2 143.8 %copy-start.43 = (bf16[512,768]{1,0:T(8,128)(2,1)S(1)}, bf16[512,768]{1,0:T(8,128)(2,1)}, u32[]{:S(2)}) copy-start(bf16[512,768]{1,0:T(8,128)(2,1)} %param.17) | copy-start | bytes 2359300
  89.1 143.2 %copy-start.188 = (f32[8,12]{1,0:T(8,128)S(1)}, f32[8,12]{1,0:T(8,128)}, u32[]{:S(2)}) copy-start(f32[8,12]{1,0:T(8,128)} %param.22) | copy-start | bytes 1156
  89.1 376.7 %all-gather.26.cloned.1.call-start = ((), (), s32[]{:S(2)}) async-start(), calls=%async_computation.27 | async-start | bytes 1474560 | tf_op jit(solution)/shard_map/all_gather | solution.py:457
  115.7 359.9 %all-gather.22.cloned.1.call-start = ((), (), s32[]{:S(2)}) async-start(), calls=%async_computation.25 | async-start | bytes 1474560 | tf_op jit(solution)/shard_map/all_gather | solution.py:458
  141.5 359.7 %all-gather.20.cloned.1.call-start = ((), (), s32[]{:S(2)}) async-start(), calls=%async_computation.24 | async-start | bytes 1474560 | tf_op jit(solution)/shard_map/all_gather | solution.py:455
  167.9 336.5 %all-gather.24.cloned.1.call-start = ((), (), s32[]{:S(2)}) async-start(), calls=%async_computation.26 | async-start | bytes 1474560 | tf_op jit(solution)/shard_map/all_gather | solution.py:456
  194.1 384.3 %all-gather.34.cloned.1.call-start = ((), (), s32[]{:S(2)}) async-start(), calls=%async_computation.31 | async-start | bytes 1327104 | tf_op jit(solution)/shard_map/all_gather | solution.py:448
  194.9 408.4 %all-gather.30.cloned.1.call-start = ((), (), s32[]{:S(2)}) async-start(), calls=%async_computation.29 | async-start | bytes 1327104 | tf_op jit(solution)/shard_map/all_gather | solution.py:447
  195.7 430.0 %all-gather.28.cloned.1.call-start = ((), (), s32[]{:S(2)}) async-start(), calls=%async_computation.28 | async-start | bytes 1474560 | tf_op jit(solution)/shard_map/all_gather | solution.py:459
  222.4 405.9 %all-gather.36.cloned.1.call-start = ((), (), s32[]{:S(2)}) async-start(), calls=%async_computation.32 | async-start | bytes 5898240 | tf_op jit(solution)/shard_map/all_gather | solution.py:461
  222.5 93.6 %copy-start.198 = (s32[512]{0:T(512)}, s32[512]{0:T(512)S(1)}, u32[]{:S(2)}) copy-start(s32[512]{0:T(512)S(1)} %iota_select_fusion) | copy-start | bytes 6148
  223.3 271.4 %copy-start.49 = (pred[512,512]{0,1:T(8,128)(4,1)}, pred[512,512]{0,1:T(8,128)(4,1)S(1)}, u32[]{:S(2)}) copy-start(pred[512,512]{0,1:T(8,128)(4,1)S(1)} %fusion.107) | copy-start | bytes 786436
  232.3 53.6 %copy-start.176 = (f32[512]{0:T(512)}, f32[512]{0:T(512)S(1)}, u32[]{:S(2)}) copy-start(f32[512]{0:T(512)S(1)} %fusion.73) | copy-start | bytes 6148
  232.3 229.9 %copy-start.178 = (f32[512]{0:T(512)}, f32[512]{0:T(512)S(1)}, u32[]{:S(2)}) copy-start(f32[512]{0:T(512)S(1)} %fusion.118) | copy-start | bytes 6148
  303.9 158.3 %copy-start.163 = (f32[768]{0:T(1024)}, f32[768]{0:T(1024)S(1)}, u32[]{:S(2)}) copy-start(f32[768]{0:T(1024)S(1)} %get-tuple-element.293) | copy-start | bytes 9220
  303.9 200.5 %copy-start.165 = (f32[768]{0:T(1024)}, f32[768]{0:T(1024)S(1)}, u32[]{:S(2)}) copy-start(f32[768]{0:T(1024)S(1)} %get-tuple-element.292) | copy-start | bytes 9220
  475.6 73.4 %copy-start.27 = (bf16[512,768]{0,1:T(8,128)(2,1)}, bf16[512,768]{0,1:T(8,128)(2,1)S(1)}, u32[]{:S(2)}) copy-start(bf16[512,768]{0,1:T(8,128)(2,1)S(1)} %get-tuple-element.305) | copy-start | bytes 2359300
  475.6 80.7 %copy-start.25 = (bf16[512,768]{0,1:T(8,128)(2,1)}, bf16[512,768]{0,1:T(8,128)(2,1)S(1)}, u32[]{:S(2)}) copy-start(bf16[512,768]{0,1:T(8,128)(2,1)S(1)} %get-tuple-element.304) | copy-start | bytes 2359300
  509.4 54.0 %copy-start = (bf16[512,768]{0,1:T(8,128)(2,1)}, bf16[512,768]{0,1:T(8,128)(2,1)S(1)}, u32[]{:S(2)}) copy-start(bf16[512,768]{0,1:T(8,128)(2,1)S(1)} %copy.369) | copy-start | bytes 2359300
  521.1 49.5 %copy-start.127 = (f32[12,512]{1,0:T(8,128)}, f32[12,512]{1,0:T(8,128)S(1)}, u32[]{:S(2)}) copy-start(f32[12,512]{1,0:T(8,128)S(1)} %broadcast_select_fusion.15) | copy-start | bytes 73732
  525.7 44.9 %copy-start.154 = (f32[12,512]{1,0:T(8,128)}, f32[12,512]{1,0:T(8,128)S(1)}, u32[]{:S(2)}) copy-start(f32[12,512]{1,0:T(8,128)S(1)} %broadcast_select_fusion.6) | copy-start | bytes 73732
  528.2 50.3 %copy-start.115 = (f32[12,512]{1,0:T(8,128)}, f32[12,512]{1,0:T(8,128)S(1)}, u32[]{:S(2)}) copy-start(f32[12,512]{1,0:T(8,128)S(1)} %broadcast_select_fusion.14) | copy-start | bytes 73732
  551.1 48.0 %copy-start.110 = (f32[12,512]{1,0:T(8,128)}, f32[12,512]{1,0:T(8,128)S(1)}, u32[]{:S(2)}) copy-start(f32[12,512]{1,0:T(8,128)S(1)} %broadcast_select_fusion.11) | copy-start | bytes 73732
  558.3 45.1 %copy-start.108 = (f32[12,512]{1,0:T(8,128)}, f32[12,512]{1,0:T(8,128)S(1)}, u32[]{:S(2)}) copy-start(f32[12,512]{1,0:T(8,128)S(1)} %broadcast_select_fusion.10) | copy-start | bytes 73732
  565.4 120.9 %copy-start.106 = (f32[12,512]{1,0:T(8,128)}, f32[12,512]{1,0:T(8,128)S(1)}, u32[]{:S(2)}) copy-start(f32[12,512]{1,0:T(8,128)S(1)} %broadcast_select_fusion.9) | copy-start | bytes 73732
  578.4 77.4 %all-gather.32.cloned.1.call-start = ((), (), s32[]{:S(2)}) async-start(), calls=%async_computation.30 | async-start | bytes 5898240 | tf_op jit(solution)/shard_map/all_gather | solution.py:460
  603.3 504.3 %reduce-scatter.56.cloned.1.call-start = ((), (), s32[]{:S(2)}) async-start(), calls=%async_computation.40 | async-start | bytes 1474560 | tf_op jit(solution)/shard_map/reduce_scatter | solution.py:536
  628.3 43.5 %copy-start.47 = (f32[512,768]{1,0:T(8,128)}, f32[512,768]{1,0:T(8,128)S(1)}, u32[]{:S(2)}) copy-start(f32[512,768]{1,0:T(8,128)S(1)} %get-tuple-element.347) | copy-start | bytes 4718596
  628.3 43.4 %copy-start.182 = (f32[512]{0:T(512)}, f32[512]{0:T(512)S(1)}, u32[]{:S(2)}) copy-start(f32[512]{0:T(512)S(1)} %fusion.120) | copy-start | bytes 6148
  768.0 341.7 %reduce-scatter.48.cloned.1.call-start = ((), (), s32[]{:S(2)}) async-start(), calls=%async_computation.36 | async-start | bytes 1474560 | tf_op jit(solution)/shard_map/reduce_scatter | solution.py:524
  930.7 181.1 %reduce-scatter.50.cloned.1.call-start = ((), (), s32[]{:S(2)}) async-start(), calls=%async_computation.37 | async-start | bytes 1474560 | tf_op jit(solution)/shard_map/reduce_scatter | solution.py:527
  947.3 166.7 %reduce-scatter.46.cloned.1.call-start = ((), (), s32[]{:S(2)}) async-start(), calls=%async_computation.35 | async-start | bytes 1474560 | tf_op jit(solution)/shard_map/reduce_scatter | solution.py:521
  966.6 149.5 %reduce-scatter.44.cloned.1.call-start = ((), (), s32[]{:S(2)}) async-start(), calls=%async_computation.34 | async-start | bytes 1474560 | tf_op jit(solution)/shard_map/reduce_scatter | solution.py:518
  990.4 127.8 %reduce-scatter.42.cloned.1.call-start = ((), (), s32[]{:S(2)}) async-start(), calls=%async_computation.33 | async-start | bytes 1474560 | tf_op jit(solution)/shard_map/reduce_scatter | solution.py:515
  1019.9 100.4 %reduce-scatter.76.cloned.1.call-start = ((), (), s32[]{:S(2)}) async-start(), calls=%async_computation.50 | async-start | bytes 1474560
  1047.7 78.4 %reduce-scatter.74.cloned.1.call-start = ((), (), s32[]{:S(2)}) async-start(), calls=%async_computation.49 | async-start | bytes 1474560
  1083.4 93.1 %reduce-scatter.62.cloned.1.call-start = ((), (), s32[]{:S(2)}) async-start(), calls=%async_computation.43 | async-start | bytes 5898240 | tf_op jit(solution)/shard_map/reduce_scatter | solution.py:542
  1091.8 240.0 %reduce-scatter.58.cloned.1.call-start = ((), (), s32[]{:S(2)}) async-start(), calls=%async_computation.41 | async-start | bytes 5898240 | tf_op jit(solution)/shard_map/reduce_scatter | solution.py:539
  1098.3 264.6 %reduce-scatter.82.cloned.1.call-start = ((), (), s32[]{:S(2)}) async-start(), calls=%async_computation.53 | async-start | bytes 442368
  1107.5 266.7 %reduce-scatter.78.cloned.1.call-start = ((), (), s32[]{:S(2)}) async-start(), calls=%async_computation.51 | async-start | bytes 884736
  1109.6 310.2 %reduce-scatter.70.cloned.1.call-start = ((), (), s32[]{:S(2)}) async-start(), calls=%async_computation.47 | async-start | bytes 884736
  1111.7 372.7 %reduce-scatter.72.cloned.1.call-start = ((), (), s32[]{:S(2)}) async-start(), calls=%async_computation.48 | async-start | bytes 884736
  1113.9 435.6 %reduce-scatter.68.cloned.1.call-start = ((), (), s32[]{:S(2)}) async-start(), calls=%async_computation.46 | async-start | bytes 884736
  1116.0 498.1 %reduce-scatter.66.cloned.1.call-start = ((), (), s32[]{:S(2)}) async-start(), calls=%async_computation.45 | async-start | bytes 884736
  1118.1 61.2 %copy-start.206 = (u32[32]{0:T(128)S(1)}, u32[32]{0:T(128)}, u32[]{:S(2)}) copy-start(u32[32]{0:T(128)} %constant.248) | copy-start | bytes 388
  1118.1 561.1 %reduce-scatter.64.cloned.1.call-start = ((), (), s32[]{:S(2)}) async-start(), calls=%async_computation.44 | async-start | bytes 884736
  1120.2 623.5 %reduce-scatter.54.cloned.1.call-start = ((), (), s32[]{:S(2)}) async-start(), calls=%async_computation.39 | async-start | bytes 884736 | tf_op jit(solution)/shard_map/reduce_scatter | solution.py:557
  1122.4 686.4 %reduce-scatter.52.cloned.1.call-start = ((), (), s32[]{:S(2)}) async-start(), calls=%async_computation.38 | async-start | bytes 884736 | tf_op jit(solution)/shard_map/reduce_scatter | solution.py:556
  1128.2 753.4 %reduce-scatter.80.cloned.1.call-start = ((), (), s32[]{:S(2)}) async-start(), calls=%async_computation.52 | async-start | bytes 2654208
  1179.3 774.3 %reduce-scatter.60.cloned.1.call-start = ((), (), s32[]{:S(2)}) async-start(), calls=%async_computation.42 | async-start | bytes 2654208 | tf_op jit(solution)/shard_map/reduce_scatter | solution.py:559
  1295.1 33.9 %copy-start.177 = (f32[512]{0:T(512)S(1)}, f32[512]{0:T(512)}, u32[]{:S(2)}) copy-start(f32[512]{0:T(512)} %copy-done.176) | copy-start | bytes 6148
  1295.1 34.0 %copy-start.15 = (f32[512,768]{1,0:T(8,128)S(1)}, f32[512,768]{1,0:T(8,128)}, u32[]{:S(2)}) copy-start(f32[512,768]{1,0:T(8,128)} %copy-done.14) | copy-start | bytes 4718596
  (238 other events, 2082.2 us)
Sparse Core Ops, SparseCore 0:
  35.6 24.8 all-gather.15
  62.6 30.8 all-gather.17
  95.6 30.7 all-gather.13
  127.8 31.4 all-gather.25
  161.3 30.1 all-gather.21
  193.5 30.3 all-gather.19
  225.4 30.4 all-gather.23
  258.0 39.3 all-gather.33
  299.5 38.5 all-gather.29
  339.5 19.1 all-gather.27
  578.6 38.3 all-gather.35
  618.3 37.4 all-gather.31
  768.1 25.2 reduce-scatter.55
  930.8 25.5 reduce-scatter.47
  958.8 25.7 reduce-scatter.49
  987.2 25.7 reduce-scatter.45
  1015.3 25.7 reduce-scatter.43
  1043.7 25.7 reduce-scatter.41
  1072.0 25.7 reduce-scatter.75
  1100.3 25.7 reduce-scatter.73
  1128.6 47.8 reduce-scatter.61
  1179.2 47.8 reduce-scatter.57
  1230.3 59.4 reduce-scatter.81
  1293.0 61.6 reduce-scatter.77
  1358.3 61.4 reduce-scatter.69
  1423.0 61.4 reduce-scatter.71
  1488.0 61.4 reduce-scatter.67
  1552.7 61.3 reduce-scatter.65
  1617.8 61.3 reduce-scatter.63
  1682.3 61.3 reduce-scatter.53
  1747.4 61.3 reduce-scatter.51
  1812.9 68.6 reduce-scatter.79
  1885.5 68.0 reduce-scatter.59
where the time goes:
time: 1970 us; the launch traced here: 1960 us
  waiting for transfers between devices  638 us (32%)
  matrix products  468 us (24%)
  local copies, waits for them, and re-layouts  378 us (19%)
  blocking collectives  307 us (16%)
  other arithmetic  149 us (8%)
    unnamed x43, waiting for transfers between devices  372 us
    unnamed x575, local copies, waits for them, and re-layouts  193 us
    dot_general x9, matrix products, attention_back(): jnp.einsum('qhd,khd->hqk', delta_rows, value_rows, preferred_element_type...  90.6 us
    convert_element_type x8, other arithmetic, attention_back(): low_scores = delta_scores.astype(jnp.bfloat16)  83.6 us
    reshape x2, local copies, waits for them, and re-layouts, bias_build(): repeated.reshape(head_count, length, 2 * length - 1)[:, :, length - 1:]  80 us
    reduce_scatter x1, waiting for transfers between devices, body(): lax.psum_scatter(row_sums[8], 'fsdp', scatter_dimension=1, tiled=True)  72 us
    dot_general x9, matrix products, attention_back(): jnp.einsum('hqk,qhd->khd', attention.astype(jnp.bfloat16), delta_rows, pr...  65.7 us
    reduce_scatter x1, waiting for transfers between devices, body(): lax.psum_scatter(row_sums[5], 'fsdp', scatter_dimension=1, tiled=True)  63.5 us
  transfers between devices with their start and end apart: 33, of which 12 were waited for; matrix products, arithmetic and copies ran while one was open for 43% of the time, Pallas kernels for 0%

commit v1 on v0

v1 whole, which is shorter than its diff:
```python
import functools
import math

import jax
import jax.numpy as jnp
from jax import lax
from jax.experimental import pallas as pl
from jax.experimental.pallas import tpu as pltpu
from jax.sharding import PartitionSpec as P

HEADS = 12
HEAD_DIM = 64
BUCKETS = 32
MAX_DIST = 128
MOST = 128
PAIRS = HEADS // 2
EPSILON = 1e-06
HIDDEN_SCORE = -1e30
BF = jnp.bfloat16
F32 = jnp.float32
VMEM_LIMIT = 60 * 1024 * 1024


def nn(a, b):
    return lax.dot_general(a, b, (((1,), (0,)), ((), ())), preferred_element_type=F32)


def nt(a, b):
    return lax.dot_general(a, b, (((1,), (1,)), ((), ())), preferred_element_type=F32)


def tn(a, b):
    return lax.dot_general(a, b, (((0,), (0,)), ((), ())), preferred_element_type=F32)


def rms(z, gain):
    factor = lax.rsqrt(jnp.mean(z * z, axis=-1, keepdims=True) + EPSILON)
    return z * factor * gain


def rms_back(z, gain, dy):
    factor = lax.rsqrt(jnp.mean(z * z, axis=-1, keepdims=True) + EPSILON)
    wdy = dy * gain
    inner = jnp.mean(z * wdy, axis=-1, keepdims=True)
    dz = factor * wdy - z * (factor * factor * factor * inner)
    return dz, jnp.sum(dy * z * factor, axis=0, keepdims=True)


def split_heads(rows):
    first = lax.broadcasted_iota(jnp.int32, rows.shape, 1) < HEAD_DIM
    zero = jnp.zeros_like(rows)
    return jnp.concatenate([jnp.where(first, rows, zero), jnp.where(first, zero, rows)], axis=0)


def join_heads(rows):
    half = rows.shape[0] // 2
    first = lax.broadcasted_iota(jnp.int32, (half, rows.shape[1]), 1) < HEAD_DIM
    return jnp.where(first, rows[:half], rows[half:])


def softmax(scores):
    raised = jnp.exp(scores - jnp.max(scores, axis=-1, keepdims=True))
    return raised * (1.0 / jnp.sum(raised, axis=-1, keepdims=True))


def lanes(index, width):
    return pl.ds(pl.multiple_of(index * width, width), width)


def loop(count, step):
    def run(index, carry):
        step(index)
        return carry

    lax.fori_loop(0, count, run, 0)


def bucket_of(distance):
    half_count = BUCKETS // 2
    counted = jnp.zeros_like(distance)
    for section_index in range(1, half_count):
        edge_at = int(
            math.ceil(half_count * (MAX_DIST / half_count) ** (section_index / half_count))
        )
        counted = counted + (distance >= edge_at).astype(jnp.int32)
    return jnp.where(distance < half_count, distance, half_count + counted)


def distance_hot():
    distance = jnp.maximum(MOST - jnp.arange(2 * MOST, dtype=jnp.int32), 0)
    return (bucket_of(distance)[:, None] == jnp.arange(BUCKETS, dtype=jnp.int32)[None, :]).astype(F32)


def self_masks(seg_col, seg_row, mask_ref):
    blocks = mask_ref.shape[0]
    a = lax.broadcasted_iota(jnp.int32, (MOST, 2 * MOST), 0)
    b = lax.broadcasted_iota(jnp.int32, (MOST, 2 * MOST), 1)
    causal = b <= a + MOST
    for i in range(blocks):
        same = seg_col[MOST * i : MOST * (i + 1), :] == seg_row[:, MOST * i : MOST * (i + 2)]
        mask_ref[i] = jnp.where(causal & same, 0.0, HIDDEN_SCORE)


def pair_bias(dist_ref, pair):
    parts = []
    for h in range(2):
        row = dist_ref[pl.ds(2 * pair + h, 1), :]
        parts.append(
            pltpu.roll(jnp.broadcast_to(row, (MOST, 2 * MOST)), 0, 1, stride=1, stride_axis=0)
        )
    return jnp.concatenate(parts, axis=0)


def masked_scores(scores, bias, mask):
    both = scores + bias
    return (both.reshape(2, MOST, 2 * MOST) + mask[None]).reshape(2 * MOST, 2 * MOST)


def front_kernel(
    x_ref, gains_ref, dist_ref, segc_ref, segr_ref, w_ref,
    n1_ref, q1_ref, k1_ref, v1_ref, a1_ref, h1_ref, n2_ref, q2_ref,
    mask_ref,
):
    rows, width = x_ref.shape
    blocks = rows // MOST
    n1_ref[...] = rms(x_ref[...].astype(F32), gains_ref[0:1, :]).astype(BF)
    k1_ref[0:MOST, :] = jnp.zeros((MOST, width), BF)
    v1_ref[0:MOST, :] = jnp.zeros((MOST, width), BF)

    def qkv(j):
        n1 = n1_ref[...]
        at = lanes(j, 256)
        q1_ref[:, at] = nt(n1, w_ref[0, at, :]).astype(BF)
        k1_ref[MOST:, at] = nt(n1, w_ref[1, at, :]).astype(BF)
        v1_ref[MOST:, at] = nt(n1, w_ref[2, at, :]).astype(BF)

    loop(width // 256, qkv)
    self_masks(segc_ref[...], segr_ref[...], mask_ref)

    def attend(pair):
        at = lanes(pair, 128)
        bias = pair_bias(dist_ref, pair)
        for i in range(blocks):
            queries = split_heads(q1_ref[MOST * i : MOST * (i + 1), at])
            keys = k1_ref[MOST * i : MOST * (i + 2), at]
            values = v1_ref[MOST * i : MOST * (i + 2), at]
            probs = softmax(masked_scores(nt(queries, keys), bias, mask_ref[i])).astype(BF)
            a1_ref[MOST * i : MOST * (i + 1), at] = join_heads(nn(probs, values)).astype(BF)

    loop(PAIRS, attend)

    def out(j):
        at = lanes(j, 256)
        h1_ref[:, at] = x_ref[:, at].astype(F32) + nt(a1_ref[...], w_ref[3, at, :])

    loop(width // 256, out)
    n2_ref[...] = rms(h1_ref[...], gains_ref[1:2, :]).astype(BF)

    def query(j):
        at = lanes(j, 256)
        q2_ref[:, at] = nt(n2_ref[...], w_ref[4, at, :]).astype(BF)

    loop(width // 256, query)


def example_rows(segr_ref, offr_ref, example, total):
    place = lax.broadcasted_iota(jnp.int32, (MOST, total), 0)
    return ((segr_ref[...] == example) & (offr_ref[...] == place)).astype(F32).astype(BF)


def cross_kernel(
    enc_ref, q2_ref, segr_ref, offr_ref, valid_ref, w_ref,
    k2_ref, v2_ref, a2_ref,
    qe_ref, ae_ref, sum_ref,
):
    e = pl.program_id(0)
    rows, width = q2_ref.shape
    keys_n = enc_ref.shape[0]

    @pl.when(e == 0)
    def _():
        sum_ref[...] = jnp.zeros_like(sum_ref)

    def project(j):
        at = lanes(j, 256)
        k2_ref[:, at] = nt(enc_ref[...], w_ref[0, at, :]).astype(BF)
        v2_ref[:, at] = nt(enc_ref[...], w_ref[1, at, :]).astype(BF)

    loop(width // 256, project)
    pick = example_rows(segr_ref, offr_ref, e, rows)
    qe_ref[...] = nn(pick, q2_ref[...]).astype(BF)
    hidden = valid_ref[pl.ds(e, 1), :]

    def attend(pair):
        at = lanes(pair, 128)
        probs = softmax(nt(split_heads(qe_ref[:, at]), k2_ref[:, at]) + hidden).astype(BF)
        ae_ref[:, at] = join_heads(nn(probs, v2_ref[:, at])).astype(BF)

    loop(PAIRS, attend)
    sum_ref[...] += tn(pick, ae_ref[...])

    @pl.when(e == pl.num_programs(0) - 1)
    def _():
        a2_ref[...] = sum_ref[...].astype(BF)


GELU_A = math.sqrt(2.0 / math.pi)
GELU_B = 0.044715


def feed_kernel(
    a2_ref, h1_ref, c_ref, gains_ref, w_ref, win_ref, wout_ref,
    out_ref, dwin_ref, dwout_ref, dwoc_ref, da2_ref, dh2_ref, gain_ref,
    h2_ref, n3_ref, sum_ref, back_ref,
):
    rows, width = a2_ref.shape
    hidden = win_ref.shape[1]

    def cross_out(j):
        at = lanes(j, 256)
        h2_ref[:, at] = h1_ref[:, at] + nt(a2_ref[...], w_ref[0, at, :])

    loop(width // 256, cross_out)
    n3_ref[...] = rms(h2_ref[...], gains_ref[2:3, :]).astype(BF)
    sum_ref[...] = h2_ref[...]
    back_ref[...] = jnp.zeros_like(back_ref)

    def part(j):
        at = lanes(j, 256)
        u = nn(n3_ref[...], win_ref[:, at])
        t = jnp.tanh(GELU_A * (u + GELU_B * (u * u * u)))
        g = (0.5 * u * (1.0 + t)).astype(BF)
        slope = 0.5 * (1.0 + t) + 0.5 * u * (1.0 - t * t) * (
            GELU_A * (1.0 + (3.0 * GELU_B) * (u * u))
        )
        du = (nn(c_ref[...], wout_ref[:, at]) * slope).astype(BF)
        dwout_ref[:, at] = tn(c_ref[...], g).astype(BF)
        dwin_ref[:, at] = tn(n3_ref[...], du).astype(BF)
        sum_ref[...] += nt(g, wout_ref[:, at])
        back_ref[...] += nt(du, win_ref[:, at])

    loop(hidden // 256, part)
    out_ref[...] = sum_ref[...].astype(BF)
    dz, dw = rms_back(h2_ref[...], gains_ref[2:3, :], back_ref[...])
    gain_ref[...] = dw
    dh2_ref[...] = c_ref[...].astype(F32) + dz

    def tail(j):
        at = lanes(j, 256)
        da2_ref[:, at] = nn(dh2_ref[...].astype(BF), w_ref[0, :, at]).astype(BF)
        dwoc_ref[at, :] = tn(dh2_ref[:, at].astype(BF), a2_ref[...]).astype(BF)

    loop(width // 256, tail)


def cross_back_kernel(
    enc_ref, k2_ref, v2_ref, q2_ref, da2_ref, segr_ref, offr_ref, valid_ref, w_ref,
    denc_ref, dq2_ref, dw_ref,
    qe_ref, dae_ref, dqe_ref, dk_ref, dv_ref, sum_ref, dwsum_ref,
):
    e = pl.program_id(0)
    rows, width = q2_ref.shape

    @pl.when(e == 0)
    def _():
        sum_ref[...] = jnp.zeros_like(sum_ref)
        dwsum_ref[...] = jnp.zeros_like(dwsum_ref)

    pick = example_rows(segr_ref, offr_ref, e, rows)
    qe_ref[...] = nn(pick, q2_ref[...]).astype(BF)
    dae_ref[...] = nn(pick, da2_ref[...]).astype(BF)
    hidden = valid_ref[pl.ds(e, 1), :]

    def attend(pair):
        at = lanes(pair, 128)
        queries = split_heads(qe_ref[:, at])
        deltas = split_heads(dae_ref[:, at])
        probs = softmax(nt(queries, k2_ref[:, at]) + hidden)
        dprobs = nt(deltas, v2_ref[:, at])
        low = (probs * (dprobs - jnp.sum(dprobs * probs, axis=-1, keepdims=True))).astype(BF)
        dv_ref[:, at] = tn(probs.astype(BF), deltas).astype(BF)
        dk_ref[:, at] = tn(low, queries).astype(BF)
        dqe_ref[:, at] = join_heads(nn(low, k2_ref[:, at])).astype(BF)

    loop(PAIRS, attend)
    sum_ref[...] += tn(pick, dqe_ref[...])

    def dense(j):
        at = lanes(j, 256)
        denc_ref[:, at] = (nn(dk_ref[...], w_ref[0, :, at]) + nn(dv_ref[...], w_ref[1, :, at])).astype(BF)
        dwsum_ref[0, at, :] += tn(dk_ref[:, at], enc_ref[...])
        dwsum_ref[1, at, :] += tn(dv_ref[:, at], enc_ref[...])

    loop(width // 256, dense)

    @pl.when(e == pl.num_programs(0) - 1)
    def _():
        dq2_ref[...] = sum_ref[...].astype(BF)
        dw_ref[...] = dwsum_ref[...].astype(BF)


def self_back_kernel(
    dq2_ref, n2_ref, h1_ref, dh2_ref, x_ref, n1_ref, q1_ref, k1_ref, v1_ref, a1_ref,
    gains_ref, dist_ref, segc_ref, segr_ref, w_ref,
    dx_ref, dw_ref, gain_ref, dist_out_ref,
    mask_ref, dh1_ref, b1_ref, da1_ref, dq_ref, dk_ref, dv_ref, dksum_ref, dvsum_ref, back_ref,
):
    rows, width = x_ref.shape
    blocks = rows // MOST

    def query(j):
        at = lanes(j, 256)
        dw_ref[4, at, :] = tn(dq2_ref[:, at], n2_ref[...]).astype(BF)
        back_ref[:, at] = nn(dq2_ref[...], w_ref[4, :, at])

    loop(width // 256, query)
    dz, dw = rms_back(h1_ref[...], gains_ref[1:2, :], back_ref[...])
    gain_ref[1:2, :] = dw
    dh1_ref[...] = dh2_ref[...] + dz
    b1_ref[...] = dh1_ref[...].astype(BF)

    def out(j):
        at = lanes(j, 256)
        dw_ref[3, at, :] = tn(b1_ref[:, at], a1_ref[...]).astype(BF)
        da1_ref[:, at] = nn(b1_ref[...], w_ref[3, :, at]).astype(BF)

    loop(width // 256, out)
    self_masks(segc_ref[...], segr_ref[...], mask_ref)

    def attend(pair):
        at = lanes(pair, 128)
        bias = pair_bias(dist_ref, pair)
        dksum_ref[...] = jnp.zeros_like(dksum_ref)
        dvsum_ref[...] = jnp.zeros_like(dvsum_ref)
        skewed = jnp.zeros((2 * MOST, 2 * MOST), F32)
        for i in range(blocks):
            own = slice(MOST * i, MOST * (i + 1))
            band = slice(MOST * i, MOST * (i + 2))
            queries = split_heads(q1_ref[own, at])
            deltas = split_heads(da1_ref[own, at])
            keys = k1_ref[band, at]
            probs = softmax(masked_scores(nt(queries, keys), bias, mask_ref[i]))
            dprobs = nt(deltas, v1_ref[band, at])
            dscores = probs * (dprobs - jnp.sum(dprobs * probs, axis=-1, keepdims=True))
            low = dscores.astype(BF)
            skewed = skewed + dscores
            dvsum_ref[band, :] += tn(probs.astype(BF), deltas)
            dksum_ref[band, :] += tn(low, queries)
            dq_ref[own, at] = join_heads(nn(low, keys)).astype(BF)
        dk_ref[:, at] = dksum_ref[MOST:, :].astype(BF)
        dv_ref[:, at] = dvsum_ref[MOST:, :].astype(BF)
        a = lax.broadcasted_iota(jnp.int32, (MOST, MOST), 0)
        b = lax.broadcasted_iota(jnp.int32, (MOST, MOST), 1)
        flip = (a + b == MOST - 1).astype(F32)
        for h in range(2):
            flipped = jnp.dot(
                flip,
                skewed[MOST * h : MOST * (h + 1)],
                precision=lax.Precision.HIGHEST,
                preferred_element_type=F32,
            )
            straight = pltpu.roll(flipped, MOST + 1, 1, stride=1, stride_axis=0)
            dist_out_ref[pl.ds(2 * pair + h, 1), :] = jnp.sum(straight, axis=0, keepdims=True)

    loop(PAIRS, attend)

    def qkv(j):
        at = lanes(j, 256)
        dw_ref[0, at, :] = tn(dq_ref[:, at], n1_ref[...]).astype(BF)
        dw_ref[1, at, :] = tn(dk_ref[:, at], n1_ref[...]).astype(BF)
        dw_ref[2, at, :] = tn(dv_ref[:, at], n1_ref[...]).astype(BF)
        back_ref[:, at] = (
            nn(dq_ref[...], w_ref[0, :, at])
            + nn(dk_ref[...], w_ref[1, :, at])
            + nn(dv_ref[...], w_ref[2, :, at])
        )

    loop(width // 256, qkv)
    dz, dw = rms_back(x_ref[...].astype(F32), gains_ref[0:1, :], back_ref[...])
    gain_ref[0:1, :] = dw
    dx_ref[...] = (dh1_ref[...] + dz).astype(BF)


def whole():
    return pl.BlockSpec(memory_space=pltpu.VMEM)


def call(kernel, outs, scratch, args, specs=None, grid=None, out_specs=None, name=None, flops=0):
    specs = specs or [whole()] * len(args)
    out_specs = out_specs or [whole()] * len(outs)
    return pl.pallas_call(
        kernel,
        grid=grid or (),
        in_specs=specs,
        out_specs=out_specs,
        out_shape=[jax.ShapeDtypeStruct(shape, kind) for shape, kind in outs],
        scratch_shapes=[pltpu.VMEM(shape, kind) for shape, kind in scratch],
        compiler_params=pltpu.CompilerParams(vmem_limit_bytes=VMEM_LIMIT),
        cost_estimate=pl.CostEstimate(flops=flops, bytes_accessed=20_000_000, transcendentals=0),
        name=name,
    )(*args)


def square_spec(first, count, width):
    return pl.BlockSpec((count, width, width), lambda *_: (first // count, 0, 0))


def body(decoder_in, encoder_out, decoder_lengths, encoder_lengths, norm_gains, rel_table,
         query_self, key_self, value_self, out_self, query_cross, key_cross, value_cross, out_cross,
         feed_in, feed_out, upstream):
    rows, width = decoder_in.shape
    row_count, examples = decoder_lengths.shape
    keys_n = encoder_out.shape[1]

    order = (query_self, key_self, value_self, out_self, query_cross, out_cross, key_cross, value_cross)
    square = jnp.stack([m.astype(BF).T for m in order])
    square = lax.all_gather(square, "fsdp", axis=1, tiled=True)
    square = lax.all_gather(square, "dp", axis=2, tiled=True)
    win = lax.all_gather(feed_in.astype(BF), "fsdp", axis=1, tiled=True)
    win = lax.all_gather(win, "dp", axis=0, tiled=True)
    wout = lax.all_gather(feed_out.astype(BF).T, "fsdp", axis=0, tiled=True)
    wout = lax.all_gather(wout, "dp", axis=1, tiled=True)
    gains = lax.all_gather(norm_gains.astype(BF), "fsdp", axis=1, tiled=True).astype(F32)
    table = lax.all_gather(rel_table.astype(BF), "dp", axis=0, tiled=True).astype(F32)
    hidden = win.shape[1]

    places = jnp.arange(rows, dtype=jnp.int32)
    ends = jnp.cumsum(decoder_lengths[0], dtype=jnp.int32)
    segment = jnp.sum((places[:, None] >= ends[None, :]).astype(jnp.int32), axis=-1)
    starts = ends - decoder_lengths[0]
    offset = places - jnp.sum(
        jnp.where(segment[:, None] == jnp.arange(examples)[None, :], starts[None, :], 0), axis=-1
    )
    seg_col = segment[:, None]
    seg_row = segment[None, :]
    off_row = offset[None, :]
    seg_band = jnp.concatenate([jnp.full((1, MOST), -1, jnp.int32), seg_row], axis=1)
    valid = jnp.where(
        jnp.arange(keys_n, dtype=jnp.int32)[None, :] < encoder_lengths[:, None], 0.0, HIDDEN_SCORE
    )
    hot = distance_hot()
    dist = jnp.dot(hot, table, precision=lax.Precision.HIGHEST).T

    small = (rows, width)
    n1, q1, k1, v1, a1, h1, n2, q2 = call(
        front_kernel,
        [(small, BF), (small, BF), ((rows + MOST, width), BF), ((rows + MOST, width), BF), (small, BF),
         (small, F32), (small, BF), (small, BF)],
        [((rows // MOST, MOST, 2 * MOST), F32)],
        (decoder_in, gains, dist, seg_col, seg_band, square),
        specs=[whole()] * 5 + [square_spec(0, 5, width)],
        grid=(1,),
        name="front",
    )
    enc = encoder_out.reshape(-1, width)
    per_example = pl.BlockSpec((keys_n, width), lambda e: (e, 0))
    k2, v2, a2 = call(
        cross_kernel,
        [(enc.shape, BF), (enc.shape, BF), (small, BF)],
        [((MOST, width), BF), ((MOST, width), BF), (small, F32)],
        (enc, q2, seg_row, off_row, valid, square),
        specs=[per_example] + [whole()] * 4 + [square_spec(6, 2, width)],
        out_specs=[per_example, per_example, whole()],
        grid=(examples,),
        name="cross",
    )
    out, dwin, dwout, dwoc, da2, dh2, gain3 = call(
        feed_kernel,
        [(small, BF), (win.shape, BF), (wout.shape, BF), ((width, width), BF), (small, BF), (small, F32),
         ((1, width), F32)],
        [(small, F32), (small, BF), (small, F32), (small, F32)],
        (a2, h1, upstream, gains, square, win, wout),
        specs=[whole()] * 4 + [square_spec(5, 1, width)] + [whole()] * 2,
        grid=(1,),
        name="feed",
    )
    denc, dq2, dw_kv = call(
        cross_back_kernel,
        [(enc.shape, BF), (small, BF), ((2, width, width), BF)],
        [((MOST, width), BF), ((MOST, width), BF), ((MOST, width), BF), ((keys_n, width), BF),
         ((keys_n, width), BF), (small, F32), ((2, width, width), F32)],
        (enc, k2, v2, q2, da2, seg_row, off_row, valid, square),
        specs=[per_example] * 3 + [whole()] * 5 + [square_spec(6, 2, width)],
        out_specs=[per_example, whole(), whole()],
        grid=(examples,),
        name="cross_back",
    )
    dx, dw_five, gain12, dist_sum = call(
        self_back_kernel,
        [(small, BF), ((5, width, width), BF), ((2, width), F32), ((HEADS, 2 * MOST), F32)],
        [((rows // MOST, MOST, 2 * MOST), F32), (small, F32), (small, BF), (small, BF), (small, BF),
         (small, BF), (small, BF), ((rows + MOST, 128), F32), ((rows + MOST, 128), F32), (small, F32)],
        (dq2, n2, h1, dh2, decoder_in, n1, q1, k1, v1, a1, gains, dist, seg_col, seg_band, square),
        specs=[whole()] * 14 + [square_spec(0, 5, width)],
        grid=(1,),
        name="self_back",
    )

    dsquare = jnp.concatenate([dw_five, dwoc[None], dw_kv], axis=0)
    dsquare = lax.psum_scatter(dsquare, "dp", scatter_dimension=2, tiled=True)
    dsquare = lax.psum_scatter(dsquare, "fsdp", scatter_dimension=1, tiled=True)
    dwin = lax.psum_scatter(dwin, "dp", scatter_dimension=0, tiled=True)
    dwin = lax.psum_scatter(dwin, "fsdp", scatter_dimension=1, tiled=True)
    dwout = lax.psum_scatter(dwout, "dp", scatter_dimension=1, tiled=True)
    dwout = lax.psum_scatter(dwout, "fsdp", scatter_dimension=0, tiled=True)
    gains_delta = lax.psum(jnp.concatenate([gain12, gain3], axis=0), "dp")
    gains_delta = lax.psum_scatter(gains_delta, "fsdp", scatter_dimension=1, tiled=True)
    table_delta = jnp.dot(dist_sum, hot, precision=lax.Precision.HIGHEST).T
    table_delta = lax.psum_scatter(table_delta, "dp", scatter_dimension=0, tiled=True)
    table_delta = lax.psum(table_delta, "fsdp")
    squares = [dsquare[i].astype(F32).T for i in range(8)]
    q_s, k_s, v_s, o_s, q_c, o_c, k_c, v_c = squares
    return (out, dx, denc.reshape(encoder_out.shape), gains_delta, table_delta,
            q_s, k_s, v_s, o_s, q_c, k_c, v_c, o_c, dwin.astype(F32), dwout.astype(F32).T)


def solution(mesh):
    tokens = P(("dp", "fsdp"), None)
    weight = P("dp", "fsdp")
    return jax.shard_map(
        body,
        mesh=mesh,
        in_specs=(tokens, P(("dp", "fsdp"), None, None), tokens, P(("dp", "fsdp")), P(None, "fsdp"),
                  P("dp", None)) + (weight,) * 10 + (tokens,),
        out_specs=(tokens, tokens, P(("dp", "fsdp"), None, None), P(None, "fsdp"), P("dp", None))
        + (weight,) * 10,
        check_vma=False,
    )
```

time: 1970 us -> 943 us (0.48)
  matrix products: 468 us -> 1.11 us
  blocking collectives: 307 us -> 55.1 us
  waiting for transfers between devices: 638 us -> 399 us
  Pallas kernels: 0 us -> 217 us
  local copies, waits for them, and re-layouts: 378 us -> 194 us
  other arithmetic: 149 us -> 55.9 us
    dot_general x86 -> x2, matrix products: 468 us -> 1.11 us  [the longest x1 0.84 us: body(): dist = jnp.dot(hot, table, precision=lax.Precision.HIGHEST).T]
    unnamed x43 -> x16, waiting for transfers between devices: 372 us -> 87.1 us
    all_gather x10 -> x2, blocking collectives: 272 us -> 25.2 us  [the longest x1 14.6 us: body(): lax.all_gather(norm_gains.astype(BF), 'fsdp', axis=1, tiled=True)]
    pallas_call x0 -> x5, Pallas kernels: none -> 217 us  [call(): pl.pallas_call(kernel, grid=grid or (), in_specs=specs, out_specs=out_spe...]
    all_gather x12 -> x6, waiting for transfers between devices: 19.2 us -> 175 us  [the longest x1 58.4 us: body(): square = lax.all_gather(square, 'fsdp', axis=1, tiled=True)]
    reduce_scatter x11 -> x4, waiting for transfers between devices: 246 us -> 138 us  [the longest x1 73.2 us: body(): dsquare = lax.psum_scatter(dsquare, 'dp', scatter_dimension=2, tiled=True)]
    convert_element_type x17 -> x4, other arithmetic: 92.8 us -> 2.39 us  [the longest x1 1.64 us: body(): win = lax.all_gather(feed_in.astype(BF), 'fsdp', axis=1, tiled=True)]
    reshape x5 -> x0, local copies, waits for them, and re-layouts: 80 us -> none  [the longest x2 80 us: bias_build(): repeated.reshape(head_count, length, 2 * length - 1)[:, :, length - 1:]]
  transfers between devices with their start and end apart: 33 -> 13, of which waited for: 12 -> 8; matrix products, arithmetic and copies ran while one was open for 43% -> 15% of each run, Pallas kernels for 0% -> 20%
where the time goes in v1:
time: 943 us; the launch traced here: 938 us
  waiting for transfers between devices  399 us (42%)
  Pallas kernels  217 us (23%)
  local copies, waits for them, and re-layouts  194 us (21%)
  other arithmetic  55.9 us (6%)
  blocking collectives  55.1 us (6%)
  between operations  14.9 us (2%)
    pallas_call x5, Pallas kernels, call(): pl.pallas_call(kernel, grid=grid or (), in_specs=specs, out_specs=out_spe...  217 us
    unnamed x56, local copies, waits for them, and re-layouts  160 us
    unnamed x16, waiting for transfers between devices  87.1 us
    reduce_scatter x1, waiting for transfers between devices, body(): dsquare = lax.psum_scatter(dsquare, 'dp', scatter_dimension=2, tiled=True)  73.2 us
    reduce_scatter x1, waiting for transfers between devices, body(): dwout = lax.psum_scatter(dwout, 'fsdp', scatter_dimension=0, tiled=True)  64.4 us
    all_gather x1, waiting for transfers between devices, body(): square = lax.all_gather(square, 'fsdp', axis=1, tiled=True)  58.4 us
    all_gather x1, waiting for transfers between devices, body(): wout = lax.all_gather(feed_out.astype(BF).T, 'fsdp', axis=0, tiled=True)  43.8 us
    transpose x1, other arithmetic, body(): squares = [dsquare[i].astype(F32).T for i in range(8)]  40.9 us
  transfers between devices with their start and end apart: 13, of which 8 were waited for; matrix products, arithmetic and copies ran while one was open for 15% of the time, Pallas kernels for 20%

profile of v1, /device:TPU:1, one launch (start us, length us, event | category | flops | bytes accessed | tf_op | source)
XLA Modules:
  0.0 938.1 jit_solution(16305785635575651107)
XLA Ops:
  7.2 1.0 copy.132
  8.2 1.0 copy.133
  9.2 1.0 copy.134
  10.2 1.0 copy.135
  11.2 1.0 copy.136
  12.2 1.0 copy.138
  13.2 1.0 copy.139
  14.2 1.0 copy.137
  15.3 0.7 copy-done.2
  16.1 1.6 convert_element_type.242
  17.8 1.6 convert_bitcast_fusion.1
  19.5 58.4 %all-gather.8.cloned.1.call-done = bf16[8,768,192]{2,1,0:T(8,128)(2,1)} async-done(((bf16[8,96,192]{2,1,0:T(8,128)(2,1)}), bf16[8,768,192]{2,1,0:T(8,128)(2,1)}) %all-gather.8.cloned.1.call-update) | async-done | bytes 2359312 | tf_op jit(solution)/shard_map/all_gather | solution.py:417
  77.9 4.8 copy.140
  82.8 35.7 %all-gather.12.cloned.1.call-done = bf16[192,3072]{1,0:T(8,128)(2,1)} async-done(((bf16[192,384]{1,0:T(8,128)(2,1)}), bf16[192,3072]{1,0:T(8,128)(2,1)}) %all-gather.12.cloned.1.call-update) | async-done | bytes 1179664 | tf_op jit(solution)/shard_map/all_gather | solution.py:419
  118.7 43.8 %all-gather.16.cloned.1.call-done = bf16[768,768]{1,0:T(8,128)(2,1)} async-done(((bf16[96,768]{1,0:T(8,128)(2,1)}), bf16[768,768]{1,0:T(8,128)(2,1)}) %all-gather.16.cloned.1.call-update) | async-done | bytes 1179664 | tf_op jit(solution)/shard_map/all_gather | solution.py:421
  162.6 14.6 %all-gather = bf16[8,96,3]{1,2,0:T(4,128)(2,1)S(1)} all-gather(bf16[1,96,3]{1,2,0:T(4,128)(2,1)S(1)} %convert_bitcast_fusion.2), channel_id=1, replica_groups=mesh['dp'=4,'fsdp'=8] {'fsdp'}, dimensions={0}, use_global_device_ids=true | all-gather | bytes 5184 | tf_op jit(solution)/shard_map/all_gather | solution.py:423
  177.2 0.7 reshape.141
  177.9 0.2 reduce-window.4
  178.1 0.1 convert_reduce_fusion
  178.2 0.9 copy.141.segc_ref
  179.0 0.6 concatenate.9.segr_ref
  179.6 10.6 %all_gather.25 = bf16[32,12]{1,0:T(8,128)(2,1)S(1)} all-gather(bf16[8,12]{1,0:T(8,128)(2,1)S(1)} %convert_element_type.232), channel_id=1, replica_groups=mesh['dp'=4,'fsdp'=8] {'dp'}, dimensions={0}, use_global_device_ids=true | all-gather | bytes 960 | tf_op jit(solution)/shard_map/all_gather | solution.py:424
  190.3 0.6 iota_subtract_fusion.offr_ref
  190.9 0.7 fusion.5.valid_ref
  191.6 0.8 convolution_bitcast_fusion.dist_ref
  192.4 36.8 %all-gather.10.cloned.1.call-done = bf16[8,768,768]{1,0,2:T(8,128)(2,1)} async-done(((bf16[8,768,192]{1,0,2:T(8,128)(2,1)}), bf16[8,768,768]{1,0,2:T(8,128)(2,1)}) %all-gather.10.cloned.1.call-update) | async-done | bytes 9437200 | tf_op jit(solution)/shard_map/all_gather | solution.py:418
  229.2 13.5 %copy.142.w_ref = bf16[8,768,768]{2,1,0:T(8,128)(2,1)} copy(bf16[8,768,768]{1,0,2:T(8,128)(2,1)} %all-gather.10.cloned.1.call-done) | data formatting | bytes 18874368 | tf_op jit(solution)/shard_map/all_gather | solution.py:418
  242.7 18.3 %front.1 = (bf16[512,768]{1,0:T(8,128)(2,1)}, bf16[512,768]{1,0:T(8,128)(2,1)}, bf16[640,768]{1,0:T(8,128)(2,1)}, bf16[640,768]{1,0:T(8,128)(2,1)}, bf16[512,768...) custom-call(bf16[512,768]{1,0:T(8,128)(2,1)} %x_ref.3, ...), custom_call_target="tpu_custom_call" | custom-call | bytes 20000000 | tf_op jit(solution)/shard_map/front/pallas_call | solution.py:391
  261.0 51.4 %cross.1 = (bf16[4096,768]{1,0:T(8,128)(2,1)}, bf16[4096,768]{1,0:T(8,128)(2,1)}, bf16[512,768]{1,0:T(8,128)(2,1)}) custom-call(bf16[4096,768]{1,0:T(8,128)(2,1)} %bitcast.95, bf16[512,768]{1,0:T(8,128)(2,1)} %get-tuple-element.40.q2_ref, s32[1,512]{1,0:T(1,128)} %bitcast.114, s32[1,512]{1,0:T(1,128)} %iota_subtract_fusion.offr_ref, ...), custom_call_target="tpu_custom_call" | custom-call | bytes 20000000 | tf_op jit(solution)/shard_map/cross/pallas_call | solution.py:391
  312.5 33.7 %feed.1 = (bf16[512,768]{1,0:T(8,128)(2,1)}, bf16[768,3072]{1,0:T(8,128)(2,1)}, bf16[768,3072]{1,0:T(8,128)(2,1)}, bf16[768,768]{1,0:T(8,128)(2,1)}, bf16[512,76...) custom-call(bf16[512,768]{1,0:T(8,128)(2,1)} %get-tuple-element.41.a2_ref, ...), custom_call_target="tpu_custom_call" | custom-call | bytes 20000000 | tf_op jit(solution)/shard_map/feed/pallas_call | solution.py:391
  346.3 0.7 reduce-scatter.18.cloned.1.call-update
  347.0 0.2 reduce-scatter.14.cloned.1.call-start
  347.2 80.5 %cross_back.1 = (bf16[4096,768]{1,0:T(8,128)(2,1)}, bf16[512,768]{1,0:T(8,128)(2,1)}, bf16[2,768,768]{2,1,0:T(8,128)(2,1)}) custom-call(bf16[4096,768]{1,0:T(8,128)(2,1)} %bitcast.96, bf16[4096,768]{1,0:T(8,128)(2,1)} %get-tuple-element.44.k2_ref, bf16[4096,768]{1,0:T(8,128)(2,1)} %get-tuple-element.45.v2_ref, bf16[512,768]{1,0:T(8,128)(2,1)} %get-tuple-element.40.q2_ref, ...), custom_call_target="tpu_custom_call" | custom-call | bytes 20000000 | tf_op jit(solution)/shard_map/cross_back/pallas_call | solution.py:391
  427.8 33.2 %self_back.1 = (bf16[512,768]{1,0:T(8,128)(2,1)}, bf16[5,768,768]{2,1,0:T(8,128)(2,1)}, f32[2,768]{1,0:T(2,128)}, f32[12,256]{1,0:T(8,128)}) custom-call(bf16[512,768]{1,0:T(8,128)(2,1)} %get-tuple-element.47.dq2_ref, bf16[512,768]{1,0:T(8,128)(2,1)} %get-tuple-element.48.n2_ref, f32[512,768]{1,0:T(8,128)} %get-tuple-element.42.h1_ref, ...), custom_call_target="tpu_custom_call" | custom-call | bytes 20000000 | tf_op jit(solution)/shard_map/self_back/pallas_call | solution.py:391
  461.1 7.7 pad_maximum_fusion
  468.8 13.1 %copy.148 = bf16[8,768,768]{1,0,2:T(8,128)(2,1)} copy(bf16[8,768,768]{2,1,0:T(8,128)(2,1)} %pad_maximum_fusion) | data formatting | bytes 18874368 | tf_op jit(solution)/shard_map/concatenate | solution.py:499
  481.9 0.6 copy-done.4
  482.6 1.0 copy.153
  483.6 2.6 copy.151
  486.3 0.5 reduce-scatter.20.cloned.1.call-update
  486.8 73.2 %reduce-scatter.14.cloned.1.call-done = bf16[8,768,192]{1,0,2:T(8,128)(2,1)} async-done(((bf16[8,768,768]{1,0,2:T(8,128)(2,1)}), bf16[8,768,192]{1,0,2:T(8,128)(2,1)}) %reduce-scatter.14.cloned.1.call-update) | async-done | bytes 2359312 | tf_op jit(solution)/shard_map/reduce_scatter | solution.py:500
  560.0 27.8 %copy.149 = bf16[8,768,192]{0,2,1:T(8,128)(2,1)} copy(bf16[8,768,192]{1,0,2:T(8,128)(2,1)} %reduce-scatter.14.cloned.1.call-done) | data formatting | bytes 4718592
  587.9 55.7 %reshape.142 = bf16[768,1536]{1,0:T(8,128)(2,1)} reshape(bf16[768,192,8]{2,1,0:T(8,128)(2,1)} %bitcast.94) | data formatting | bytes 4718592
  643.6 0.6 dynamic-slice
  644.9 0.3 fusion.1
  645.2 0.9 copy.154
  646.0 11.4 %all-reduce.2 = (f32[3,96]{1,0:T(4,128)}, f32[32,12]{1,0:T(8,128)S(1)}) all-reduce(f32[3,96]{1,0:T(4,128)S(1)} %copy.154, f32[32,12]{1,0:T(8,128)S(1)} %fusion.1), channel_id=1, replica_groups=mesh['dp'=4,'fsdp'=8] {'dp'}, use_global_device_ids=true, to_apply=%region_3.4 | all-reduce | flops 672 | bytes 5376 | tf_op jit(solution)/shard_map/psum | solution.py:506
  657.4 18.5 %psum.15 = f32[8,12]{1,0:T(8,128)} all-reduce(f32[8,12]{1,0:T(8,128)S(1)} %constant_dynamic-slice_fusion), channel_id=1, replica_groups=mesh['dp'=4,'fsdp'=8] {'fsdp'}, use_global_device_ids=true, to_apply=%region_6.7 | all-reduce | flops 96 | bytes 768 | tf_op jit(solution)/shard_map/psum | solution.py:510
  675.9 14.8 %reduce-scatter.24.cloned.1.call-done = bf16[384,192]{1,0:T(8,128)(2,1)} async-done(((bf16[3072,192]{1,0:T(8,128)(2,1)}), bf16[384,192]{1,0:T(8,128)(2,1)}) %reduce-scatter.24.cloned.1.call-update) | async-done | bytes 147472
  690.7 1.1 copy.152
  691.8 0.7 convert_element_type.252
  692.5 64.4 %reduce-scatter.20.cloned.1.call-done = bf16[96,768]{1,0:T(8,128)(2,1)} async-done(((bf16[768,768]{1,0:T(8,128)(2,1)}), bf16[96,768]{1,0:T(8,128)(2,1)}) %reduce-scatter.20.cloned.1.call-update) | async-done | bytes 147472 | tf_op jit(solution)/shard_map/reduce_scatter | solution.py:505
  756.9 1.6 convert_bitcast_fusion
  758.6 70.8 %reduce-scatter.22.cloned.1.call-done = bf16[96,1536]{1,0:T(8,128)(2,1)} async-done(((bf16[768,1536]{1,0:T(8,128)(2,1)}), bf16[96,1536]{1,0:T(8,128)(2,1)}) %reduce-scatter.22.cloned.1.call-update) | async-done | bytes 294928
  829.4 7.6 reshape.143
  837.0 40.9 %slice_convert_fusion = (f32[1,96,192]{0,2,1:T(8,128)}, f32[1,96,192]{0,2,1:T(8,128)}, f32[1,96,192]{0,2,1:T(8,128)}, f32[1,96,192]{0,2,1:T(8,128)}, f32[1,96,19...) fusion(bf16[8,96,192]{0,2,1:T(8,128)(2,1)} %bitcast.93), kind=kLoop, calls=%fused_computation.1 | loop fusion | flops 147456 | bytes 884736 | tf_op jit(solution)/shard_map/transpose | solution.py:511
  877.9 6.7 copy.170
  884.6 6.7 copy.169
  891.3 6.7 copy.168
  898.0 6.7 copy.167
  904.7 6.7 copy.166
  911.4 6.7 copy.165
  918.1 6.7 copy.164
  924.9 6.7 copy.163
  (66 shorter events, 1.0 us)
Async XLA Ops:
  7.2 70.8 %all-gather.8.cloned.1.call-start = ((), (), s32[]{:S(2)}) async-start(), calls=%async_computation.7 | async-start | bytes 3538944 | tf_op jit(solution)/shard_map/all_gather | solution.py:417
  15.3 0.7 copy-start.2
  15.3 147.3 %copy-start.5 = (f32[8,12]{1,0:T(8,128)S(1)}, f32[8,12]{1,0:T(8,128)}, u32[]{:S(2)}) copy-start(f32[8,12]{1,0:T(8,128)} %param.22) | copy-start | bytes 1156
  15.3 147.3 %copy-start.7 = (f32[3,96]{1,0:T(4,128)S(1)}, f32[3,96]{1,0:T(4,128)}, u32[]{:S(2)}) copy-start(f32[3,96]{1,0:T(4,128)} %param.21) | copy-start | bytes 3460
  15.3 162.6 %copy-start.10 = (s32[1,8]{1,0:T(1,128)S(1)}, s32[1,8]{1,0:T(1,128)}, u32[]{:S(2)}) copy-start(s32[1,8]{1,0:T(1,128)} %param.19) | copy-start | bytes 100
  16.0 174.9 %copy-start.8 = (s32[8]{0:T(128)S(1)}, s32[8]{0:T(128)}, u32[]{:S(2)}) copy-start(s32[8]{0:T(128)} %param.20) | copy-start | bytes 100
  16.0 102.5 %all-gather.12.cloned.1.call-start = ((), (), s32[]{:S(2)}) async-start(), calls=%async_computation.9 | async-start | bytes 1327104 | tf_op jit(solution)/shard_map/all_gather | solution.py:419
  17.8 144.7 %all-gather.16.cloned.1.call-start = ((), (), s32[]{:S(2)}) async-start(), calls=%async_computation.11 | async-start | bytes 1327104 | tf_op jit(solution)/shard_map/all_gather | solution.py:421
  19.5 209.7 %all-gather.10.cloned.1.call-start = ((), (), s32[]{:S(2)}) async-start(), calls=%async_computation.8 | async-start | bytes 11796480 | tf_op jit(solution)/shard_map/all_gather | solution.py:418
  82.8 229.7 %all-gather.14.cloned.1.call-start = ((), (), s32[]{:S(2)}) async-start(), calls=%async_computation.10 | async-start | bytes 5898240 | tf_op jit(solution)/shard_map/all_gather | solution.py:420
  118.6 193.9 %all-gather.18.cloned.1.call-start = ((), (), s32[]{:S(2)}) async-start(), calls=%async_computation.12 | async-start | bytes 5898240 | tf_op jit(solution)/shard_map/all_gather | solution.py:422
  162.5 321.2 %reduce-scatter.16.cloned.1.call-start = ((), (), s32[]{:S(2)}) async-start(), calls=%async_computation.14 | async-start | bytes 5898240 | tf_op jit(solution)/shard_map/reduce_scatter | solution.py:502
  178.2 64.5 %copy-start.3 = (s32[512]{0:T(512)}, s32[512]{0:T(512)S(1)}, u32[]{:S(2)}) copy-start(s32[512]{0:T(512)S(1)} %convert_reduce_fusion) | copy-start | bytes 6148
  346.3 140.0 %reduce-scatter.18.cloned.1.call-start = ((), (), s32[]{:S(2)}) async-start(), calls=%async_computation.15 | async-start | bytes 5898240 | tf_op jit(solution)/shard_map/reduce_scatter | solution.py:504
  347.0 213.0 %reduce-scatter.14.cloned.1.call-start = ((), (), s32[]{:S(2)}) async-start(), calls=%async_computation.13 | async-start | bytes 11796480 | tf_op jit(solution)/shard_map/reduce_scatter | solution.py:500
  427.8 33.3 %copy-start = (bf16[2,768,768]{2,1,0:T(8,128)(2,1)S(1)}, bf16[2,768,768]{2,1,0:T(8,128)(2,1)}, u32[]{:S(2)}) copy-start(bf16[2,768,768]{2,1,0:T(8,128)(2,1)} %get-tuple-element.62) | copy-start | bytes 7077892
  427.8 33.3 %copy-start.1 = (bf16[768,768]{1,0:T(8,128)(2,1)S(1)}, bf16[768,768]{1,0:T(8,128)(2,1)}, u32[]{:S(2)}) copy-start(bf16[768,768]{1,0:T(8,128)(2,1)} %get-tuple-element.61) | copy-start | bytes 3538948
  481.8 0.7 copy-start.4
  481.8 0.7 copy-start.6
  481.9 163.3 %reduce-scatter.26.cloned.1.call-start = ((), (), s32[]{:S(2)}) async-start(), calls=%async_computation.19 | async-start | bytes 442368
  483.6 207.2 %reduce-scatter.24.cloned.1.call-start = ((), (), s32[]{:S(2)}) async-start(), calls=%async_computation.18 | async-start | bytes 1769472
  486.2 270.7 %reduce-scatter.20.cloned.1.call-start = ((), (), s32[]{:S(2)}) async-start(), calls=%async_computation.16 | async-start | bytes 1327104 | tf_op jit(solution)/shard_map/reduce_scatter | solution.py:505
  486.8 342.6 %reduce-scatter.22.cloned.1.call-start = ((), (), s32[]{:S(2)}) async-start(), calls=%async_computation.17 | async-start | bytes 2654208
  587.9 55.7 %copy-start.11 = (u32[32]{0:T(128)S(1)}, u32[32]{0:T(128)}, u32[]{:S(2)}) copy-start(u32[32]{0:T(128)} %constant.53) | copy-start | bytes 388
  587.9 57.0 %copy-start.9 = (f32[12,256]{1,0:T(8,128)S(1)}, f32[12,256]{1,0:T(8,128)}, u32[]{:S(2)}) copy-start(f32[12,256]{1,0:T(8,128)} %get-tuple-element.59) | copy-start | bytes 36868
Sparse Core Ops, SparseCore 0:
  16.1 61.7 all-gather.7
  80.6 37.9 all-gather.11
  121.3 41.0 all-gather.15
  164.4 64.7 all-gather.9
  230.6 37.5 all-gather.13
  269.6 37.5 all-gather.17
  346.4 47.4 reduce-scatter.15
  396.5 47.8 reduce-scatter.17
  482.0 77.9 reduce-scatter.13
  563.1 59.4 reduce-scatter.25
  626.1 64.6 reduce-scatter.23
  694.3 62.5 reduce-scatter.19
  760.8 68.5 reduce-scatter.21

commit v2 on v1

--- a/solution.py
+++ b/solution.py
@@ -214,7 +214,7 @@
     h2_ref, n3_ref, sum_ref, back_ref,
 ):
     rows, width = a2_ref.shape
-    hidden = win_ref.shape[1]
+    hidden = win_ref.shape[0]
 
     def cross_out(j):
         at = lanes(j, 256)
@@ -227,7 +227,7 @@
 
     def part(j):
         at = lanes(j, 256)
-        u = nn(n3_ref[...], win_ref[:, at])
+        u = nt(n3_ref[...], win_ref[at, :])
         t = jnp.tanh(GELU_A * (u + GELU_B * (u * u * u)))
         g = (0.5 * u * (1.0 + t)).astype(BF)
         slope = 0.5 * (1.0 + t) + 0.5 * u * (1.0 - t * t) * (
@@ -235,9 +235,9 @@
         )
         du = (nn(c_ref[...], wout_ref[:, at]) * slope).astype(BF)
         dwout_ref[:, at] = tn(c_ref[...], g).astype(BF)
-        dwin_ref[:, at] = tn(n3_ref[...], du).astype(BF)
+        dwin_ref[at, :] = tn(du, n3_ref[...]).astype(BF)
         sum_ref[...] += nt(g, wout_ref[:, at])
-        back_ref[...] += nt(du, win_ref[:, at])
+        back_ref[...] += nn(du, win_ref[at, :])
 
     loop(hidden // 256, part)
     out_ref[...] = sum_ref[...].astype(BF)
@@ -381,6 +381,314 @@
     dx_ref[...] = (dh1_ref[...] + dz).astype(BF)
 
 
+MESH = pl.DeviceIdType.MESH
+PIECE = 48
+WIDE = 384
+UNITS = 16
+
+class Place:
+    def __init__(self):
+        d, f = lax.axis_index("dp"), lax.axis_index("fsdp")
+        self.d, self.f = d, f
+        self.y, self.c = d // 2, d % 2
+        self.z, self.x = f // 2, f % 2
+    def at(self, z=None, x=None, y=None, c=None):
+        z = self.z if z is None else z
+        x = self.x if x is None else x
+        y = self.y if y is None else y
+        c = self.c if c is None else c
+        return (y * 2 + c, z * 2 + x)
+
+def eye(n):
+    a = lax.broadcasted_iota(jnp.int32, (n, n), 0)
+    b = lax.broadcasted_iota(jnp.int32, (n, n), 1)
+    return (a == b).astype(F32).astype(BF)
+
+def remote(src, dst, send, recv, dev):
+    return pltpu.make_async_remote_copy(src_ref=src, dst_ref=dst, send_sem=send, recv_sem=recv,
+                                        device_id=dev, device_id_type=MESH)
+
+ALL = slice(None)
+
+def unit_piece(sq, fi, fo, u, z, x, c, y):
+    if u < 8:
+        return sq.at[u, z, x, c, :, pl.ds(pl.multiple_of(y * WIDE, WIDE), WIDE)]
+    if u < 12:
+        return fi.at[z, x, c, u - 8, :, pl.ds(pl.multiple_of(y * WIDE, WIDE), WIDE)]
+    return fo.at[z, x, c, :, pl.ds(pl.multiple_of(y * (4 * WIDE) + (u - 12) * WIDE, WIDE), WIDE)]
+
+class Gather:
+    def __init__(self, place, own, sq, fi, fo, sems):
+        self.p, self.own = place, own
+        self.bufs = (sq, fi, fo)
+        self.sems = sems
+        self.made = []
+    def piece(self, u, z, x, c, y):
+        return unit_piece(*self.bufs, u, z, x, c, y)
+    def go(self, u, slot, src, dst, dev):
+        copy = remote(src, dst, self.sems[0].at[u, slot], self.sems[1].at[u, slot], dev)
+        copy.start()
+        self.made.append(copy)
+        return copy
+    def first(self, u):
+        p = self.p
+        mine = self.piece(u, p.z, p.x, p.c, p.y)
+        self.zc = getattr(self, "zc", {})
+        self.zc[u] = [self.go(u, k - 1, self.own.at[u], mine, p.at(z=(p.z + k) % 4)) for k in (1, 2, 3)]
+    def even(self, u):
+        return u % 2 == 0
+    def second(self, u):
+        p = self.p
+        for copy in self.zc[u]:
+            copy.wait_recv()
+        here = self.piece(u, ALL, p.x, p.c, p.y)
+        dev = p.at(x=1 - p.x) if self.even(u) else p.at(y=1 - p.y)
+        self.sc = getattr(self, "sc", {})
+        self.sc[u] = self.go(u, 3, here, here, dev)
+    def third(self, u):
+        p = self.p
+        self.sc[u].wait_recv()
+        self.tc = getattr(self, "tc", {})
+        self.cc = getattr(self, "cc", {})
+        if self.even(u):
+            here = self.piece(u, ALL, ALL, p.c, p.y)
+            self.tc[u] = [self.go(u, 4, here, here, p.at(y=1 - p.y))]
+            self.cc[u] = [self.go(u, 6, here, here, p.at(c=1 - p.c))]
+        else:
+            here = [self.piece(u, ALL, p.x, p.c, y) for y in (0, 1)]
+            self.tc[u] = [self.go(u, 4 + y, here[y], here[y], p.at(x=1 - p.x)) for y in (0, 1)]
+            self.cc[u] = [self.go(u, 6 + y, here[y], here[y], p.at(c=1 - p.c)) for y in (0, 1)]
+    def fourth(self, u):
+        p = self.p
+        for copy in self.tc[u]:
+            copy.wait_recv()
+        if self.even(u):
+            here = self.piece(u, ALL, ALL, p.c, 1 - p.y)
+            self.cc[u] += [self.go(u, 8, here, here, p.at(c=1 - p.c))]
+        else:
+            here = [self.piece(u, ALL, 1 - p.x, p.c, y) for y in (0, 1)]
+            self.cc[u] += [self.go(u, 8 + y, here[y], here[y], p.at(c=1 - p.c)) for y in (0, 1)]
+    def fifth(self, u):
+        for copy in self.cc[u]:
+            copy.wait_recv()
+    def drain(self):
+        for copy in self.made:
+            copy.wait_send()
+
+def ag_kernel(q_s, k_s, v_s, o_s, q_c, o_c, k_c, v_c, f_i, f_o, sq, fi, fo,
+              xt, xf, land, landf, own, xsem, lsem, ssem, rsem):
+    p = Place()
+    barrier = pltpu.get_barrier_semaphore()
+    peers = [p.at(z=(p.z + k) % 4) for k in (1, 2, 3)] + [p.at(x=1 - p.x), p.at(y=1 - p.y), p.at(c=1 - p.c)]
+    for dev in peers:
+        pl.semaphore_signal(barrier, inc=1, device_id=dev, device_id_type=MESH)
+    e96 = eye(96)
+    for m, ref in enumerate((k_c, v_c, q_s, k_s, v_s, o_s, q_c, o_c)):
+        xt[m] = nt(e96, ref[...].astype(BF)).astype(BF).reshape(2, PIECE, 192)
+    t = nt(eye(384), f_i[...].astype(BF)).astype(BF).reshape(2, 4, PIECE, 192)
+    for s in range(4):
+        for h in range(2):
+            xt[8 + s, h] = t[h, s]
+    xf[...] = nt(e96, f_o[...].astype(BF)).astype(BF).reshape(2, PIECE, 768)
+    pl.semaphore_wait(barrier, len(peers))
+    sib = p.at(c=1 - p.c)
+    ex = [remote(xt.at[:, 1 - p.c], land, xsem.at[0], xsem.at[1], sib),
+          remote(xf.at[1 - p.c], landf, xsem.at[2], xsem.at[3], sib)]
+    for e in ex:
+        e.start()
+    ex[0].wait_recv()
+    first = p.c == 0
+    mine, other = xt[:, pl.ds(p.c, 1)].reshape(12, PIECE, 192), land[...]
+    own[0:12] = jnp.concatenate([jnp.where(first, mine, other), jnp.where(first, other, mine)], axis=-1)
+    ex[1].wait_recv()
+    mine, other = xf[pl.ds(p.c, 1)].reshape(PIECE, 768), landf[...]
+    lo, hi = jnp.where(first, mine, other), jnp.where(first, other, mine)
+    own[12] = lo[:, :WIDE]
+    own[13] = lo[:, WIDE:]
+    own[14] = hi[:, :WIDE]
+    own[15] = hi[:, WIDE:]
+    g = Gather(p, own, sq, fi, fo, (ssem, rsem))
+    local = []
+    for u in range(UNITS):
+        copy = pltpu.make_async_copy(own.at[u], g.piece(u, p.z, p.x, p.c, p.y), lsem.at[u])
+        copy.start()
+        local.append(copy)
+        g.first(u)
+    for u in range(UNITS):
+        local[u].wait()
+    for tick in range(UNITS + 4):
+        if tick < UNITS:
+            g.second(tick)
+        if 0 <= tick - 1 < UNITS:
+            g.third(tick - 1)
+        if 0 <= tick - 2 < UNITS:
+            g.fourth(tick - 2)
+    for u in range(UNITS):
+        g.fifth(u)
+    g.drain()
+    for e in ex:
+        e.wait_send()
+
+def gather(q_s, k_s, v_s, o_s, q_c, o_c, k_c, v_c, f_i, f_o):
+    hbm = pl.BlockSpec(memory_space=pl.ANY)
+    vm = pl.BlockSpec(memory_space=pltpu.VMEM)
+    return pl.pallas_call(
+        ag_kernel,
+        out_shape=[jax.ShapeDtypeStruct((8, 4, 2, 2, PIECE, 768), BF),
+                   jax.ShapeDtypeStruct((4, 2, 2, 4, PIECE, 768), BF),
+                   jax.ShapeDtypeStruct((4, 2, 2, PIECE, 3072), BF)],
+        in_specs=[vm] * 10,
+        out_specs=[hbm] * 3,
+        scratch_shapes=[pltpu.VMEM((12, 2, PIECE, 192), BF), pltpu.VMEM((2, PIECE, 768), BF),
+                        pltpu.VMEM((12, PIECE, 192), BF), pltpu.VMEM((PIECE, 768), BF),
+                        pltpu.VMEM((UNITS, PIECE, WIDE), BF),
+                        pltpu.SemaphoreType.DMA((4,)), pltpu.SemaphoreType.DMA((UNITS,)),
+                        pltpu.SemaphoreType.DMA((UNITS, 10)), pltpu.SemaphoreType.DMA((UNITS, 10))],
+        compiler_params=pltpu.CompilerParams(collective_id=0, has_side_effects=True, vmem_limit_bytes=60*1024*1024),
+        name="gather",
+    )(q_s, k_s, v_s, o_s, q_c, o_c, k_c, v_c, f_i, f_o)
+
+
+class Scatter:
+    def __init__(self, place, parts, count, refs, sems):
+        self.p, self.parts, self.count = place, parts, count
+        self.land, self.acc, self.land1, self.land2, self.land3, self.fin = refs
+        self.ssem, self.rsem, self.lsem = sems
+        self.c = {}
+        self.made = []
+    def go(self, u, slot, src, dst, dev):
+        copy = remote(src, dst, self.ssem.at[u, slot], self.rsem.at[u, slot], dev)
+        copy.start()
+        self.made.append(copy)
+        self.c.setdefault(u, {})[slot] = copy
+    def wait(self, u, slots):
+        for s in slots:
+            self.c[u][s].wait_recv()
+    def r0(self, u):
+        p = self.p
+        self.c.setdefault(u, {})["l"] = []
+        for y in (0, 1):
+            self.go(u, y, self.parts(u, 1 - p.c, y), self.land.at[u, y], p.at(c=1 - p.c))
+            copy = pltpu.make_async_copy(self.parts(u, p.c, y), self.acc.at[u, y], self.lsem.at[u, y])
+            copy.start()
+            self.c[u]["l"].append(copy)
+    def r1(self, u):
+        p = self.p
+        self.wait(u, (0, 1))
+        for copy in self.c[u]["l"]:
+            copy.wait()
+        if u % 2 == 0:
+            other, own = pl.ds(1 - p.y, 1), pl.ds(p.y, 1)
+            self.acc[u, other] = self.acc[u, other] + self.land[u, other]
+            self.go(u, 2, self.acc.at[u, 1 - p.y], self.land1.at[u], p.at(y=1 - p.y))
+            self.acc[u, own] = self.acc[u, own] + self.land[u, own]
+        else:
+            for y in (0, 1):
+                self.acc[u, y] = self.acc[u, y] + self.land[u, y]
+                self.go(u, 2 + y, self.acc.at[u, y, :, 1 - p.x], self.land1.at[u, :, y], p.at(x=1 - p.x))
+    def r2(self, u):
+        p = self.p
+        if u % 2 == 0:
+            self.wait(u, (2,))
+            own = pl.ds(p.y, 1)
+            self.acc[u, own] = self.acc[u, own] + self.land1[u][None]
+            self.go(u, 4, self.acc.at[u, p.y, :, 1 - p.x], self.land2.at[u], p.at(x=1 - p.x))
+        else:
+            self.wait(u, (2, 3))
+            x = pl.ds(p.x, 1)
+            for y in (0, 1):
+                self.acc[u, y, :, x] = self.acc[u, y, :, x] + self.land1[u, :, y][:, None]
+            self.go(u, 4, self.acc.at[u, 1 - p.y, :, p.x], self.land2.at[u], p.at(y=1 - p.y))
+    def r3(self, u):
+        p = self.p
+        self.wait(u, (4,))
+        y, x = pl.ds(p.y, 1), pl.ds(p.x, 1)
+        self.acc[u, y, :, x] = self.acc[u, y, :, x] + self.land2[u][None, :, None]
+        for k in (1, 2, 3):
+            z = (p.z + k) % 4
+            self.go(u, 4 + k, self.acc.at[u, p.y, z, p.x], self.land3.at[u, k - 1], p.at(z=z))
+    def r4(self, u):
+        p = self.p
+        self.wait(u, (5, 6, 7))
+        total = self.acc[u, pl.ds(p.y, 1), pl.ds(p.z, 1), pl.ds(p.x, 1)].reshape(PIECE, WIDE).astype(F32)
+        for k in range(3):
+            total = total + self.land3[u, k].astype(F32)
+        self.fin[u] = total.astype(BF)
+    def drain(self):
+        for copy in self.made:
+            copy.wait_send()
+
+def scatter_scratch(count):
+    return [pltpu.VMEM((count, 2, 4, 2, PIECE, WIDE), BF), pltpu.VMEM((count, 2, 4, 2, PIECE, WIDE), BF),
+            pltpu.VMEM((count, 4, 2, PIECE, WIDE), BF), pltpu.VMEM((count, 4, PIECE, WIDE), BF),
+            pltpu.VMEM((count, 3, PIECE, WIDE), BF), pltpu.VMEM((count, PIECE, WIDE), BF),
+            pltpu.SemaphoreType.DMA((count, 8)), pltpu.SemaphoreType.DMA((count, 8)), pltpu.SemaphoreType.DMA((count, 2))]
+
+def rs_kernel(sq, fi, fo, *rest):
+    outs, scr = rest[:10], rest[10:]
+    refs, sems = scr[:6], scr[6:9]
+    give, take, giveo, takeo, xsem = scr[9:]
+    p = Place()
+    barrier = pltpu.get_barrier_semaphore()
+    peers = [p.at(z=(p.z + k) % 4) for k in (1, 2, 3)] + [p.at(x=1 - p.x), p.at(y=1 - p.y), p.at(c=1 - p.c)]
+    for dev in peers:
+        pl.semaphore_signal(barrier, inc=1, device_id=dev, device_id_type=MESH)
+    pl.semaphore_wait(barrier, len(peers))
+    def parts(u, c, y):
+        if u < 8:
+            return sq.at[u, :, :, c, :, y * WIDE:(y + 1) * WIDE]
+        if u < 12:
+            return fi.at[:, :, c, u - 8, :, y * WIDE:(y + 1) * WIDE]
+        return fo.at[:, :, c, :, y * 4 * WIDE + (u - 12) * WIDE:y * 4 * WIDE + (u - 11) * WIDE]
+    s = Scatter(p, parts, 16, refs, sems)
+    P2 = 8
+    for t in range(P2 + 4):
+        for step, f in ((4, s.r4), (3, s.r3), (2, s.r2), (1, s.r1), (0, s.r0)):
+            if 0 <= t - step < P2:
+                for u in (2 * (t - step), 2 * (t - step) + 1):
+                    f(u)
+    fin = refs[5]
+    first = p.c == 0
+    def trade(lo, n):
+        low, high = fin[lo:lo + n, :, :192], fin[lo:lo + n, :, 192:]
+        give[lo:lo + n] = jnp.where(first, high, low)
+        return jnp.where(first, low, high)
+    mine = trade(0, 12)
+    sib = p.at(c=1 - p.c)
+    giveo[...] = fin[pl.ds(12 + 2 * (1 - p.c), 2)]
+    ex = [remote(give, take, xsem.at[0], xsem.at[1], sib), remote(giveo, takeo, xsem.at[2], xsem.at[3], sib)]
+    for e in ex: e.start()
+    ex[0].wait_recv()
+    e192 = eye(192)
+    def both(a, b):
+        return jnp.concatenate([jnp.where(first, a, b), jnp.where(first, b, a)], axis=0)
+    for m in range(8):
+        outs[m][...] = nt(e192, both(mine[m], take[m]))
+    t = both(mine[8:12].reshape(192, 192), take[8:12].reshape(192, 192))
+    outs[8][...] = nt(e192, t)
+    ex[1].wait_recv()
+    own = fin[pl.ds(12 + 2 * p.c, 2)]
+    t = both(jnp.concatenate([own[0], own[1]], axis=1), jnp.concatenate([takeo[0], takeo[1]], axis=1))
+    e768 = eye(WIDE)
+    outs[9][0:WIDE] = nt(e768, t[:, :WIDE])
+    outs[9][WIDE:] = nt(e768, t[:, WIDE:])
+    s.drain()
+    for e in ex: e.wait_send()
+
+def scatter(sq, fi, fo):
+    hbm = pl.BlockSpec(memory_space=pl.ANY)
+    vm = pl.BlockSpec(memory_space=pltpu.VMEM)
+    return pl.pallas_call(
+        rs_kernel,
+        out_shape=[jax.ShapeDtypeStruct((192, 96), F32)] * 8 + [jax.ShapeDtypeStruct((192, 384), F32), jax.ShapeDtypeStruct((768, 96), F32)],
+        in_specs=[hbm] * 3, out_specs=[vm] * 10,
+        scratch_shapes=scatter_scratch(16) + [pltpu.VMEM((12, PIECE, 192), BF), pltpu.VMEM((12, PIECE, 192), BF),
+            pltpu.VMEM((2, PIECE, WIDE), BF), pltpu.VMEM((2, PIECE, WIDE), BF), pltpu.SemaphoreType.DMA((4,))],
+        compiler_params=pltpu.CompilerParams(collective_id=1, has_side_effects=True, vmem_limit_bytes=60*1024*1024),
+        name="scatter",
+    )(sq, fi, fo)
+
+
 def whole():
     return pl.BlockSpec(memory_space=pltpu.VMEM)
 
@@ -401,28 +709,29 @@
     )(*args)
 
 
-def square_spec(first, count, width):
-    return pl.BlockSpec((count, width, width), lambda *_: (first // count, 0, 0))
-
-
-def body(decoder_in, encoder_out, decoder_lengths, encoder_lengths, norm_gains, rel_table,
+def body(custom, decoder_in, encoder_out, decoder_lengths, encoder_lengths, norm_gains, rel_table,
          query_self, key_self, value_self, out_self, query_cross, key_cross, value_cross, out_cross,
          feed_in, feed_out, upstream):
     rows, width = decoder_in.shape
     row_count, examples = decoder_lengths.shape
     keys_n = encoder_out.shape[1]
 
-    order = (query_self, key_self, value_self, out_self, query_cross, out_cross, key_cross, value_cross)
-    square = jnp.stack([m.astype(BF).T for m in order])
-    square = lax.all_gather(square, "fsdp", axis=1, tiled=True)
-    square = lax.all_gather(square, "dp", axis=2, tiled=True)
-    win = lax.all_gather(feed_in.astype(BF), "fsdp", axis=1, tiled=True)
-    win = lax.all_gather(win, "dp", axis=0, tiled=True)
-    wout = lax.all_gather(feed_out.astype(BF).T, "fsdp", axis=0, tiled=True)
-    wout = lax.all_gather(wout, "dp", axis=1, tiled=True)
+    if custom:
+        sq, fi, fo = gather(query_self, key_self, value_self, out_self, query_cross, out_cross, key_cross,
+                            value_cross, feed_in, feed_out)
+        sq, fi, fo = sq.reshape(8, width, width), fi.reshape(-1, width), fo.reshape(width, -1)
+    else:
+        order = (key_cross, value_cross, query_self, key_self, value_self, out_self, query_cross, out_cross)
+        sq = jnp.stack([m.astype(BF).T for m in order])
+        sq = lax.all_gather(sq, "fsdp", axis=1, tiled=True)
+        sq = lax.all_gather(sq, "dp", axis=2, tiled=True)
+        fi = lax.all_gather(feed_in.astype(BF).T, "fsdp", axis=0, tiled=True)
+        fi = lax.all_gather(fi, "dp", axis=1, tiled=True)
+        fo = lax.all_gather(feed_out.astype(BF).T, "fsdp", axis=0, tiled=True)
+        fo = lax.all_gather(fo, "dp", axis=1, tiled=True)
+    w_kv, w_five, w_oc = sq[0:2], sq[2:7], sq[7:8]
     gains = lax.all_gather(norm_gains.astype(BF), "fsdp", axis=1, tiled=True).astype(F32)
     table = lax.all_gather(rel_table.astype(BF), "dp", axis=0, tiled=True).astype(F32)
-    hidden = win.shape[1]
 
     places = jnp.arange(rows, dtype=jnp.int32)
     ends = jnp.cumsum(decoder_lengths[0], dtype=jnp.int32)
@@ -447,8 +756,8 @@
         [(small, BF), (small, BF), ((rows + MOST, width), BF), ((rows + MOST, width), BF), (small, BF),
          (small, F32), (small, BF), (small, BF)],
         [((rows // MOST, MOST, 2 * MOST), F32)],
-        (decoder_in, gains, dist, seg_col, seg_band, square),
-        specs=[whole()] * 5 + [square_spec(0, 5, width)],
+        (decoder_in, gains, dist, seg_col, seg_band, w_five),
+        specs=[whole()] * 6,
         grid=(1,),
         name="front",
     )
@@ -458,19 +767,19 @@
         cross_kernel,
         [(enc.shape, BF), (enc.shape, BF), (small, BF)],
         [((MOST, width), BF), ((MOST, width), BF), (small, F32)],
-        (enc, q2, seg_row, off_row, valid, square),
-        specs=[per_example] + [whole()] * 4 + [square_spec(6, 2, width)],
+        (enc, q2, seg_row, off_row, valid, w_kv),
+        specs=[per_example] + [whole()] * 5,
         out_specs=[per_example, per_example, whole()],
         grid=(examples,),
         name="cross",
     )
     out, dwin, dwout, dwoc, da2, dh2, gain3 = call(
         feed_kernel,
-        [(small, BF), (win.shape, BF), (wout.shape, BF), ((width, width), BF), (small, BF), (small, F32),
+        [(small, BF), (fi.shape, BF), (fo.shape, BF), ((width, width), BF), (small, BF), (small, F32),
          ((1, width), F32)],
         [(small, F32), (small, BF), (small, F32), (small, F32)],
-        (a2, h1, upstream, gains, square, win, wout),
-        specs=[whole()] * 4 + [square_spec(5, 1, width)] + [whole()] * 2,
+        (a2, h1, upstream, gains, w_oc, fi, fo),
+        specs=[whole()] * 7,
         grid=(1,),
         name="feed",
     )
@@ -479,8 +788,8 @@
         [(enc.shape, BF), (small, BF), ((2, width, width), BF)],
         [((MOST, width), BF), ((MOST, width), BF), ((MOST, width), BF), ((keys_n, width), BF),
          ((keys_n, width), BF), (small, F32), ((2, width, width), F32)],
-        (enc, k2, v2, q2, da2, seg_row, off_row, valid, square),
-        specs=[per_example] * 3 + [whole()] * 5 + [square_spec(6, 2, width)],
+        (enc, k2, v2, q2, da2, seg_row, off_row, valid, w_kv),
+        specs=[per_example] * 3 + [whole()] * 6,
         out_specs=[per_example, whole(), whole()],
         grid=(examples,),
         name="cross_back",
@@ -490,35 +799,39 @@
         [(small, BF), ((5, width, width), BF), ((2, width), F32), ((HEADS, 2 * MOST), F32)],
         [((rows // MOST, MOST, 2 * MOST), F32), (small, F32), (small, BF), (small, BF), (small, BF),
          (small, BF), (small, BF), ((rows + MOST, 128), F32), ((rows + MOST, 128), F32), (small, F32)],
-        (dq2, n2, h1, dh2, decoder_in, n1, q1, k1, v1, a1, gains, dist, seg_col, seg_band, square),
-        specs=[whole()] * 14 + [square_spec(0, 5, width)],
+        (dq2, n2, h1, dh2, decoder_in, n1, q1, k1, v1, a1, gains, dist, seg_col, seg_band, w_five),
+        specs=[whole()] * 15,
         grid=(1,),
         name="self_back",
     )
 
-    dsquare = jnp.concatenate([dw_five, dwoc[None], dw_kv], axis=0)
-    dsquare = lax.psum_scatter(dsquare, "dp", scatter_dimension=2, tiled=True)
-    dsquare = lax.psum_scatter(dsquare, "fsdp", scatter_dimension=1, tiled=True)
-    dwin = lax.psum_scatter(dwin, "dp", scatter_dimension=0, tiled=True)
-    dwin = lax.psum_scatter(dwin, "fsdp", scatter_dimension=1, tiled=True)
-    dwout = lax.psum_scatter(dwout, "dp", scatter_dimension=1, tiled=True)
-    dwout = lax.psum_scatter(dwout, "fsdp", scatter_dimension=0, tiled=True)
+    dsq = jnp.concatenate([dw_kv, dw_five, dwoc[None]], axis=0)
+    if custom:
+        parts = scatter(dsq.reshape(8, 4, 2, 2, PIECE, width), dwin.reshape(4, 2, 2, 4, PIECE, width),
+                        dwout.reshape(4, 2, 2, PIECE, -1))
+    else:
+        dsq = lax.psum_scatter(dsq, "dp", scatter_dimension=2, tiled=True)
+        dsq = lax.psum_scatter(dsq, "fsdp", scatter_dimension=1, tiled=True).astype(F32)
+        dwin = lax.psum_scatter(dwin, "dp", scatter_dimension=1, tiled=True)
+        dwin = lax.psum_scatter(dwin, "fsdp", scatter_dimension=0, tiled=True)
+        dwout = lax.psum_scatter(dwout, "dp", scatter_dimension=1, tiled=True)
+        dwout = lax.psum_scatter(dwout, "fsdp", scatter_dimension=0, tiled=True)
+        parts = [dsq[i].T for i in range(8)] + [dwin.astype(F32).T, dwout.astype(F32).T]
+    k_c, v_c, q_s, k_s, v_s, o_s, q_c, o_c, f_i, f_o = parts
     gains_delta = lax.psum(jnp.concatenate([gain12, gain3], axis=0), "dp")
     gains_delta = lax.psum_scatter(gains_delta, "fsdp", scatter_dimension=1, tiled=True)
     table_delta = jnp.dot(dist_sum, hot, precision=lax.Precision.HIGHEST).T
     table_delta = lax.psum_scatter(table_delta, "dp", scatter_dimension=0, tiled=True)
     table_delta = lax.psum(table_delta, "fsdp")
-    squares = [dsquare[i].astype(F32).T for i in range(8)]
-    q_s, k_s, v_s, o_s, q_c, o_c, k_c, v_c = squares
     return (out, dx, denc.reshape(encoder_out.shape), gains_delta, table_delta,
-            q_s, k_s, v_s, o_s, q_c, k_c, v_c, o_c, dwin.astype(F32), dwout.astype(F32).T)
+            q_s, k_s, v_s, o_s, q_c, k_c, v_c, o_c, f_i, f_o)
 
 
 def solution(mesh):
     tokens = P(("dp", "fsdp"), None)
     weight = P("dp", "fsdp")
     return jax.shard_map(
-        body,
+        functools.partial(body, (mesh.shape["dp"], mesh.shape["fsdp"]) == (4, 8)),
         mesh=mesh,
         in_specs=(tokens, P(("dp", "fsdp"), None, None), tokens, P(("dp", "fsdp")), P(None, "fsdp"),
                   P("dp", None)) + (weight,) * 10 + (tokens,),

time: 943 us -> 548 us (0.58)
  waiting for transfers between devices: 399 us -> 0.04 us
  Pallas kernels: 217 us -> 429 us
  local copies, waits for them, and re-layouts: 194 us -> 33.8 us
  other arithmetic: 55.9 us -> 9.34 us
    pallas_call x0 -> x2, Pallas kernels: none -> 211 us  [the longest x1 109 us: gather(): pl.pallas_call(ag_kernel, out_shape=[jax.ShapeDtypeStruct((8, 4, 2, 2, PI...]
    all_gather x6 -> x0, waiting for transfers between devices: 175 us -> none  [the longest x1 58.4 us: body(): square = lax.all_gather(square, 'fsdp', axis=1, tiled=True)]
    unnamed x56 -> x35, local copies, waits for them, and re-layouts: 160 us -> 20.2 us
    reduce_scatter x4 -> x0, waiting for transfers between devices: 138 us -> none  [the longest x1 73.2 us: body(): dsquare = lax.psum_scatter(dsquare, 'dp', scatter_dimension=2, tiled=True)]
    unnamed x16 -> x2, waiting for transfers between devices: 87.1 us -> 0.04 us
    transpose x3 -> x0, other arithmetic: 44.2 us -> none  [the longest x1 40.9 us: body(): squares = [dsquare[i].astype(F32).T for i in range(8)]]
    all_gather x2 -> x0, local copies, waits for them, and re-layouts: 18.3 us -> none  [the longest x1 13.5 us: body(): square = lax.all_gather(square, 'dp', axis=2, tiled=True)]
    concatenate x1 -> x0, local copies, waits for them, and re-layouts: 13.1 us -> none  [body(): dsquare = jnp.concatenate([dw_five, dwoc[None], dw_kv], axis=0)]
  transfers between devices with their start and end apart: 13 -> 1, of which waited for: 8 -> 0; matrix products, arithmetic and copies ran while one was open for 15% -> 2% of each run, Pallas kernels for 20% -> 19%
where the time goes in v2:
time: 548 us; the launch traced here: 542 us
  Pallas kernels  429 us (78%)
  blocking collectives  53.6 us (10%)
  local copies, waits for them, and re-layouts  33.8 us (6%)
  between operations  14.8 us (3%)
  other arithmetic  9.34 us (2%)
    pallas_call x5, Pallas kernels, call(): pl.pallas_call(kernel, grid=grid or (), in_specs=specs, out_specs=out_spe...  218 us
    pallas_call x1, Pallas kernels, gather(): pl.pallas_call(ag_kernel, out_shape=[jax.ShapeDtypeStruct((8, 4, 2, 2, PI...  109 us
    pallas_call x1, Pallas kernels, scatter(): pl.pallas_call(rs_kernel, out_shape=[jax.ShapeDtypeStruct((192, 96), F32)...  102 us
    unnamed x35, local copies, waits for them, and re-layouts  20.2 us
    psum x1, blocking collectives, body(): table_delta = lax.psum(table_delta, 'fsdp')  17.3 us
    all_gather x1, blocking collectives, body(): lax.all_gather(norm_gains.astype(BF), 'fsdp', axis=1, tiled=True)  17 us
    slice x3, local copies, waits for them, and re-layouts, body(): w_kv, w_five, w_oc = (sq[0:2], sq[2:7], sq[7:8])  11.5 us
  transfers between devices with their start and end apart: 1, of which 0 were waited for; matrix products, arithmetic and copies ran while one was open for 2% of the time, Pallas kernels for 19%

profile of v2, /device:TPU:1, one launch (start us, length us, event | category | flops | bytes accessed | tf_op | source)
XLA Modules:
  0.0 542.2 jit_solution(14373178211856599801)
XLA Ops:
  7.2 0.0 reduce-scatter.4.cloned.1.call-start
  7.2 1.9 copy.51.f_o
  9.1 109.1 %gather.1 = (bf16[8,4,2,2,48,768]{5,4,3,2,1,0:T(8,128)(2,1)}, bf16[4,2,2,4,48,768]{5,4,3,2,1,0:T(8,128)(2,1)}, bf16[4,2,2,48,3072]{4,3,2,1,0:T(8,128)(2,1)}) custom-call(f32[192,96]{1,0:T(8,128)} %q_s.1, f32[192,96]{1,0:T(8,128)} %k_s.1, f32[192,96]{1,0:T(8,128)} %v_s.1, f32[192,96]{1,0:T(8,128)} %o_s.1, f32[192,96]{1,0:T(8,128)} %q_c.1, f32[192,96]{1,0:T(8,128)} %o_c.1, ...), custom_call_target="tpu_custom_call" | custom-call | tf_op jit(solution)/shard_map/gather/pallas_call | solution.py:535
  118.2 5.8 %slice.18 = bf16[5,4,2,2,48,768]{5,4,3,2,1,0:T(8,128)(2,1)} slice(bf16[8,4,2,2,48,768]{5,4,3,2,1,0:T(8,128)(2,1)} %get-tuple-element.53), slice={[2:7], [0:4], [0:2], [0:2], [0:48], [0:768]} | slice | bytes 11796480 | tf_op jit(solution)/shard_map/slice | solution.py:732
  124.0 0.0 copy-start.8
  124.0 0.0 copy-start.5
  124.0 0.0 copy-start.3
  124.0 0.0 copy-start.6
  124.1 3.3 slice.20
  127.4 2.4 slice.22
  129.8 0.0 copy-done.8
  129.8 0.2 reduce-window.4
  129.9 0.1 convert_reduce_fusion
  130.0 0.0 copy-start.2
  130.0 0.9 copy.52.segc_ref
  130.9 0.0 copy-done.5
  130.9 17.0 %all-gather = bf16[8,96,3]{1,2,0:T(4,128)(2,1)S(1)} all-gather(bf16[1,96,3]{1,2,0:T(4,128)(2,1)S(1)} %convert_bitcast_fusion), channel_id=1, replica_groups=mesh['dp'=4,'fsdp'=8] {'fsdp'}, dimensions={0}, use_global_device_ids=true | all-gather | bytes 5184 | tf_op jit(solution)/shard_map/all_gather | solution.py:733
  147.9 0.7 reshape.142
  148.6 0.0 copy-done.3
  148.6 8.6 %all_gather.7 = bf16[32,12]{1,0:T(8,128)(2,1)S(1)} all-gather(bf16[8,12]{1,0:T(8,128)(2,1)S(1)} %convert_element_type.166), channel_id=1, replica_groups=mesh['dp'=4,'fsdp'=8] {'dp'}, dimensions={0}, use_global_device_ids=true | all-gather | bytes 960 | tf_op jit(solution)/shard_map/all_gather | solution.py:734
  157.2 0.1 select_reduce_fusion
  157.3 0.6 iota_subtract_fusion.offr_ref
  157.9 0.0 copy-done.6
  157.9 0.7 fusion.5.valid_ref
  158.5 0.6 concatenate.16.segr_ref
  159.1 0.8 convolution_bitcast_fusion.dist_ref
  160.0 18.5 %front.1 = (bf16[512,768]{1,0:T(8,128)(2,1)}, bf16[512,768]{1,0:T(8,128)(2,1)}, bf16[640,768]{1,0:T(8,128)(2,1)}, bf16[640,768]{1,0:T(8,128)(2,1)}, bf16[512,768...) custom-call(bf16[512,768]{1,0:T(8,128)(2,1)} %x_ref.3, ...), custom_call_target="tpu_custom_call" | custom-call | bytes 20000000 | tf_op jit(solution)/shard_map/front/pallas_call | solution.py:699
  178.4 0.0 copy-done.2
  178.4 51.5 %cross.1 = (bf16[4096,768]{1,0:T(8,128)(2,1)}, bf16[4096,768]{1,0:T(8,128)(2,1)}, bf16[512,768]{1,0:T(8,128)(2,1)}) custom-call(bf16[4096,768]{1,0:T(8,128)(2,1)} %bitcast.39, bf16[512,768]{1,0:T(8,128)(2,1)} %get-tuple-element.54.q2_ref, s32[1,512]{1,0:T(1,128)} %bitcast.57, s32[1,512]{1,0:T(1,128)} %iota_subtract_fusion.offr_ref, ...), custom_call_target="tpu_custom_call" | custom-call | bytes 20000000 | tf_op jit(solution)/shard_map/cross/pallas_call | solution.py:699
  229.9 34.6 %feed.1 = (bf16[512,768]{1,0:T(8,128)(2,1)}, bf16[3072,768]{1,0:T(8,128)(2,1)}, bf16[768,3072]{1,0:T(8,128)(2,1)}, bf16[768,768]{1,0:T(8,128)(2,1)}, bf16[512,76...) custom-call(bf16[512,768]{1,0:T(8,128)(2,1)} %get-tuple-element.55.a2_ref, ...), custom_call_target="tpu_custom_call" | custom-call | bytes 20000000 | tf_op jit(solution)/shard_map/feed/pallas_call | solution.py:699
  264.5 80.5 %cross_back.1 = (bf16[4096,768]{1,0:T(8,128)(2,1)}, bf16[512,768]{1,0:T(8,128)(2,1)}, bf16[2,768,768]{2,1,0:T(8,128)(2,1)}) custom-call(bf16[4096,768]{1,0:T(8,128)(2,1)} %bitcast.40, bf16[4096,768]{1,0:T(8,128)(2,1)} %get-tuple-element.60.k2_ref, bf16[4096,768]{1,0:T(8,128)(2,1)} %get-tuple-element.61.v2_ref, bf16[512,768]{1,0:T(8,128)(2,1)} %get-tuple-element.54.q2_ref, ...), custom_call_target="tpu_custom_call" | custom-call | bytes 20000000 | tf_op jit(solution)/shard_map/cross_back/pallas_call | solution.py:699
  345.0 0.0 copy-start.4
  345.0 0.0 copy-start
  345.0 0.0 copy-start.1
  345.0 33.4 %self_back.1 = (bf16[512,768]{1,0:T(8,128)(2,1)}, bf16[5,768,768]{2,1,0:T(8,128)(2,1)}, f32[2,768]{1,0:T(2,128)}, f32[12,256]{1,0:T(8,128)}) custom-call(bf16[512,768]{1,0:T(8,128)(2,1)} %get-tuple-element.63.dq2_ref, bf16[512,768]{1,0:T(8,128)(2,1)} %get-tuple-element.64.n2_ref, f32[512,768]{1,0:T(8,128)} %get-tuple-element.56.h1_ref, ...), custom_call_target="tpu_custom_call" | custom-call | bytes 20000000 | tf_op jit(solution)/shard_map/self_back/pallas_call | solution.py:699
  378.4 0.0 copy-done.4
  378.4 0.7 pad_maximum_fusion.1
  379.1 0.9 copy.55
  380.0 0.0 reduce-scatter.4.cloned.1.call-update
  380.1 0.0 copy-done
  380.1 0.0 copy-done.1
  380.1 0.0 copy-start.7
  380.1 7.0 %pad_maximum_fusion.sq = bf16[8,4,2,2,48,768]{5,4,3,2,1,0:T(8,128)(2,1)} fusion(bf16[1,4,2,2,48,768]{5,4,3,2,1,0:T(8,128)(2,1)S(1)} %bitcast.51, bf16[5,4,2,2,48,768]{5,4,3,2,1,0:T(8,128)(2,1)} %bitcast.43, bf16[2,4,2,2,48,768]{5,4,3,2,1,0:T(8,128)(2,1)S(1)} %bitcast.49), kind=kLoop, calls=%fused_computation | loop fusion | flops 9437184 | bytes 18874368 | tf_op jit(solution)/shard_map/concatenate | solution.py:808
  387.1 0.0 copy-done.7
  387.1 0.3 fusion.1
  387.4 0.0 copy-start.9
  387.4 101.9 %scatter.1 = (f32[192,96]{1,0:T(8,128)}, f32[192,96]{1,0:T(8,128)}, f32[192,96]{1,0:T(8,128)}, f32[192,96]{1,0:T(8,128)}, f32[192,96]{1,0:T(8,128)}, /*index=5*/...) custom-call(bf16[8,4,2,2,48,768]{5,4,3,2,1,0:T(8,128)(2,1)} %pad_maximum_fusion.s, ...), custom_call_target="tpu_custom_call" | custom-call | tf_op jit(solution)/shard_map/scatter/pallas_call | solution.py:681
  489.3 1.9 copy.54
  491.2 0.0 copy-done.9
  491.2 0.6 dynamic-slice
  492.4 0.0 reduce-scatter.4.cloned.1.call-done
  492.5 0.9 copy.56
  493.3 10.7 %all-reduce.2 = (f32[3,96]{1,0:T(4,128)}, f32[32,12]{1,0:T(8,128)S(1)}) all-reduce(f32[3,96]{1,0:T(4,128)S(1)} %copy.56, f32[32,12]{1,0:T(8,128)S(1)} %fusion.1), channel_id=1, replica_groups=mesh['dp'=4,'fsdp'=8] {'dp'}, use_global_device_ids=true, to_apply=%region_3.4 | all-reduce | flops 672 | bytes 5376 | tf_op jit(solution)/shard_map/psum | solution.py:821
  504.0 17.3 %psum.15 = f32[8,12]{1,0:T(8,128)} all-reduce(f32[8,12]{1,0:T(8,128)S(1)} %constant_dynamic-slice_fusion), channel_id=1, replica_groups=mesh['dp'=4,'fsdp'=8] {'fsdp'}, use_global_device_ids=true, to_apply=%region_6.7 | all-reduce | flops 96 | bytes 768 | tf_op jit(solution)/shard_map/psum | solution.py:825
  521.4 1.5 copy.67
  522.9 1.5 copy.68
  524.4 1.5 copy.69
  526.0 1.5 copy.70
  527.5 1.5 copy.71
  529.0 1.5 copy.72
  530.6 1.5 copy.73
  532.1 1.5 copy.74
  533.7 1.7 copy.75
  (6 shorter events, 0.0 us)
Async XLA Ops:
  7.2 485.3 %reduce-scatter.4.cloned.1.call-start = ((), (), s32[]{:S(2)}) async-start(), calls=%async_computation.1 | async-start | bytes 442368
  124.0 5.7 %copy-start.8 = (s32[1,8]{1,0:T(1,128)S(1)}, s32[1,8]{1,0:T(1,128)}, u32[]{:S(2)}) copy-start(s32[1,8]{1,0:T(1,128)} %param.19) | copy-start | bytes 100
  124.0 6.9 %copy-start.5 = (f32[3,96]{1,0:T(4,128)S(1)}, f32[3,96]{1,0:T(4,128)}, u32[]{:S(2)}) copy-start(f32[3,96]{1,0:T(4,128)} %param.21) | copy-start | bytes 3460
  124.0 24.5 %copy-start.3 = (f32[8,12]{1,0:T(8,128)S(1)}, f32[8,12]{1,0:T(8,128)}, u32[]{:S(2)}) copy-start(f32[8,12]{1,0:T(8,128)} %param.22) | copy-start | bytes 1156
  124.0 33.8 %copy-start.6 = (s32[8]{0:T(128)S(1)}, s32[8]{0:T(128)}, u32[]{:S(2)}) copy-start(s32[8]{0:T(128)} %param.20) | copy-start | bytes 100
  130.0 48.4 %copy-start.2 = (s32[512]{0:T(512)}, s32[512]{0:T(512)S(1)}, u32[]{:S(2)}) copy-start(s32[512]{0:T(512)S(1)} %convert_reduce_fusion) | copy-start | bytes 6148
  345.0 33.4 %copy-start.4 = (f32[1,768]{1,0:T(1,128)S(1)}, f32[1,768]{1,0:T(1,128)}, u32[]{:S(2)}) copy-start(f32[1,768]{1,0:T(1,128)} %get-tuple-element.74) | copy-start | bytes 9220
  345.0 35.1 %copy-start = (bf16[2,768,768]{2,1,0:T(8,128)(2,1)S(1)}, bf16[2,768,768]{2,1,0:T(8,128)(2,1)}, u32[]{:S(2)}) copy-start(bf16[2,768,768]{2,1,0:T(8,128)(2,1)} %get-tuple-element.76) | copy-start | bytes 7077892
  345.0 35.1 %copy-start.1 = (bf16[768,768]{1,0:T(8,128)(2,1)S(1)}, bf16[768,768]{1,0:T(8,128)(2,1)}, u32[]{:S(2)}) copy-start(bf16[768,768]{1,0:T(8,128)(2,1)} %get-tuple-element.78) | copy-start | bytes 3538948
  380.1 7.0 %copy-start.7 = (f32[12,256]{1,0:T(8,128)S(1)}, f32[12,256]{1,0:T(8,128)}, u32[]{:S(2)}) copy-start(f32[12,256]{1,0:T(8,128)} %get-tuple-element.75) | copy-start | bytes 36868
  387.4 103.8 %copy-start.9 = (u32[32]{0:T(128)S(1)}, u32[32]{0:T(128)}, u32[]{:S(2)}) copy-start(u32[32]{0:T(128)} %constant.53) | copy-start | bytes 388
Sparse Core Ops, SparseCore 0:
  380.2 57.7 reduce-scatter.3

commit v3 on v1

v3 whole, which is shorter than its diff:
```python
import functools
import math
import types

import jax
import jax.numpy as jnp
from jax import lax
from jax.experimental import pallas as pl
from jax.experimental.pallas import tpu as pltpu
from jax.sharding import PartitionSpec as P

HEADS = 12
HEAD_DIM = 64
BUCKETS = 32
MAX_DIST = 128
MOST = 128
PAIRS = HEADS // 2
EPSILON = 1e-06
HIDDEN_SCORE = -1e30
BF = jnp.bfloat16
F32 = jnp.float32
VMEM_LIMIT = 60 * 1024 * 1024


def nn(a, b):
    return lax.dot_general(a, b, (((1,), (0,)), ((), ())), preferred_element_type=F32)


def nt(a, b):
    return lax.dot_general(a, b, (((1,), (1,)), ((), ())), preferred_element_type=F32)


def tn(a, b):
    return lax.dot_general(a, b, (((0,), (0,)), ((), ())), preferred_element_type=F32)


def rms(z, gain):
    factor = lax.rsqrt(jnp.mean(z * z, axis=-1, keepdims=True) + EPSILON)
    return z * factor * gain


def rms_back(z, gain, dy):
    factor = lax.rsqrt(jnp.mean(z * z, axis=-1, keepdims=True) + EPSILON)
    wdy = dy * gain
    inner = jnp.mean(z * wdy, axis=-1, keepdims=True)
    dz = factor * wdy - z * (factor * factor * factor * inner)
    return dz, jnp.sum(dy * z * factor, axis=0, keepdims=True)


def split_heads(rows):
    first = lax.broadcasted_iota(jnp.int32, rows.shape, 1) < HEAD_DIM
    zero = jnp.zeros_like(rows)
    return jnp.concatenate([jnp.where(first, rows, zero), jnp.where(first, zero, rows)], axis=0)


def join_heads(rows):
    half = rows.shape[0] // 2
    first = lax.broadcasted_iota(jnp.int32, (half, rows.shape[1]), 1) < HEAD_DIM
    return jnp.where(first, rows[:half], rows[half:])


def softmax(scores):
    raised = jnp.exp(scores - jnp.max(scores, axis=-1, keepdims=True))
    return raised * (1.0 / jnp.sum(raised, axis=-1, keepdims=True))


def lanes(index, width):
    return pl.ds(pl.multiple_of(index * width, width), width)


def loop(low, high, step):
    def run(index, carry):
        step(index)
        return carry

    lax.fori_loop(low, high, run, 0)


def bucket_of(distance):
    half_count = BUCKETS // 2
    counted = jnp.zeros_like(distance)
    for section_index in range(1, half_count):
        edge_at = int(
            math.ceil(half_count * (MAX_DIST / half_count) ** (section_index / half_count))
        )
        counted = counted + (distance >= edge_at).astype(jnp.int32)
    return jnp.where(distance < half_count, distance, half_count + counted)


def distance_hot():
    distance = jnp.maximum(MOST - jnp.arange(2 * MOST, dtype=jnp.int32), 0)
    return (bucket_of(distance)[:, None] == jnp.arange(BUCKETS, dtype=jnp.int32)[None, :]).astype(F32)


def local(src, dst, sem):
    return pltpu.make_async_copy(src, dst, sem)


def w_rows(ref, m, j):
    return ref[m, pl.ds(2 * j, 2)].reshape(2 * WIDE // 2, ref.shape[-1])


def w_lanes(ref, m, at):
    part = ref[m, :, :, :, :, at]
    return part.reshape(-1, part.shape[-1])


MESH = pl.DeviceIdType.MESH
PIECE = 48
WIDE = 384
UNITS = 16
ALL = slice(None)


class Place:
    def __init__(self):
        self.d, self.f = lax.axis_index("dp"), lax.axis_index("fsdp")
        self.y, self.c = self.d // 2, self.d % 2
        self.z, self.x = self.f // 2, self.f % 2

    def at(self, z=None, x=None, y=None, c=None):
        z = self.z if z is None else z
        x = self.x if x is None else x
        y = self.y if y is None else y
        c = self.c if c is None else c
        return (y * 2 + c, z * 2 + x)

    def near(self):
        others = [self.at(z=(self.z + k) % 4) for k in (1, 2, 3)]
        return others + [self.at(x=1 - self.x), self.at(y=1 - self.y), self.at(c=1 - self.c)]


def greet(peers):
    barrier = pltpu.get_barrier_semaphore()
    for dev in peers:
        pl.semaphore_signal(barrier, inc=1, device_id=dev, device_id_type=MESH)
    pl.semaphore_wait(barrier, len(peers))


def eye(n):
    a = lax.broadcasted_iota(jnp.int32, (n, n), 0)
    b = lax.broadcasted_iota(jnp.int32, (n, n), 1)
    return (a == b).astype(F32).astype(BF)


def remote(src, dst, send, recv, dev):
    return pltpu.make_async_remote_copy(
        src_ref=src, dst_ref=dst, send_sem=send, recv_sem=recv, device_id=dev, device_id_type=MESH
    )


class Sends:
    def __init__(self, place, ssem, rsem):
        self.p, self.ssem, self.rsem, self.made = place, ssem, rsem, {}

    def to_x(self):
        return self.p.at(x=1 - self.p.x)

    def to_y(self):
        return self.p.at(y=1 - self.p.y)

    def to_c(self):
        return self.p.at(c=1 - self.p.c)

    def go(self, u, slot, src, dst, dev):
        def make():
            return remote(src(), dst(), self.ssem.at[u, slot], self.rsem.at[u, slot], dev())

        make().start()
        self.made[u, slot] = make

    def wait(self, u, *slots):
        for slot in slots:
            self.made[u, slot]().wait_recv()

    def drain(self):
        for make in self.made.values():
            make().wait_send()


class Gather(Sends):
    def __init__(self, place, own, sq, fi, fo, ssem, rsem):
        super().__init__(place, ssem, rsem)
        self.own, self.sq, self.fi, self.fo = own, sq, fi, fo

    def piece(self, u, z, x, c, y):
        if u < 8:
            return self.sq.at[u, z, x, c, :, pl.ds(pl.multiple_of(y * WIDE, WIDE), WIDE)]
        if u < 12:
            return self.fi.at[z, x, c, u - 8, :, pl.ds(pl.multiple_of(y * WIDE, WIDE), WIDE)]
        at = y * (4 * WIDE) + (u - 12) * WIDE
        return self.fo.at[z, x, c, :, pl.ds(pl.multiple_of(at, WIDE), WIDE)]

    def same(self, u, slot, dev, z, x, c, y):
        def here():
            return self.piece(u, z, x, c, y)

        self.go(u, slot, here, here, dev)

    def first(self, u):
        p = self.p
        for k in (1, 2, 3):
            self.go(
                u, k - 1, lambda: self.own.at[u], lambda: self.piece(u, p.z, p.x, p.c, p.y),
                lambda k=k: p.at(z=(p.z + k) % 4),
            )

    def second(self, u):
        p = self.p
        self.wait(u, 0, 1, 2)
        self.same(u, 3, self.to_x if u % 2 == 0 else self.to_y, ALL, p.x, p.c, p.y)

    def third(self, u):
        p = self.p
        self.wait(u, 3)
        if u % 2 == 0:
            self.same(u, 4, self.to_y, ALL, ALL, p.c, p.y)
            self.same(u, 6, self.to_c, ALL, ALL, p.c, p.y)
        else:
            for y in (0, 1):
                self.same(u, 4 + y, self.to_x, ALL, p.x, p.c, y)
            for y in (0, 1):
                self.same(u, 6 + y, self.to_c, ALL, p.x, p.c, y)

    def fourth(self, u):
        p = self.p
        if u % 2 == 0:
            self.wait(u, 4)
            self.same(u, 8, self.to_c, ALL, ALL, p.c, 1 - p.y)
        else:
            self.wait(u, 4, 5)
            for y in (0, 1):
                self.same(u, 8 + y, self.to_c, ALL, 1 - p.x, p.c, y)

    def fifth(self, u):
        self.wait(u, *((6, 8) if u % 2 == 0 else (6, 7, 8, 9)))

    def tick(self, t):
        for step, act in ((2, self.fourth), (1, self.third), (0, self.second)):
            if 0 <= t - step < UNITS // 2:
                act(2 * (t - step))
                act(2 * (t - step) + 1)


class Scatter(Sends):
    def __init__(self, place, parts, r):
        super().__init__(place, r.ssem, r.rsem)
        self.parts, self.r = parts, r

    def halves(self, u):
        p, r = self.p, self.r
        return [local(self.parts(u, p.c, y), r.acc.at[u, y], r.lsem.at[u, y]) for y in (0, 1)]

    def r0(self, u):
        p, r = self.p, self.r
        for y in (0, 1):
            self.go(
                u, y, lambda y=y: self.parts(u, 1 - p.c, y), lambda y=y: r.land.at[u, y], self.to_c
            )
        for copy in self.halves(u):
            copy.start()

    def r1(self, u):
        p, r = self.p, self.r
        self.wait(u, 0, 1)
        for copy in self.halves(u):
            copy.wait()
        if u % 2 == 0:
            other, own = pl.ds(1 - p.y, 1), pl.ds(p.y, 1)
            r.acc[u, other] = r.acc[u, other] + r.land[u, other]
            self.go(u, 2, lambda: r.acc.at[u, 1 - p.y], lambda: r.land1.at[u], self.to_y)
            r.acc[u, own] = r.acc[u, own] + r.land[u, own]
        else:
            for y in (0, 1):
                r.acc[u, y] = r.acc[u, y] + r.land[u, y]
                self.go(
                    u, 2 + y, lambda y=y: r.acc.at[u, y, :, 1 - p.x], lambda y=y: r.land1.at[u, :, y],
                    self.to_x,
                )

    def r2(self, u):
        p, r = self.p, self.r
        if u % 2 == 0:
            self.wait(u, 2)
            own = pl.ds(p.y, 1)
            r.acc[u, own] = r.acc[u, own] + r.land1[u][None]
            self.go(
                u, 4, lambda: r.acc.at[u, p.y, :, 1 - p.x], lambda: r.land2.at[u], self.to_x
            )
        else:
            self.wait(u, 2, 3)
            x = pl.ds(p.x, 1)
            for y in (0, 1):
                r.acc[u, y, :, x] = r.acc[u, y, :, x] + r.land1[u, :, y][:, None]
            self.go(
                u, 4, lambda: r.acc.at[u, 1 - p.y, :, p.x], lambda: r.land2.at[u], self.to_y
            )

    def r3(self, u):
        p, r = self.p, self.r
        self.wait(u, 4)
        y, x = pl.ds(p.y, 1), pl.ds(p.x, 1)
        r.acc[u, y, :, x] = r.acc[u, y, :, x] + r.land2[u][None, :, None]
        for k in (1, 2, 3):
            self.go(
                u, 4 + k, lambda k=k: r.acc.at[u, p.y, (p.z + k) % 4, p.x],
                lambda k=k: r.land3.at[u, k - 1], lambda k=k: p.at(z=(p.z + k) % 4),
            )

    def r4(self, u):
        p, r = self.p, self.r
        self.wait(u, 5, 6, 7)
        part = r.acc[u, pl.ds(p.y, 1), pl.ds(p.z, 1), pl.ds(p.x, 1)]
        total = part.reshape(PIECE, WIDE).astype(F32)
        for k in range(3):
            total = total + r.land3[u, k].astype(F32)
        r.fin[u] = total.astype(BF)

    def step(self, number, *units):
        act = (self.r0, self.r1, self.r2, self.r3, self.r4)[number]
        for u in units:
            act(u)


def scatter_scratch(count):
    return dict(
        land=pltpu.VMEM((count, 2, 4, 2, PIECE, WIDE), BF),
        acc=pltpu.VMEM((count, 2, 4, 2, PIECE, WIDE), BF),
        land1=pltpu.VMEM((count, 4, 2, PIECE, WIDE), BF),
        land2=pltpu.VMEM((count, 4, PIECE, WIDE), BF),
        land3=pltpu.VMEM((count, 3, PIECE, WIDE), BF),
        ssem=pltpu.SemaphoreType.DMA((count, 8)),
        rsem=pltpu.SemaphoreType.DMA((count, 8)),
        lsem=pltpu.SemaphoreType.DMA((count, 2)),
    )


def self_masks(seg_col, seg_row, mask_ref):
    blocks = mask_ref.shape[0]
    a = lax.broadcasted_iota(jnp.int32, (MOST, 2 * MOST), 0)
    b = lax.broadcasted_iota(jnp.int32, (MOST, 2 * MOST), 1)
    causal = b <= a + MOST
    for i in range(blocks):
        same = seg_col[MOST * i : MOST * (i + 1), :] == seg_row[:, MOST * i : MOST * (i + 2)]
        mask_ref[i] = jnp.where(causal & same, 0.0, HIDDEN_SCORE)


def pair_bias(dist_ref, pair):
    parts = []
    for h in range(2):
        row = dist_ref[pl.ds(2 * pair + h, 1), :]
        parts.append(
            pltpu.roll(jnp.broadcast_to(row, (MOST, 2 * MOST)), 0, 1, stride=1, stride_axis=0)
        )
    return jnp.concatenate(parts, axis=0)


def masked_scores(scores, bias, mask):
    both = scores + bias
    return (both.reshape(2, MOST, 2 * MOST) + mask[None]).reshape(2 * MOST, 2 * MOST)


def example_rows(segr_ref, offr_ref, example, total):
    place = lax.broadcasted_iota(jnp.int32, (MOST, total), 0)
    return ((segr_ref[...] == example) & (offr_ref[...] == place)).astype(F32).astype(BF)


def spread_shards(p, r):
    e96 = eye(96)
    shards = (r.k_c, r.v_c, r.q_s, r.k_s, r.v_s, r.o_s, r.q_c, r.o_c)
    for m, ref in enumerate(shards):
        r.xt[m] = nt(e96, ref[...].astype(BF)).astype(BF).reshape(2, PIECE, 192)
    t = nt(eye(384), r.f_i[...].astype(BF)).astype(BF).reshape(2, 4, PIECE, 192)
    for s in range(4):
        for h in range(2):
            r.xt[8 + s, h] = t[h, s]
    r.xf[...] = nt(e96, r.f_o[...].astype(BF)).astype(BF).reshape(2, PIECE, 768)


def small_sends(p, r):
    made = []
    for k in range(1, 8):
        dev = (p.d, (p.f + k) % 8)
        made.append(
            remote(r.gt.at[p.f], r.gt.at[p.f], r.smsem.at[0, k - 1], r.smsem.at[1, k - 1], dev)
        )
    for k in range(1, 4):
        dev = ((p.d + k) % 4, p.f)
        made.append(
            remote(r.tt.at[p.d], r.tt.at[p.d], r.smsem.at[0, 6 + k], r.smsem.at[1, 6 + k], dev)
        )
    return made


def forward_kernel(comm, r):
    rows, width = r.x.shape
    examples, keys_n = r.valid.shape
    blocks = rows // MOST
    enc_copies = [local(r.enc.at[e], r.encv.at[e], r.esem.at[e]) for e in range(examples)]
    for copy in enc_copies:
        copy.start()

    if comm:
        p = Place()
        peers = [(p.d, (p.f + k) % 8) for k in range(1, 8)] + [((p.d + k) % 4, p.f) for k in range(1, 4)]
        r.gt[pl.ds(p.f, 1)] = jnp.zeros((1, 8, 128), F32)
        r.gt[pl.ds(p.f, 1), 0:3, 0:96] = r.gains_s[...].astype(BF).astype(F32)[None]
        r.tt[pl.ds(p.d, 1)] = jnp.zeros((1, 8, 128), F32)
        r.tt[pl.ds(p.d, 1), :, 0:HEADS] = r.table_s[...].astype(BF).astype(F32)[None]
        spread_shards(p, r)
        greet(peers)
        sib = p.at(c=1 - p.c)
        trade = [
            remote(r.xt.at[:, 1 - p.c], r.took, r.xsem.at[0], r.xsem.at[1], sib),
            remote(r.xf.at[1 - p.c], r.tookf, r.xsem.at[2], r.xsem.at[3], sib),
        ]
        small = small_sends(p, r)
        for copy in trade + small:
            copy.start()
        first = p.c == 0
        trade[0].wait_recv()
        mine, other = r.xt[:, pl.ds(p.c, 1)].reshape(12, PIECE, 192), r.took[...]
        r.own[0:12] = jnp.concatenate(
            [jnp.where(first, mine, other), jnp.where(first, other, mine)], axis=-1
        )
        trade[1].wait_recv()
        mine, other = r.xf[pl.ds(p.c, 1)].reshape(PIECE, 768), r.tookf[...]
        low, high = jnp.where(first, mine, other), jnp.where(first, other, mine)
        r.own[12], r.own[13] = low[:, :WIDE], low[:, WIDE:]
        r.own[14], r.own[15] = high[:, :WIDE], high[:, WIDE:]
        g = Gather(p, r.own, r.sq, r.fi, r.fo, r.ssem, r.rsem)
        placed = [
            local(r.own.at[u], g.piece(u, p.z, p.x, p.c, p.y), r.psem.at[u]) for u in range(UNITS)
        ]
        for u in range(UNITS):
            g.first(u)
            placed[u].start()
        for copy in small:
            copy.wait_recv()
        spot = lax.broadcasted_iota(jnp.int32, (128, width), 1)
        lane = lax.broadcasted_iota(jnp.int32, (128, width), 0)
        gains = jnp.zeros((8, width), F32)
        for f in range(8):
            put = ((spot == lane + 96 * f) & (lane < 96)).astype(F32).astype(BF)
            gains = gains + nn(r.gt[f].astype(BF), put)
        r.gains[...] = gains[0:3]
        table = r.tt[...].reshape(BUCKETS, 128).astype(BF)
        r.dist[...] = tn(table, r.hot[...].astype(BF))[0:HEADS]
        for copy in placed:
            copy.wait()
        tick, arrived = g.tick, g.fifth
    else:
        tick = arrived = lambda index: None

    loads = [local(r.sq.at[m], r.wv.at[m], r.wsem.at[m]) for m in range(7)]

    def fetch(*which):
        for m in which:
            arrived(m)
            loads[m].start()

    def have(*which):
        for m in which:
            loads[m].wait()

    r.n1[...] = rms(r.x[...].astype(F32), r.gains[0:1, :]).astype(BF)
    r.k1[0:MOST, :] = jnp.zeros((MOST, width), BF)
    r.v1[0:MOST, :] = jnp.zeros((MOST, width), BF)
    self_masks(r.seg_col[...], r.seg_band[...], r.mask)
    halves = width // WIDE

    def save(e):
        return [local(r.k2v.at[e], r.k2.at[e], r.ksem.at[e, 0]), local(r.v2v.at[e], r.v2.at[e], r.ksem.at[e, 1])]

    def project(e):
        local(r.enc.at[e], r.encv.at[e], r.esem.at[e]).wait()
        for j in range(halves):
            at = slice(WIDE * j, WIDE * (j + 1))
            r.k2v[e, :, at] = nt(r.encv[e], w_rows(r.wv, 0, j)).astype(BF)
            r.v2v[e, :, at] = nt(r.encv[e], w_rows(r.wv, 1, j)).astype(BF)
        for copy in save(e):
            copy.start()

    tick(0)
    tick(1)
    tick(2)
    fetch(0, 1)
    have(0, 1)
    loop(0, examples // 2, project)
    tick(3)
    fetch(2, 3)
    loop(examples // 2, examples, project)
    tick(4)
    fetch(4, 5)
    have(2, 3, 4)

    for j in range(halves):
        at = slice(WIDE * j, WIDE * (j + 1))
        r.q1[:, at] = nt(r.n1[...], w_rows(r.wv, 2, j)).astype(BF)
        r.k1[MOST:, at] = nt(r.n1[...], w_rows(r.wv, 3, j)).astype(BF)
        r.v1[MOST:, at] = nt(r.n1[...], w_rows(r.wv, 4, j)).astype(BF)

    def attend(pair):
        at = lanes(pair, 128)
        bias = pair_bias(r.dist, pair)
        for i in range(blocks):
            queries = split_heads(r.q1[MOST * i : MOST * (i + 1), at])
            keys = r.k1[MOST * i : MOST * (i + 2), at]
            values = r.v1[MOST * i : MOST * (i + 2), at]
            probs = softmax(masked_scores(nt(queries, keys), bias, r.mask[i])).astype(BF)
            r.a1[MOST * i : MOST * (i + 1), at] = join_heads(nn(probs, values)).astype(BF)

    loop(0, PAIRS // 2, attend)
    tick(5)
    fetch(6)
    loop(PAIRS // 2, PAIRS, attend)
    have(5, 6)
    for j in range(halves):
        at = slice(WIDE * j, WIDE * (j + 1))
        r.h1[:, at] = r.x[:, at].astype(F32) + nt(r.a1[...], w_rows(r.wv, 5, j))
    r.n2[...] = rms(r.h1[...], r.gains[1:2, :]).astype(BF)
    for j in range(halves):
        at = slice(WIDE * j, WIDE * (j + 1))
        r.q2[:, at] = nt(r.n2[...], w_rows(r.wv, 6, j)).astype(BF)

    r.sum[...] = jnp.zeros_like(r.sum)

    def cross(e):
        pick = example_rows(r.seg_row, r.off_row, e, rows)
        r.qe[...] = nn(pick, r.q2[...]).astype(BF)
        hidden = r.valid[pl.ds(e, 1), :]

        def pair_step(pair):
            at = lanes(pair, 128)
            probs = softmax(nt(split_heads(r.qe[:, at]), r.k2v[e, :, at]) + hidden).astype(BF)
            r.ae[:, at] = join_heads(nn(probs, r.v2v[e, :, at])).astype(BF)

        loop(0, PAIRS, pair_step)
        r.sum[...] += tn(pick, r.ae[...])

    tick(6)
    loop(0, 3, cross)
    tick(7)
    loop(3, 6, cross)
    tick(8)
    loop(6, examples, cross)
    r.a2[...] = r.sum[...].astype(BF)
    tick(9)

    def saved(e):
        for copy in save(e):
            copy.wait()

    loop(0, examples, saved)
    if comm:
        for u in range(7, UNITS):
            g.fifth(u)
        g.drain()
        for copy in trade + small:
            copy.wait_send()


GELU_A = math.sqrt(2.0 / math.pi)
GELU_B = 0.044715


def feed_kernel(r):
    rows, width = r.a2.shape
    hidden = r.fi.shape[0]

    def cross_out(j):
        at = lanes(j, 256)
        r.h2[:, at] = r.h1[:, at] + nt(r.a2[...], r.w[0, at, :])

    loop(0, width // 256, cross_out)
    r.n3[...] = rms(r.h2[...], r.gains[2:3, :]).astype(BF)
    r.sum[...] = r.h2[...]
    r.back[...] = jnp.zeros_like(r.back)

    def part(j):
        at = lanes(j, 256)
        u = nt(r.n3[...], r.fi[at, :])
        t = jnp.tanh(GELU_A * (u + GELU_B * (u * u * u)))
        g = (0.5 * u * (1.0 + t)).astype(BF)
        slope = 0.5 * (1.0 + t) + 0.5 * u * (1.0 - t * t) * (
            GELU_A * (1.0 + (3.0 * GELU_B) * (u * u))
        )
        du = (nn(r.c[...], r.fo[:, at]) * slope).astype(BF)
        r.dfo[:, at] = tn(r.c[...], g).astype(BF)
        r.dfi[at, :] = tn(du, r.n3[...]).astype(BF)
        r.sum[...] += nt(g, r.fo[:, at])
        r.back[...] += nn(du, r.fi[at, :])

    loop(0, hidden // 256, part)
    r.out[...] = r.sum[...].astype(BF)
    dz, dw = rms_back(r.h2[...], r.gains[2:3, :], r.back[...])
    r.gain[...] = dw
    r.dh2[...] = r.c[...].astype(F32) + dz

    def tail(j):
        at = lanes(j, 256)
        r.da2[:, at] = nn(r.dh2[...].astype(BF), r.w[0, :, at]).astype(BF)
        r.dwoc[at, :] = tn(r.dh2[:, at].astype(BF), r.a2[...]).astype(BF)

    loop(0, width // 256, tail)


def cross_back_kernel(comm, r):
    rows, width = r.q2.shape
    examples, keys_n = r.valid.shape
    halves = width // WIDE

    def fetches(e):
        return [local(getattr(r, a).at[e], getattr(r, b).at[e], r.esem.at[e, i])
                for i, (a, b) in enumerate((("enc", "encv"), ("k2", "k2v"), ("v2", "v2v")))]

    for e in range(examples):
        for copy in fetches(e):
            copy.start()
    if comm:
        p = Place()

        def parts(u, c, y):
            if u < 4:
                return r.dfi.at[:, :, c, u, :, y * WIDE : (y + 1) * WIDE]
            at = y * 4 * WIDE + (u - 4) * WIDE
            return r.dfo.at[:, :, c, :, at : at + WIDE]

        s = Scatter(p, parts, r)
        greet(p.near())
    r.sum[...] = jnp.zeros_like(r.sum)
    r.dwsum[...] = jnp.zeros_like(r.dwsum)

    def out_copy(e):
        return local(r.denv.at[e % 2], r.denc.at[e], r.dsem.at[e % 2])

    def example(e):
        if comm:
            for t in range(8):

                @pl.when(e == t)
                def _():
                    for number in (4, 3, 2, 1, 0):
                        if 0 <= t - number < 4:
                            s.step(number, t - number, 4 + t - number)

        for copy in fetches(e):
            copy.wait()
        pick = example_rows(r.seg_row, r.off_row, e, rows)
        r.qe[...] = nn(pick, r.q2[...]).astype(BF)
        r.dae[...] = nn(pick, r.da2[...]).astype(BF)
        hidden = r.valid[pl.ds(e, 1), :]

        def attend(pair):
            at = lanes(pair, 128)
            queries = split_heads(r.qe[:, at])
            deltas = split_heads(r.dae[:, at])
            keys = r.k2v[e, :, at]
            probs = softmax(nt(queries, keys) + hidden)
            dprobs = nt(deltas, r.v2v[e, :, at])
            low = (probs * (dprobs - jnp.sum(dprobs * probs, axis=-1, keepdims=True))).astype(BF)
            r.dv[:, at] = tn(probs.astype(BF), deltas).astype(BF)
            r.dk[:, at] = tn(low, queries).astype(BF)
            r.dqe[:, at] = join_heads(nn(low, keys)).astype(BF)

        loop(0, PAIRS, attend)
        r.sum[...] += tn(pick, r.dqe[...])

        @pl.when(e >= 2)
        def _():
            out_copy(e - 2).wait()

        def dense(j):
            at = lanes(j, 256)
            r.denv[e % 2, :, at] = (
                nn(r.dk[...], w_lanes(r.w, 0, at)) + nn(r.dv[...], w_lanes(r.w, 1, at))
            ).astype(BF)
            r.dwsum[0, at, :] += tn(r.dk[:, at], r.encv[e])
            r.dwsum[1, at, :] += tn(r.dv[:, at], r.encv[e])

        loop(0, width // 256, dense)
        out_copy(e).start()

    loop(0, examples, example)
    r.dq2[...] = r.sum[...].astype(BF)
    r.dwkv[...] = r.dwsum[...].astype(BF)
    for e in (examples - 2, examples - 1):
        out_copy(e).wait()
    if comm:
        s.drain()


def self_back_kernel(comm, r):
    rows, width = r.x.shape
    blocks = rows // MOST
    thirds = width // 256
    if comm:
        p = Place()

        def parts(u, c, y):
            at = slice(y * WIDE, (y + 1) * WIDE)
            if u < 2:
                return r.dwkv.at[u, :, :, c, :, at]
            if u == 2:
                return r.dwoc.at[:, :, c, :, at]
            return r.dw.at[u - 3, :, :, c, :, at]

        s = Scatter(p, parts, r)
        greet(p.near())
        step = s.step
    else:
        step = lambda *units: None

    def put(m, j, value):
        if comm:
            r.dw[m, 2 * j : 2 * j + 2] = value.astype(BF).reshape(2, 2, 2, PIECE, width)
        else:
            r.dw[m, WIDE * j : WIDE * (j + 1), :] = value.astype(BF)

    halves = width // WIDE
    step(0, 0, 1, 2)
    for j in range(halves):
        at = slice(WIDE * j, WIDE * (j + 1))
        put(0, j, tn(r.dq2[:, at], r.n2[...]))
    step(0, 3)

    def query(j):
        at = lanes(j, 256)
        r.back[:, at] = nn(r.dq2[...], w_lanes(r.w, 4, at))

    loop(0, thirds, query)
    step(1, 0, 1)
    dz, dw = rms_back(r.h1[...], r.gains[1:2, :], r.back[...])
    r.gain[1:2, :] = dw
    r.dh1[...] = r.dh2[...] + dz
    r.b1[...] = r.dh1[...].astype(BF)
    for j in range(halves):
        at = slice(WIDE * j, WIDE * (j + 1))
        put(1, j, tn(r.b1[:, at], r.a1[...]))
    step(0, 4)
    step(2, 0, 1)

    def out(j):
        at = lanes(j, 256)
        r.da1[:, at] = nn(r.b1[...], w_lanes(r.w, 3, at)).astype(BF)

    loop(0, thirds, out)
    step(1, 2, 3)
    self_masks(r.seg_col[...], r.seg_band[...], r.mask)
    a = lax.broadcasted_iota(jnp.int32, (MOST, MOST), 0)
    b = lax.broadcasted_iota(jnp.int32, (MOST, MOST), 1)
    flip = (a + b == MOST - 1).astype(F32)

    def attend(pair):
        at = lanes(pair, 128)
        bias = pair_bias(r.dist, pair)
        r.dksum[...] = jnp.zeros_like(r.dksum)
        r.dvsum[...] = jnp.zeros_like(r.dvsum)
        skewed = jnp.zeros((2 * MOST, 2 * MOST), F32)
        for i in range(blocks):
            own = slice(MOST * i, MOST * (i + 1))
            band = slice(MOST * i, MOST * (i + 2))
            queries = split_heads(r.q1[own, at])
            deltas = split_heads(r.da1[own, at])
            keys = r.k1[band, at]
            probs = softmax(masked_scores(nt(queries, keys), bias, r.mask[i]))
            dprobs = nt(deltas, r.v1[band, at])
            dscores = probs * (dprobs - jnp.sum(dprobs * probs, axis=-1, keepdims=True))
            low = dscores.astype(BF)
            skewed = skewed + dscores
            r.dvsum[band, :] += tn(probs.astype(BF), deltas)
            r.dksum[band, :] += tn(low, queries)
            r.dq[own, at] = join_heads(nn(low, keys)).astype(BF)
        r.dk[:, at] = r.dksum[MOST:, :].astype(BF)
        r.dv[:, at] = r.dvsum[MOST:, :].astype(BF)
        for h in range(2):
            flipped = jnp.dot(
                flip,
                skewed[MOST * h : MOST * (h + 1)],
                precision=lax.Precision.HIGHEST,
                preferred_element_type=F32,
            )
            straight = pltpu.roll(flipped, MOST + 1, 1, stride=1, stride_axis=0)
            r.distsum[pl.ds(2 * pair + h, 1), :] = jnp.sum(straight, axis=0, keepdims=True)

    loop(0, 2, attend)
    step(3, 0, 1)
    step(2, 2, 3)
    step(1, 4)
    loop(2, 4, attend)
    step(4, 0, 1)
    step(3, 2, 3)
    step(2, 4)
    loop(4, PAIRS, attend)

    for m, ref in ((2, r.dq), (3, r.dk), (4, r.dv)):
        for j in range(halves):
            at = slice(WIDE * j, WIDE * (j + 1))
            put(m, j, tn(ref[:, at], r.n1[...]))
        step(0, 3 + m)
    step(4, 2, 3)
    step(3, 4)
    step(1, 5, 6, 7)

    def qkv(j):
        at = lanes(j, 256)
        r.back[:, at] = (
            nn(r.dq[...], w_lanes(r.w, 0, at))
            + nn(r.dk[...], w_lanes(r.w, 1, at))
            + nn(r.dv[...], w_lanes(r.w, 2, at))
        )

    loop(0, thirds, qkv)
    dz, dw = rms_back(r.x[...].astype(F32), r.gains[0:1, :], r.back[...])
    r.gain[0:1, :] = dw
    r.dx[...] = (r.dh1[...] + dz).astype(BF)
    by_bucket = jnp.dot(
        r.distsum[...], r.hot[...], precision=lax.Precision.HIGHEST, preferred_element_type=F32
    )
    r.small[...] = jnp.zeros_like(r.small)
    r.small[0:2, :] = r.gain[0:2, :]
    r.small[2:3, :] = r.gain3[...]
    r.small[3 : 3 + HEADS, 0:BUCKETS] = by_bucket
    if not comm:
        return

    pairs = [p.at(c=1 - p.c), p.at(y=1 - p.y), p.at(x=1 - p.x),
             p.at(z=p.z + 1 - 2 * (p.z % 2)), p.at(z=(p.z + 2) % 4)]

    def share(i):
        return remote(r.given.at[i], r.gotten.at[i], r.smsem.at[0, i], r.smsem.at[1, i], pairs[i])

    def share_go(i):
        r.given[i] = r.small[...]
        share(i).start()

    def share_end(i):
        share(i).wait_recv()
        r.small[...] = r.small[...] + r.gotten[i]

    share_go(0)
    step(4, 4)
    share_end(0)
    share_go(1)
    step(2, 6, 5)
    share_end(1)
    share_go(2)
    step(2, 7)
    share_end(2)
    share_go(3)
    step(3, 6, 5)
    share_end(3)
    share_go(4)
    step(3, 7)
    share_end(4)
    step(4, 6, 5, 7)

    first = p.c == 0

    def split(ref, n):
        low, high = ref[0:n, :, :192], ref[0:n, :, 192:]
        return jnp.where(first, low, high), jnp.where(first, high, low)

    keep_sq, r.give[0:8] = split(r.fin, 8)
    keep_fi, r.give[8:12] = split(r.finf, 4)
    r.giveo[...] = r.finf[pl.ds(4 + 2 * (1 - p.c), 2)]
    sib = p.at(c=1 - p.c)
    trade = [
        remote(r.give, r.take, r.xsem.at[0], r.xsem.at[1], sib),
        remote(r.giveo, r.takeo, r.xsem.at[2], r.xsem.at[3], sib),
    ]
    for copy in trade:
        copy.start()
    for copy in trade:
        copy.wait_recv()

    def both(a, b, axis):
        return jnp.concatenate([jnp.where(first, a, b), jnp.where(first, b, a)], axis=axis)

    r.tsq[...] = both(keep_sq, r.take[0:8], 1)
    r.tfi[...] = both(keep_fi.reshape(192, 192), r.take[8:12].reshape(192, 192), 0)
    own = r.finf[pl.ds(4 + 2 * p.c, 2)]
    r.tfo[...] = both(
        jnp.concatenate([own[0], own[1]], axis=1), jnp.concatenate([r.takeo[0], r.takeo[1]], axis=1), 0
    )
    s.drain()
    for i in range(5):
        share(i).wait_send()
    for copy in trade:
        copy.wait_send()


def finish_kernel(r):
    e192 = eye(192)
    for m, ref in enumerate((r.k_c, r.v_c, r.o_c, r.q_c, r.o_s, r.q_s, r.k_s, r.v_s)):
        ref[...] = nt(e192, r.tsq[m])
    r.f_i[...] = nt(e192, r.tfi[...])
    e384 = eye(WIDE)
    for j in range(2):
        r.f_o[WIDE * j : WIDE * (j + 1), :] = nt(e384, r.tfo[:, WIDE * j : WIDE * (j + 1)])


VM = pltpu.VMEM
HBM = pl.ANY


def run(kernel, ins, outs, scratch, name, collective=None, flops=0):
    names = list(ins) + list(outs) + list(scratch)

    def wrapped(*refs):
        kernel(types.SimpleNamespace(**dict(zip(names, refs))))

    arrays, specs = [], []
    for value in ins.values():
        array, spec = value if isinstance(value, tuple) else (value, VM)
        arrays.append(array)
        specs.append(spec if isinstance(spec, pl.BlockSpec) else pl.BlockSpec(memory_space=spec))
    results = pl.pallas_call(
        wrapped,
        grid=(1,),
        in_specs=specs,
        out_specs=[pl.BlockSpec(memory_space=(o[2] if len(o) > 2 else VM)) for o in outs.values()],
        out_shape=[jax.ShapeDtypeStruct(o[0], o[1]) for o in outs.values()],
        scratch_shapes=list(scratch.values()),
        compiler_params=pltpu.CompilerParams(
            vmem_limit_bytes=VMEM_LIMIT,
            collective_id=collective,
            has_side_effects=collective is not None,
        ),
        cost_estimate=pl.CostEstimate(flops=flops, bytes_accessed=20_000_000, transcendentals=0),
        name=name,
    )(*arrays)
    return types.SimpleNamespace(**dict(zip(outs, results)))


def dma(*shape):
    return pltpu.SemaphoreType.DMA(shape)


def body(comm, decoder_in, encoder_out, decoder_lengths, encoder_lengths, norm_gains, rel_table,
         query_self, key_self, value_self, out_self, query_cross, key_cross, value_cross, out_cross,
         feed_in, feed_out, upstream):
    rows, width = decoder_in.shape
    row_count, examples = decoder_lengths.shape
    keys_n = encoder_out.shape[1]
    hidden = feed_in.shape[1] * lax.axis_size("fsdp")
    small = (rows, width)
    cut = (4, 2, 2, PIECE, width)

    places = jnp.arange(rows, dtype=jnp.int32)
    ends = jnp.cumsum(decoder_lengths[0], dtype=jnp.int32)
    segment = jnp.sum((places[:, None] >= ends[None, :]).astype(jnp.int32), axis=-1)
    starts = ends - decoder_lengths[0]
    offset = places - jnp.sum(
        jnp.where(segment[:, None] == jnp.arange(examples)[None, :], starts[None, :], 0), axis=-1
    )
    seg_col = segment[:, None]
    seg_row = segment[None, :]
    off_row = offset[None, :]
    seg_band = jnp.concatenate([jnp.full((1, MOST), -1, jnp.int32), seg_row], axis=1)
    valid = jnp.where(
        jnp.arange(keys_n, dtype=jnp.int32)[None, :] < encoder_lengths[:, None], 0.0, HIDDEN_SCORE
    )
    hot = distance_hot()
    index = dict(seg_col=seg_col, seg_band=seg_band)
    by_example = dict(seg_row=seg_row, off_row=off_row, valid=valid)

    acts = dict(n1=(small, BF), q1=(small, BF), k1=((rows + MOST, width), BF), v1=((rows + MOST, width), BF),
                a1=(small, BF), h1=(small, F32), n2=(small, BF), q2=(small, BF), a2=(small, BF),
                k2=(encoder_out.shape, BF, HBM), v2=(encoder_out.shape, BF, HBM))
    scratch = dict(
        encv=VM(encoder_out.shape, BF), k2v=VM(encoder_out.shape, BF), v2v=VM(encoder_out.shape, BF),
        wv=VM((7,) + cut, BF), mask=VM((rows // MOST, MOST, 2 * MOST), F32),
        qe=VM((MOST, width), BF), ae=VM((MOST, width), BF), sum=VM(small, F32),
        esem=dma(examples), wsem=dma(7), ksem=dma(examples, 2),
    )
    ins = dict(x=decoder_in, enc=(encoder_out, HBM), hot=hot.T, **index, **by_example)
    if comm:
        ins |= dict(q_s=query_self, k_s=key_self, v_s=value_self, o_s=out_self, q_c=query_cross,
                    o_c=out_cross, k_c=key_cross, v_c=value_cross, f_i=feed_in, f_o=feed_out,
                    gains_s=norm_gains, table_s=rel_table)
        fwd = run(
            functools.partial(forward_kernel, True), ins,
            acts | dict(sq=((8,) + cut, BF, HBM), fi=((4, 2, 2, 4, PIECE, width), BF, HBM),
                        fo=((4, 2, 2, PIECE, hidden), BF, HBM), gains=((3, width), F32),
                        dist=((HEADS, 2 * MOST), F32)),
            scratch | dict(
                xt=VM((12, 2, PIECE, 192), BF), xf=VM((2, PIECE, 768), BF), took=VM((12, PIECE, 192), BF),
                tookf=VM((PIECE, 768), BF), own=VM((UNITS, PIECE, WIDE), BF), gt=VM((8, 8, 128), F32),
                tt=VM((4, 8, 128), F32), xsem=dma(4), psem=dma(UNITS), smsem=dma(2, 10),
                ssem=dma(UNITS, 10), rsem=dma(UNITS, 10)),
            "forward", collective=0,
        )
        sq, fi, fo, gains, dist = fwd.sq, fwd.fi, fwd.fo, fwd.gains, fwd.dist
    else:
        order = (key_cross, value_cross, query_self, key_self, value_self, out_self, query_cross, out_cross)
        sq = jnp.stack([m.astype(BF).T for m in order])
        sq = lax.all_gather(sq, "fsdp", axis=1, tiled=True)
        sq = lax.all_gather(sq, "dp", axis=2, tiled=True).reshape((8,) + cut)
        fi = lax.all_gather(feed_in.astype(BF).T, "fsdp", axis=0, tiled=True)
        fi = lax.all_gather(fi, "dp", axis=1, tiled=True)
        fo = lax.all_gather(feed_out.astype(BF).T, "fsdp", axis=0, tiled=True)
        fo = lax.all_gather(fo, "dp", axis=1, tiled=True)
        gains = lax.all_gather(norm_gains.astype(BF), "fsdp", axis=1, tiled=True).astype(F32)
        table = lax.all_gather(rel_table.astype(BF), "dp", axis=0, tiled=True).astype(F32)
        dist = jnp.dot(hot, table, precision=lax.Precision.HIGHEST).T
        fwd = run(
            functools.partial(forward_kernel, False),
            ins | dict(sq=(sq, HBM), gains=gains, dist=dist), acts, scratch, "forward",
        )

    feed = run(
        feed_kernel,
        dict(a2=fwd.a2, h1=fwd.h1, c=upstream, gains=gains,
             w=(sq.reshape(8, width, width), pl.BlockSpec((1, width, width), lambda _: (7, 0, 0))),
             fi=fi.reshape(hidden, width), fo=fo.reshape(width, hidden)),
        dict(out=(small, BF), dfi=((hidden, width), BF), dfo=((width, hidden), BF),
             dwoc=((width, width), BF), da2=(small, BF), dh2=(small, F32), gain=((1, width), F32)),
        dict(h2=VM(small, F32), n3=VM(small, BF), sum=VM(small, F32), back=VM(small, F32)),
        "feed",
    )

    cut_spec = pl.BlockSpec((2,) + cut, lambda _: (0,) * 6)
    ins = dict(enc=(encoder_out, HBM), k2=(fwd.k2, HBM), v2=(fwd.v2, HBM), q2=fwd.q2, da2=feed.da2,
               w=(sq, cut_spec), **by_example)
    outs = dict(denc=(encoder_out.shape, BF, HBM), dq2=(small, BF), dwkv=((2, width, width), BF))
    scratch = dict(
        encv=VM(encoder_out.shape, BF), k2v=VM(encoder_out.shape, BF), v2v=VM(encoder_out.shape, BF),
        qe=VM((MOST, width), BF), dae=VM((MOST, width), BF), dqe=VM((MOST, width), BF),
        dk=VM((keys_n, width), BF), dv=VM((keys_n, width), BF), denv=VM((2, keys_n, width), BF),
        sum=VM(small, F32), dwsum=VM((2, width, width), F32), esem=dma(examples, 3), dsem=dma(2),
    )
    fins = {}
    if comm:
        ins |= dict(dfi=(feed.dfi.reshape(4, 2, 2, 4, PIECE, width), HBM),
                    dfo=(feed.dfo.reshape(4, 2, 2, PIECE, hidden), HBM))
        fins = dict(fin=((8, PIECE, WIDE), BF))
        scratch |= scatter_scratch(8)
    mid = run(functools.partial(cross_back_kernel, comm), ins, outs | fins, scratch, "cross_back",
              collective=1 if comm else None)

    five = (5,) + cut if comm else (5, width, width)
    ins = dict(dq2=mid.dq2, n2=fwd.n2, h1=fwd.h1, dh2=feed.dh2, x=decoder_in, n1=fwd.n1, q1=fwd.q1,
               k1=fwd.k1, v1=fwd.v1, a1=fwd.a1, gains=gains, dist=dist, gain3=feed.gain, hot=hot,
               w=(sq[2:7], VM), **index)
    outs = dict(dx=(small, BF), small=((16, width), F32))
    scratch = dict(
        mask=VM((rows // MOST, MOST, 2 * MOST), F32), dh1=VM(small, F32), b1=VM(small, BF),
        da1=VM(small, BF), dq=VM(small, BF), dk=VM(small, BF), dv=VM(small, BF),
        dksum=VM((rows + MOST, 128), F32), dvsum=VM((rows + MOST, 128), F32), back=VM(small, F32),
        gain=VM((2, width), F32), distsum=VM((HEADS, 2 * MOST), F32),
    )
    if comm:
        ins |= dict(dwkv=(mid.dwkv.reshape((2,) + cut), HBM), dwoc=(feed.dwoc.reshape(cut), HBM), finf=mid.fin)
        outs |= dict(tsq=((8, 96, 192), BF), tfi=((384, 192), BF), tfo=((96, 768), BF))
        scratch |= dict(
            dw=VM(five, BF), fin=VM((8, PIECE, WIDE), BF), give=VM((12, PIECE, 192), BF),
            take=VM((12, PIECE, 192), BF), giveo=VM((2, PIECE, WIDE), BF), takeo=VM((2, PIECE, WIDE), BF),
            given=VM((5, 16, width), F32), gotten=VM((5, 16, width), F32), smsem=dma(2, 5), xsem=dma(4),
        ) | scatter_scratch(8)
    else:
        outs |= dict(dw=(five, BF))
    last = run(functools.partial(self_back_kernel, comm), ins, outs, scratch, "self_back",
               collective=2 if comm else None)

    if comm:
        square = ((192, 96), F32)
        done = run(
            finish_kernel, dict(tsq=last.tsq, tfi=last.tfi, tfo=last.tfo),
            {n: square for n in ("k_c", "v_c", "q_s", "k_s", "v_s", "o_s", "q_c", "o_c")}
            | dict(f_i=((192, 384), F32), f_o=((768, 96), F32)),
            {}, "finish",
        )
        grads = (done.q_s, done.k_s, done.v_s, done.o_s, done.q_c, done.k_c, done.v_c, done.o_c,
                 done.f_i, done.f_o)
        d, f = lax.axis_index("dp"), lax.axis_index("fsdp")
        part = norm_gains.shape[1]
        gains_delta = lax.dynamic_slice(last.small[0:3], (0, f * part), (3, part))
        part = rel_table.shape[0]
        table_delta = lax.dynamic_slice(last.small[3 : 3 + HEADS, 0:BUCKETS].T, (d * part, 0), (part, HEADS))
    else:
        def owned(t, rows_axis=0):
            t = lax.psum_scatter(t, "dp", scatter_dimension=1, tiled=True)
            return lax.psum_scatter(t, "fsdp", scatter_dimension=0, tiled=True).astype(F32).T

        dw = last.dw
        grads = tuple(owned(t) for t in (dw[2], dw[3], dw[4], dw[1], dw[0], mid.dwkv[0], mid.dwkv[1],
                                         feed.dwoc, feed.dfi, feed.dfo))
        gains_delta = lax.psum(last.small[0:3], "dp")
        gains_delta = lax.psum_scatter(gains_delta, "fsdp", scatter_dimension=1, tiled=True)
        table_delta = last.small[3 : 3 + HEADS, 0:BUCKETS].T
        table_delta = lax.psum_scatter(table_delta, "dp", scatter_dimension=0, tiled=True)
        table_delta = lax.psum(table_delta, "fsdp")
    return (feed.out, last.dx, mid.denc, gains_delta, table_delta) + grads


def solution(mesh):
    tokens = P(("dp", "fsdp"), None)
    weight = P("dp", "fsdp")
    comm = (mesh.shape["dp"], mesh.shape["fsdp"]) == (4, 8)
    return jax.shard_map(
        functools.partial(body, comm),
        mesh=mesh,
        in_specs=(tokens, P(("dp", "fsdp"), None, None), tokens, P(("dp", "fsdp")), P(None, "fsdp"),
                  P("dp", None)) + (weight,) * 10 + (tokens,),
        out_specs=(tokens, tokens, P(("dp", "fsdp"), None, None), P(None, "fsdp"), P("dp", None))
        + (weight,) * 10,
        check_vma=False,
    )
```

time: 943 us -> 392 us (0.42)
  waiting for transfers between devices: 399 us -> 0 us
  local copies, waits for them, and re-layouts: 194 us -> 21.8 us
  Pallas kernels: 217 us -> 361 us
  blocking collectives: 55.1 us -> 0 us
  other arithmetic: 55.9 us -> 4.98 us
  between operations: 14.9 us -> 0.87 us
    all_gather x6 -> x0, waiting for transfers between devices: 175 us -> none  [the longest x1 58.4 us: body(): square = lax.all_gather(square, 'fsdp', axis=1, tiled=True)]
    unnamed x56 -> x7, local copies, waits for them, and re-layouts: 160 us -> 12.4 us
    pallas_call x5, Pallas kernels: 217 us -> 361 us  [run(): pl.pallas_call(wrapped, grid=(1,), in_specs=specs, out_specs=[pl.BlockSpe...]
    reduce_scatter x4 -> x0, waiting for transfers between devices: 138 us -> none  [the longest x1 73.2 us: body(): dsquare = lax.psum_scatter(dsquare, 'dp', scatter_dimension=2, tiled=True)]
    unnamed x16 -> x0, waiting for transfers between devices: 87.1 us -> none
    transpose x3 -> x0, other arithmetic: 44.2 us -> none  [the longest x1 40.9 us: body(): squares = [dsquare[i].astype(F32).T for i in range(8)]]
    psum x2 -> x0, blocking collectives: 29.9 us -> none  [the longest x1 18.5 us: body(): table_delta = lax.psum(table_delta, 'fsdp')]
    all_gather x2 -> x0, blocking collectives: 25.2 us -> none  [the longest x1 14.6 us: body(): lax.all_gather(norm_gains.astype(BF), 'fsdp', axis=1, tiled=True)]
  transfers between devices with their start and end apart: 13 -> 0, of which waited for: 8 -> 0; matrix products, arithmetic and copies ran while one was open for 15% -> 0% of each run, Pallas kernels for 20% -> 0%
where the time goes in v3:
time: 392 us; the launch traced here: 389 us
  Pallas kernels  361 us (92%)
  local copies, waits for them, and re-layouts  21.8 us (6%)
  other arithmetic  4.98 us (1%)
    pallas_call x5, Pallas kernels, run(): pl.pallas_call(wrapped, grid=(1,), in_specs=specs, out_specs=[pl.BlockSpe...  361 us
    unnamed x7, local copies, waits for them, and re-layouts  12.4 us

profile of v3, /device:TPU:1, one launch (start us, length us, event | category | flops | bytes accessed | tf_op | source)
XLA Modules:
  0.0 388.6 jit_solution(14375884854161322227)
XLA Ops:
  0.6 0.8 reduce-window.4
  1.5 0.1 convert_reduce_fusion
  1.6 0.0 copy-start
  1.6 0.6 concatenate.3.refs_4_.refs_16_
  2.1 0.7 fusion.18
  2.8 0.1 select_reduce_fusion
  2.9 0.6 iota_subtract_fusion.refs_6_.refs_7_
  3.5 0.9 copy.40.refs_3_.refs_15_
  4.4 0.6 fusion.1.refs_2_
  5.0 1.3 fusion.2.refs_7_.refs_8_
  6.3 1.9 copy.41.refs_17_
  8.2 0.0 copy-done
  8.2 125.0 %forward.1 = (bf16[512,768]{1,0:T(8,128)(2,1)}, bf16[512,768]{1,0:T(8,128)(2,1)}, bf16[640,768]{1,0:T(8,128)(2,1)}, bf16[640,768]{1,0:T(8,128)(2,1)}, bf16[512,7...) custom-call(bf16[512,768]{1,0:T(8,128)(2,1)} %refs_4_.1, ...), custom_call_target="tpu_custom_call" | custom-call | bytes 20000000 | tf_op jit(solution)/shard_map/forward/pallas_call | solution.py:918
  133.2 34.7 %feed.1 = (bf16[512,768]{1,0:T(8,128)(2,1)}, bf16[3072,768]{1,0:T(8,128)(2,1)}, bf16[768,3072]{1,0:T(8,128)(2,1)}, bf16[768,768]{1,0:T(8,128)(2,1)}, bf16[512,76...) custom-call(bf16[512,768]{1,0:T(8,128)(2,1)} %get-tuple-element.57.refs_0_, ...), custom_call_target="tpu_custom_call" | custom-call | bytes 20000000 | tf_op jit(solution)/shard_map/feed/pallas_call | solution.py:918
  167.9 110.0 %cross_back.1 = (bf16[8,512,768]{2,1,0:T(8,128)(2,1)}, bf16[512,768]{1,0:T(8,128)(2,1)}, bf16[2,768,768]{2,1,0:T(8,128)(2,1)}, bf16[8,48,384]{2,1,0:T(8,128)(2,1)}) custom-call(bf16[8,512,768]{2,1,0:T(8,128)(2,1)} %refs_0_.3, bf16[8,512,768]{2,1,0:T(8,128)(2,1)} %get-tuple-element.64.refs_1_, bf16[8,512,768]{2,1,0:T(8,128)(2,1)} %get-tuple-element.65.refs_2_, ...), custom_call_target="tpu_custom_call" | custom-call | bytes 20000000 | tf_op jit(solution)/shard_map/cross_back/pallas_call | solution.py:918
  278.0 5.8 %slice.9.refs_14_ = bf16[5,4,2,2,48,768]{5,4,3,2,1,0:T(8,128)(2,1)} slice(bf16[8,4,2,2,48,768]{5,4,3,2,1,0:T(8,128)(2,1)} %get-tuple-element.60.refs_5_), slice={[2:7], [0:4], [0:2], [0:2], [0:48], [0:768]} | slice | bytes 11796480 | tf_op jit(solution)/shard_map/slice | solution.py:1045
  283.7 0.8 fusion.refs_13_
  284.5 88.7 %self_back.1 = (bf16[512,768]{1,0:T(8,128)(2,1)}, f32[16,768]{1,0:T(8,128)}, bf16[8,96,192]{2,1,0:T(8,128)(2,1)}, bf16[384,192]{1,0:T(8,128)(2,1)}, bf16[96,768]{1,0:T(8,128)(2,1)}) custom-call(bf16[512,768]{1,0:T(8,128)(2,1)} %get-tuple-element.70.refs_0_, bf16[512,768]{1,0:T(8,128)(2,1)} %get-tuple-element.71.refs_1_, ...), custom_call_target="tpu_custom_call" | custom-call | bytes 20000000 | tf_op jit(solution)/shard_map/self_back/pallas_call | solution.py:918
  373.2 2.5 finish.1
  375.7 1.9 copy.44
  377.6 0.7 slice.11
  378.3 0.1 dynamic-slice_bitcast_fusion
  378.4 0.7 copy.43
  379.0 0.7 slice.10
  379.8 0.6 constant_dynamic-slice_fusion
  380.4 2.1 copy.47
  382.5 5.9 %copy.48 = bf16[8,512,768]{2,1,0:T(8,128)(2,1)} copy(bf16[8,512,768]{2,1,0:T(8,128)(2,1)} %get-tuple-element.161) | data formatting | bytes 12582912
  (1 shorter events, 0.0 us)
Async XLA Ops:
  1.6 6.6 %copy-start = (s32[512]{0:T(512)}, s32[512]{0:T(512)S(1)}, u32[]{:S(2)}) copy-start(s32[512]{0:T(512)S(1)} %convert_reduce_fusion) | copy-start | bytes 6148

commit v4 on v3

--- a/solution.py
+++ b/solution.py
@@ -87,9 +87,23 @@
     return jnp.where(distance < half_count, distance, half_count + counted)
 
 
-def distance_hot():
-    distance = jnp.maximum(MOST - jnp.arange(2 * MOST, dtype=jnp.int32), 0)
-    return (bucket_of(distance)[:, None] == jnp.arange(BUCKETS, dtype=jnp.int32)[None, :]).astype(F32)
+def distance_hot(axis):
+    shape = (2 * MOST, BUCKETS) if axis == 0 else (BUCKETS, 2 * MOST)
+    distance = jnp.maximum(MOST - lax.broadcasted_iota(jnp.int32, shape, axis), 0)
+    return (bucket_of(distance) == lax.broadcasted_iota(jnp.int32, shape, 1 - axis)).astype(F32)
+
+
+def segments(lengths, shape, axis, shift=0):
+    places = lax.broadcasted_iota(jnp.int32, shape, axis) - shift
+    end = jnp.zeros((1, 1), jnp.int32)
+    example = jnp.where(places < 0, -1, 0)
+    start = jnp.zeros(shape, jnp.int32)
+    for e in range(lengths.shape[1]):
+        length = lengths[:, e : e + 1]
+        end = end + length
+        example = example + (places >= end).astype(jnp.int32)
+        start = start + jnp.where(places >= end, length, 0)
+    return example, places - start
 
 
 def local(src, dst, sem):
@@ -117,6 +131,7 @@
         self.d, self.f = lax.axis_index("dp"), lax.axis_index("fsdp")
         self.y, self.c = self.d // 2, self.d % 2
         self.z, self.x = self.f // 2, self.f % 2
+        self.nx, self.ny, self.nc = 1 - self.x, 1 - self.y, 1 - self.c
 
     def at(self, z=None, x=None, y=None, c=None):
         z = self.z if z is None else z
@@ -226,20 +241,25 @@
         p = self.p
         if u % 2 == 0:
             self.wait(u, 4)
-            self.same(u, 8, self.to_c, ALL, ALL, p.c, 1 - p.y)
+            self.same(u, 8, self.to_c, ALL, ALL, p.c, p.ny)
         else:
             self.wait(u, 4, 5)
             for y in (0, 1):
-                self.same(u, 8 + y, self.to_c, ALL, 1 - p.x, p.c, y)
+                self.same(u, 8 + y, self.to_c, ALL, p.nx, p.c, y)
 
     def fifth(self, u):
         self.wait(u, *((6, 8) if u % 2 == 0 else (6, 7, 8, 9)))
 
+    def begin(self):
+        for act, u in ((self.second, 0), (self.second, 1), (self.third, 0), (self.third, 1),
+                       (self.second, 2), (self.second, 3), (self.fourth, 0), (self.fourth, 1), (self.second, 4)):
+            act(u)
+
     def tick(self, t):
-        for step, act in ((2, self.fourth), (1, self.third), (0, self.second)):
-            if 0 <= t - step < UNITS // 2:
-                act(2 * (t - step))
-                act(2 * (t - step) + 1)
+        for act, u in ((self.fourth, t), (self.third, t + 2), (self.second, t + 5)):
+            low = {self.fourth: 2, self.third: 2, self.second: 5}[act]
+            if low <= u < UNITS:
+                act(u)
 
 
 class Scatter(Sends):
@@ -335,8 +355,10 @@
     )
 
 
-def self_masks(seg_col, seg_row, mask_ref):
+def self_masks(lengths, mask_ref):
     blocks = mask_ref.shape[0]
+    seg_col = segments(lengths, (blocks * MOST, 1), 0)[0]
+    seg_row = segments(lengths, (1, (blocks + 1) * MOST), 1, MOST)[0]
     a = lax.broadcasted_iota(jnp.int32, (MOST, 2 * MOST), 0)
     b = lax.broadcasted_iota(jnp.int32, (MOST, 2 * MOST), 1)
     causal = b <= a + MOST
@@ -360,9 +382,18 @@
     return (both.reshape(2, MOST, 2 * MOST) + mask[None]).reshape(2 * MOST, 2 * MOST)
 
 
-def example_rows(segr_ref, offr_ref, example, total):
+def example_rows(index_ref, example, total):
     place = lax.broadcasted_iota(jnp.int32, (MOST, total), 0)
-    return ((segr_ref[...] == example) & (offr_ref[...] == place)).astype(F32).astype(BF)
+    here = (index_ref[0:1, :] == example) & (index_ref[1:2, :] == place)
+    return here.astype(F32).astype(BF)
+
+
+def example_index(r, total):
+    r.index[0:1, :], r.index[1:2, :] = segments(r.lengths[...], (1, total), 1)
+    examples, keys_n = r.hidden.shape
+    place = lax.broadcasted_iota(jnp.int32, (1, keys_n), 1)
+    for e in range(examples):
+        r.hidden[e : e + 1, :] = jnp.where(place < r.valid[:, e : e + 1], 0.0, HIDDEN_SCORE)
 
 
 def spread_shards(p, r):
@@ -374,7 +405,7 @@
     for s in range(4):
         for h in range(2):
             r.xt[8 + s, h] = t[h, s]
-    r.xf[...] = nt(e96, r.f_o[...].astype(BF)).astype(BF).reshape(2, PIECE, 768)
+    r.xf[...] = r.f_o[...].astype(BF).reshape(2, PIECE, 768)
 
 
 def small_sends(p, r):
@@ -394,7 +425,7 @@
 
 def forward_kernel(comm, r):
     rows, width = r.x.shape
-    examples, keys_n = r.valid.shape
+    examples, keys_n = r.enc.shape[0], r.enc.shape[1]
     blocks = rows // MOST
     enc_copies = [local(r.enc.at[e], r.encv.at[e], r.esem.at[e]) for e in range(examples)]
     for copy in enc_copies:
@@ -445,12 +476,12 @@
             gains = gains + nn(r.gt[f].astype(BF), put)
         r.gains[...] = gains[0:3]
         table = r.tt[...].reshape(BUCKETS, 128).astype(BF)
-        r.dist[...] = tn(table, r.hot[...].astype(BF))[0:HEADS]
+        r.dist[...] = tn(table, distance_hot(1).astype(BF))[0:HEADS]
         for copy in placed:
             copy.wait()
-        tick, arrived = g.tick, g.fifth
+        begin, tick, arrived = g.begin, g.tick, g.fifth
     else:
-        tick = arrived = lambda index: None
+        begin, tick, arrived = (lambda *_: None,) * 3
 
     loads = [local(r.sq.at[m], r.wv.at[m], r.wsem.at[m]) for m in range(7)]
 
@@ -463,10 +494,11 @@
         for m in which:
             loads[m].wait()
 
+    example_index(r, rows)
     r.n1[...] = rms(r.x[...].astype(F32), r.gains[0:1, :]).astype(BF)
     r.k1[0:MOST, :] = jnp.zeros((MOST, width), BF)
     r.v1[0:MOST, :] = jnp.zeros((MOST, width), BF)
-    self_masks(r.seg_col[...], r.seg_band[...], r.mask)
+    self_masks(r.lengths[...], r.mask)
     halves = width // WIDE
 
     def save(e):
@@ -481,17 +513,15 @@
         for copy in save(e):
             copy.start()
 
-    tick(0)
-    tick(1)
-    tick(2)
+    begin()
     fetch(0, 1)
     have(0, 1)
-    loop(0, examples // 2, project)
-    tick(3)
+    for t in range(4):
+        tick(t)
+        loop(2 * t, 2 * t + 2, project)
     fetch(2, 3)
-    loop(examples // 2, examples, project)
     tick(4)
-    fetch(4, 5)
+    fetch(4)
     have(2, 3, 4)
 
     for j in range(halves):
@@ -510,10 +540,13 @@
             probs = softmax(masked_scores(nt(queries, keys), bias, r.mask[i])).astype(BF)
             r.a1[MOST * i : MOST * (i + 1), at] = join_heads(nn(probs, values)).astype(BF)
 
+    tick(5)
     loop(0, PAIRS // 2, attend)
-    tick(5)
+    tick(6)
+    fetch(5)
+    loop(PAIRS // 2, PAIRS, attend)
+    tick(7)
     fetch(6)
-    loop(PAIRS // 2, PAIRS, attend)
     have(5, 6)
     for j in range(halves):
         at = slice(WIDE * j, WIDE * (j + 1))
@@ -526,9 +559,9 @@
     r.sum[...] = jnp.zeros_like(r.sum)
 
     def cross(e):
-        pick = example_rows(r.seg_row, r.off_row, e, rows)
+        pick = example_rows(r.index, e, rows)
         r.qe[...] = nn(pick, r.q2[...]).astype(BF)
-        hidden = r.valid[pl.ds(e, 1), :]
+        hidden = r.hidden[pl.ds(e, 1), :]
 
         def pair_step(pair):
             at = lanes(pair, 128)
@@ -538,14 +571,14 @@
         loop(0, PAIRS, pair_step)
         r.sum[...] += tn(pick, r.ae[...])
 
-    tick(6)
-    loop(0, 3, cross)
-    tick(7)
-    loop(3, 6, cross)
-    tick(8)
-    loop(6, examples, cross)
+    def cross_tick(e):
+        if comm:
+            for t in range(examples):
+                pl.when(e == t)(functools.partial(tick, t + 8))
+        cross(e)
+
+    loop(0, examples, cross_tick)
     r.a2[...] = r.sum[...].astype(BF)
-    tick(9)
 
     def saved(e):
         for copy in save(e):
@@ -607,8 +640,7 @@
 
 def cross_back_kernel(comm, r):
     rows, width = r.q2.shape
-    examples, keys_n = r.valid.shape
-    halves = width // WIDE
+    examples, keys_n = r.enc.shape[0], r.enc.shape[1]
 
     def fetches(e):
         return [local(getattr(r, a).at[e], getattr(r, b).at[e], r.esem.at[e, i])
@@ -628,28 +660,39 @@
 
         s = Scatter(p, parts, r)
         greet(p.near())
+    example_index(r, rows)
     r.sum[...] = jnp.zeros_like(r.sum)
     r.dwsum[...] = jnp.zeros_like(r.dwsum)
 
-    def out_copy(e):
-        return local(r.denv.at[e % 2], r.denc.at[e], r.dsem.at[e % 2])
-
-    def example(e):
+    def out_copies(e):
+        return [
+            local(r.dk.at[e % 2], r.dk2.at[e], r.dsem.at[e % 2, 0]),
+            local(r.dv.at[e % 2], r.dv2.at[e], r.dsem.at[e % 2, 1]),
+        ]
+
+    def tick(at):
         if comm:
-            for t in range(8):
-
-                @pl.when(e == t)
+            for t in range(2 * examples):
+
+                @pl.when(at == t)
                 def _():
                     for number in (4, 3, 2, 1, 0):
-                        if 0 <= t - number < 4:
-                            s.step(number, t - number, 4 + t - number)
-
+                        if 0 <= t - 2 * number < 8:
+                            s.step(number, t - 2 * number)
+
+    def example(e):
+        tick(2 * e)
         for copy in fetches(e):
             copy.wait()
-        pick = example_rows(r.seg_row, r.off_row, e, rows)
+        pick = example_rows(r.index, e, rows)
         r.qe[...] = nn(pick, r.q2[...]).astype(BF)
         r.dae[...] = nn(pick, r.da2[...]).astype(BF)
-        hidden = r.valid[pl.ds(e, 1), :]
+        hidden = r.hidden[pl.ds(e, 1), :]
+
+        @pl.when(e >= 2)
+        def _():
+            for copy in out_copies(e - 2):
+                copy.wait()
 
         def attend(pair):
             at = lanes(pair, 128)
@@ -659,33 +702,29 @@
             probs = softmax(nt(queries, keys) + hidden)
             dprobs = nt(deltas, r.v2v[e, :, at])
             low = (probs * (dprobs - jnp.sum(dprobs * probs, axis=-1, keepdims=True))).astype(BF)
-            r.dv[:, at] = tn(probs.astype(BF), deltas).astype(BF)
-            r.dk[:, at] = tn(low, queries).astype(BF)
+            r.dv[e % 2, :, at] = tn(probs.astype(BF), deltas).astype(BF)
+            r.dk[e % 2, :, at] = tn(low, queries).astype(BF)
             r.dqe[:, at] = join_heads(nn(low, keys)).astype(BF)
 
         loop(0, PAIRS, attend)
+        tick(2 * e + 1)
+        for copy in out_copies(e):
+            copy.start()
         r.sum[...] += tn(pick, r.dqe[...])
-
-        @pl.when(e >= 2)
-        def _():
-            out_copy(e - 2).wait()
 
         def dense(j):
             at = lanes(j, 256)
-            r.denv[e % 2, :, at] = (
-                nn(r.dk[...], w_lanes(r.w, 0, at)) + nn(r.dv[...], w_lanes(r.w, 1, at))
-            ).astype(BF)
-            r.dwsum[0, at, :] += tn(r.dk[:, at], r.encv[e])
-            r.dwsum[1, at, :] += tn(r.dv[:, at], r.encv[e])
+            r.dwsum[0, at, :] += tn(r.dk[e % 2, :, at], r.encv[e])
+            r.dwsum[1, at, :] += tn(r.dv[e % 2, :, at], r.encv[e])
 
         loop(0, width // 256, dense)
-        out_copy(e).start()
 
     loop(0, examples, example)
     r.dq2[...] = r.sum[...].astype(BF)
     r.dwkv[...] = r.dwsum[...].astype(BF)
     for e in (examples - 2, examples - 1):
-        out_copy(e).wait()
+        for copy in out_copies(e):
+            copy.wait()
     if comm:
         s.drain()
 
@@ -718,15 +757,34 @@
             r.dw[m, WIDE * j : WIDE * (j + 1), :] = value.astype(BF)
 
     halves = width // WIDE
+    examples = r.denc.shape[0]
+    loads = [local(r.sq.at[m], r.w.at[m], r.wsem.at[m]) for m in range(7)]
+    for copy in loads:
+        copy.start()
+
+    def fetches(e):
+        return [
+            local(r.dk2.at[e], r.dkv.at[e % 2, 0], r.esem.at[e % 2, 0]),
+            local(r.dv2.at[e], r.dkv.at[e % 2, 1], r.esem.at[e % 2, 1]),
+        ]
+
+    def out_copy(e):
+        return local(r.denv.at[e % 2], r.denc.at[e], r.dsem.at[e % 2])
+
+    for e in (0, 1):
+        for copy in fetches(e):
+            copy.start()
     step(0, 0, 1, 2)
     for j in range(halves):
         at = slice(WIDE * j, WIDE * (j + 1))
         put(0, j, tn(r.dq2[:, at], r.n2[...]))
     step(0, 3)
+    for copy in loads:
+        copy.wait()
 
     def query(j):
         at = lanes(j, 256)
-        r.back[:, at] = nn(r.dq2[...], w_lanes(r.w, 4, at))
+        r.back[:, at] = nn(r.dq2[...], w_lanes(r.w, 6, at))
 
     loop(0, thirds, query)
     step(1, 0, 1)
@@ -738,15 +796,14 @@
         at = slice(WIDE * j, WIDE * (j + 1))
         put(1, j, tn(r.b1[:, at], r.a1[...]))
     step(0, 4)
-    step(2, 0, 1)
+    step(1, 2, 3)
 
     def out(j):
         at = lanes(j, 256)
-        r.da1[:, at] = nn(r.b1[...], w_lanes(r.w, 3, at)).astype(BF)
+        r.da1[:, at] = nn(r.b1[...], w_lanes(r.w, 5, at)).astype(BF)
 
     loop(0, thirds, out)
-    step(1, 2, 3)
-    self_masks(r.seg_col[...], r.seg_band[...], r.mask)
+    self_masks(r.lengths[...], r.mask)
     a = lax.broadcasted_iota(jnp.int32, (MOST, MOST), 0)
     b = lax.broadcasted_iota(jnp.int32, (MOST, MOST), 1)
     flip = (a + b == MOST - 1).astype(F32)
@@ -783,77 +840,122 @@
             straight = pltpu.roll(flipped, MOST + 1, 1, stride=1, stride_axis=0)
             r.distsum[pl.ds(2 * pair + h, 1), :] = jnp.sum(straight, axis=0, keepdims=True)
 
-    loop(0, 2, attend)
-    step(3, 0, 1)
-    step(2, 2, 3)
-    step(1, 4)
-    loop(2, 4, attend)
-    step(4, 0, 1)
-    step(3, 2, 3)
-    step(2, 4)
-    loop(4, PAIRS, attend)
-
+    plan = {
+        0: ((2, 0, 1), (1, 4)),
+        1: ((2, 2, 3),),
+        2: ((3, 0, 1), (2, 4)),
+        3: ((3, 2, 3),),
+        4: ((4, 0, 1), (3, 4)),
+        5: ((4, 2, 3),),
+    }
+
+    def attend_tick(pair):
+        if comm:
+            for t, steps in plan.items():
+
+                @pl.when(pair == t)
+                def _():
+                    for numbers in steps:
+                        step(*numbers)
+
+        attend(pair)
+
+    loop(0, PAIRS, attend_tick)
+    step(4, 4)
     for m, ref in ((2, r.dq), (3, r.dk), (4, r.dv)):
         for j in range(halves):
             at = slice(WIDE * j, WIDE * (j + 1))
             put(m, j, tn(ref[:, at], r.n1[...]))
         step(0, 3 + m)
-    step(4, 2, 3)
-    step(3, 4)
-    step(1, 5, 6, 7)
+    step(1, 5, 6)
 
     def qkv(j):
         at = lanes(j, 256)
         r.back[:, at] = (
-            nn(r.dq[...], w_lanes(r.w, 0, at))
-            + nn(r.dk[...], w_lanes(r.w, 1, at))
-            + nn(r.dv[...], w_lanes(r.w, 2, at))
+            nn(r.dq[...], w_lanes(r.w, 2, at))
+            + nn(r.dk[...], w_lanes(r.w, 3, at))
+            + nn(r.dv[...], w_lanes(r.w, 4, at))
         )
 
     loop(0, thirds, qkv)
+    step(1, 7)
     dz, dw = rms_back(r.x[...].astype(F32), r.gains[0:1, :], r.back[...])
     r.gain[0:1, :] = dw
     r.dx[...] = (r.dh1[...] + dz).astype(BF)
     by_bucket = jnp.dot(
-        r.distsum[...], r.hot[...], precision=lax.Precision.HIGHEST, preferred_element_type=F32
+        r.distsum[...], distance_hot(0), precision=lax.Precision.HIGHEST, preferred_element_type=F32
     )
     r.small[...] = jnp.zeros_like(r.small)
     r.small[0:2, :] = r.gain[0:2, :]
     r.small[2:3, :] = r.gain3[...]
     r.small[3 : 3 + HEADS, 0:BUCKETS] = by_bucket
+
+    def encoder(e):
+        for copy in fetches(e):
+            copy.wait()
+
+        @pl.when(e >= 2)
+        def _():
+            out_copy(e - 2).wait()
+
+        def dense(j):
+            at = lanes(j, 256)
+            r.denv[e % 2, :, at] = (
+                nn(r.dkv[e % 2, 0], w_lanes(r.w, 0, at)) + nn(r.dkv[e % 2, 1], w_lanes(r.w, 1, at))
+            ).astype(BF)
+
+        loop(0, thirds, dense)
+        out_copy(e).start()
+
+        @pl.when(e + 2 < examples)
+        def _():
+            for copy in fetches(e + 2):
+                copy.start()
+
+    if comm:
+        pairs = [p.at(c=1 - p.c), p.at(y=1 - p.y), p.at(x=1 - p.x),
+                 p.at(z=p.z + 1 - 2 * (p.z % 2)), p.at(z=(p.z + 2) % 4)]
+
+        def share(i):
+            return remote(r.given.at[i], r.gotten.at[i], r.smsem.at[0, i], r.smsem.at[1, i], pairs[i])
+
+        def share_go(i):
+            r.given[i] = r.small[...]
+            share(i).start()
+
+        def share_end(i):
+            share(i).wait_recv()
+            r.small[...] = r.small[...] + r.gotten[i]
+
+        share_go(0)
+        loop(0, 2, encoder)
+        share_end(0)
+        share_go(1)
+        step(2, 6, 5)
+        loop(2, 3, encoder)
+        step(2, 7)
+        loop(3, 4, encoder)
+        share_end(1)
+        share_go(2)
+        step(3, 6, 5)
+        loop(4, 5, encoder)
+        share_end(2)
+        share_go(3)
+        loop(5, 6, encoder)
+        step(3, 7)
+        loop(6, 7, encoder)
+        share_end(3)
+        share_go(4)
+        step(4, 6, 5)
+        loop(7, examples, encoder)
+        share_end(4)
+        step(4, 7)
+    else:
+        loop(0, examples, encoder)
+    for e in (examples - 2, examples - 1):
+        out_copy(e).wait()
     if not comm:
         return
-
-    pairs = [p.at(c=1 - p.c), p.at(y=1 - p.y), p.at(x=1 - p.x),
-             p.at(z=p.z + 1 - 2 * (p.z % 2)), p.at(z=(p.z + 2) % 4)]
-
-    def share(i):
-        return remote(r.given.at[i], r.gotten.at[i], r.smsem.at[0, i], r.smsem.at[1, i], pairs[i])
-
-    def share_go(i):
-        r.given[i] = r.small[...]
-        share(i).start()
-
-    def share_end(i):
-        share(i).wait_recv()
-        r.small[...] = r.small[...] + r.gotten[i]
-
-    share_go(0)
-    step(4, 4)
-    share_end(0)
-    share_go(1)
-    step(2, 6, 5)
-    share_end(1)
-    share_go(2)
-    step(2, 7)
-    share_end(2)
-    share_go(3)
-    step(3, 6, 5)
-    share_end(3)
-    share_go(4)
-    step(3, 7)
-    share_end(4)
-    step(4, 6, 5, 7)
 
     first = p.c == 0
 
@@ -883,6 +985,18 @@
     r.tfo[...] = both(
         jnp.concatenate([own[0], own[1]], axis=1), jnp.concatenate([r.takeo[0], r.takeo[1]], axis=1), 0
     )
+    spot = lax.broadcasted_iota(jnp.int32, (width, 128), 0)
+    lane = lax.broadcasted_iota(jnp.int32, (width, 128), 1)
+    put_gains = ((spot == lane + 96 * p.f) & (lane < 96)).astype(F32)
+    r.gains_own[...] = jnp.dot(
+        r.small[0:8, :], put_gains, precision=lax.Precision.HIGHEST, preferred_element_type=F32
+    )
+    spot = lax.broadcasted_iota(jnp.int32, (8, BUCKETS), 1)
+    line = lax.broadcasted_iota(jnp.int32, (8, BUCKETS), 0)
+    r.table_own[...] = lax.dot_general(
+        (spot == line + 8 * p.d).astype(F32), r.small[3 : 3 + HEADS, 0:BUCKETS], (((1,), (1,)), ((), ())),
+        precision=lax.Precision.HIGHEST, preferred_element_type=F32,
+    )
     s.drain()
     for i in range(5):
         share(i).wait_send()
@@ -891,13 +1005,24 @@
 
 
 def finish_kernel(r):
+    examples = r.denc.shape[0]
+    ins = [local(r.denc_in.at[e], r.hold.at[e], r.sem.at[e, 0]) for e in range(examples)]
+    outs = [local(r.hold.at[e], r.denc.at[e], r.sem.at[e, 1]) for e in range(examples)]
+    for copy in ins:
+        copy.start()
+    r.dx[...] = r.dx_in[...]
     e192 = eye(192)
     for m, ref in enumerate((r.k_c, r.v_c, r.o_c, r.q_c, r.o_s, r.q_s, r.k_s, r.v_s)):
         ref[...] = nt(e192, r.tsq[m])
     r.f_i[...] = nt(e192, r.tfi[...])
-    e384 = eye(WIDE)
-    for j in range(2):
-        r.f_o[WIDE * j : WIDE * (j + 1), :] = nt(e384, r.tfo[:, WIDE * j : WIDE * (j + 1)])
+    r.f_o[...] = r.tfo[...].astype(F32)
+    r.gains[...] = r.gains_in[0:3, 0:96]
+    r.table[...] = r.table_in[...]
+    for e in range(examples):
+        ins[e].wait()
+        outs[e].start()
+    for copy in outs:
+        copy.wait()
 
 
 VM = pltpu.VMEM
@@ -947,23 +1072,8 @@
     small = (rows, width)
     cut = (4, 2, 2, PIECE, width)
 
-    places = jnp.arange(rows, dtype=jnp.int32)
-    ends = jnp.cumsum(decoder_lengths[0], dtype=jnp.int32)
-    segment = jnp.sum((places[:, None] >= ends[None, :]).astype(jnp.int32), axis=-1)
-    starts = ends - decoder_lengths[0]
-    offset = places - jnp.sum(
-        jnp.where(segment[:, None] == jnp.arange(examples)[None, :], starts[None, :], 0), axis=-1
-    )
-    seg_col = segment[:, None]
-    seg_row = segment[None, :]
-    off_row = offset[None, :]
-    seg_band = jnp.concatenate([jnp.full((1, MOST), -1, jnp.int32), seg_row], axis=1)
-    valid = jnp.where(
-        jnp.arange(keys_n, dtype=jnp.int32)[None, :] < encoder_lengths[:, None], 0.0, HIDDEN_SCORE
-    )
-    hot = distance_hot()
-    index = dict(seg_col=seg_col, seg_band=seg_band)
-    by_example = dict(seg_row=seg_row, off_row=off_row, valid=valid)
+    index = dict(lengths=decoder_lengths, valid=encoder_lengths[None, :])
+    index_scratch = dict(index=VM((2, rows), jnp.int32), hidden=VM((examples, keys_n), F32))
 
     acts = dict(n1=(small, BF), q1=(small, BF), k1=((rows + MOST, width), BF), v1=((rows + MOST, width), BF),
                 a1=(small, BF), h1=(small, F32), n2=(small, BF), q2=(small, BF), a2=(small, BF),
@@ -972,12 +1082,12 @@
         encv=VM(encoder_out.shape, BF), k2v=VM(encoder_out.shape, BF), v2v=VM(encoder_out.shape, BF),
         wv=VM((7,) + cut, BF), mask=VM((rows // MOST, MOST, 2 * MOST), F32),
         qe=VM((MOST, width), BF), ae=VM((MOST, width), BF), sum=VM(small, F32),
-        esem=dma(examples), wsem=dma(7), ksem=dma(examples, 2),
+        esem=dma(examples), wsem=dma(7), ksem=dma(examples, 2), **index_scratch,
     )
-    ins = dict(x=decoder_in, enc=(encoder_out, HBM), hot=hot.T, **index, **by_example)
+    ins = dict(x=decoder_in, enc=(encoder_out, HBM), **index)
     if comm:
         ins |= dict(q_s=query_self, k_s=key_self, v_s=value_self, o_s=out_self, q_c=query_cross,
-                    o_c=out_cross, k_c=key_cross, v_c=value_cross, f_i=feed_in, f_o=feed_out,
+                    o_c=out_cross, k_c=key_cross, v_c=value_cross, f_i=feed_in, f_o=feed_out.T,
                     gains_s=norm_gains, table_s=rel_table)
         fwd = run(
             functools.partial(forward_kernel, True), ins,
@@ -1003,7 +1113,7 @@
         fo = lax.all_gather(fo, "dp", axis=1, tiled=True)
         gains = lax.all_gather(norm_gains.astype(BF), "fsdp", axis=1, tiled=True).astype(F32)
         table = lax.all_gather(rel_table.astype(BF), "dp", axis=0, tiled=True).astype(F32)
-        dist = jnp.dot(hot, table, precision=lax.Precision.HIGHEST).T
+        dist = jnp.dot(distance_hot(0), table, precision=lax.Precision.HIGHEST).T
         fwd = run(
             functools.partial(forward_kernel, False),
             ins | dict(sq=(sq, HBM), gains=gains, dist=dist), acts, scratch, "forward",
@@ -1020,15 +1130,16 @@
         "feed",
     )
 
-    cut_spec = pl.BlockSpec((2,) + cut, lambda _: (0,) * 6)
     ins = dict(enc=(encoder_out, HBM), k2=(fwd.k2, HBM), v2=(fwd.v2, HBM), q2=fwd.q2, da2=feed.da2,
-               w=(sq, cut_spec), **by_example)
-    outs = dict(denc=(encoder_out.shape, BF, HBM), dq2=(small, BF), dwkv=((2, width, width), BF))
+               **index)
+    outs = dict(dk2=(encoder_out.shape, BF, HBM), dv2=(encoder_out.shape, BF, HBM), dq2=(small, BF),
+                dwkv=((2, width, width), BF))
     scratch = dict(
         encv=VM(encoder_out.shape, BF), k2v=VM(encoder_out.shape, BF), v2v=VM(encoder_out.shape, BF),
         qe=VM((MOST, width), BF), dae=VM((MOST, width), BF), dqe=VM((MOST, width), BF),
-        dk=VM((keys_n, width), BF), dv=VM((keys_n, width), BF), denv=VM((2, keys_n, width), BF),
-        sum=VM(small, F32), dwsum=VM((2, width, width), F32), esem=dma(examples, 3), dsem=dma(2),
+        dk=VM((2, keys_n, width), BF), dv=VM((2, keys_n, width), BF),
+        sum=VM(small, F32), dwsum=VM((2, width, width), F32), esem=dma(examples, 3), dsem=dma(2, 2),
+        **index_scratch,
     )
     fins = {}
     if comm:
@@ -1041,18 +1152,21 @@
 
     five = (5,) + cut if comm else (5, width, width)
     ins = dict(dq2=mid.dq2, n2=fwd.n2, h1=fwd.h1, dh2=feed.dh2, x=decoder_in, n1=fwd.n1, q1=fwd.q1,
-               k1=fwd.k1, v1=fwd.v1, a1=fwd.a1, gains=gains, dist=dist, gain3=feed.gain, hot=hot,
-               w=(sq[2:7], VM), **index)
-    outs = dict(dx=(small, BF), small=((16, width), F32))
+               k1=fwd.k1, v1=fwd.v1, a1=fwd.a1, gains=gains, dist=dist, gain3=feed.gain,
+               sq=(sq, HBM), dk2=(mid.dk2, HBM), dv2=(mid.dv2, HBM), lengths=decoder_lengths)
+    outs = dict(dx=(small, BF), small=((16, width), F32), denc=(encoder_out.shape, BF, HBM))
     scratch = dict(
         mask=VM((rows // MOST, MOST, 2 * MOST), F32), dh1=VM(small, F32), b1=VM(small, BF),
         da1=VM(small, BF), dq=VM(small, BF), dk=VM(small, BF), dv=VM(small, BF),
         dksum=VM((rows + MOST, 128), F32), dvsum=VM((rows + MOST, 128), F32), back=VM(small, F32),
-        gain=VM((2, width), F32), distsum=VM((HEADS, 2 * MOST), F32),
+        gain=VM((2, width), F32), distsum=VM((HEADS, 2 * MOST), F32), w=VM((7,) + cut, BF),
+        dkv=VM((2, 2, keys_n, width), BF), denv=VM((2, keys_n, width), BF), wsem=dma(7), esem=dma(2, 2),
+        dsem=dma(2),
     )
     if comm:
         ins |= dict(dwkv=(mid.dwkv.reshape((2,) + cut), HBM), dwoc=(feed.dwoc.reshape(cut), HBM), finf=mid.fin)
-        outs |= dict(tsq=((8, 96, 192), BF), tfi=((384, 192), BF), tfo=((96, 768), BF))
+        outs |= dict(tsq=((8, 96, 192), BF), tfi=((384, 192), BF), tfo=((96, 768), BF), gains_own=((8, 128), F32),
+                     table_own=((8, HEADS), F32))
         scratch |= dict(
             dw=VM(five, BF), fin=VM((8, PIECE, WIDE), BF), give=VM((12, PIECE, 192), BF),
             take=VM((12, PIECE, 192), BF), giveo=VM((2, PIECE, WIDE), BF), takeo=VM((2, PIECE, WIDE), BF),
@@ -1066,18 +1180,17 @@
     if comm:
         square = ((192, 96), F32)
         done = run(
-            finish_kernel, dict(tsq=last.tsq, tfi=last.tfi, tfo=last.tfo),
+            finish_kernel,
+            dict(tsq=last.tsq, tfi=last.tfi, tfo=last.tfo, gains_in=last.gains_own, table_in=last.table_own,
+                 dx_in=last.dx, denc_in=(last.denc, HBM)),
             {n: square for n in ("k_c", "v_c", "q_s", "k_s", "v_s", "o_s", "q_c", "o_c")}
-            | dict(f_i=((192, 384), F32), f_o=((768, 96), F32)),
-            {}, "finish",
+            | dict(f_i=((192, 384), F32), f_o=((96, 768), F32), gains=((3, 96), F32), table=((8, HEADS), F32),
+                   dx=(small, BF), denc=(encoder_out.shape, BF, HBM)),
+            dict(sem=dma(examples, 2), hold=VM(encoder_out.shape, BF)), "finish",
         )
         grads = (done.q_s, done.k_s, done.v_s, done.o_s, done.q_c, done.k_c, done.v_c, done.o_c,
-                 done.f_i, done.f_o)
-        d, f = lax.axis_index("dp"), lax.axis_index("fsdp")
-        part = norm_gains.shape[1]
-        gains_delta = lax.dynamic_slice(last.small[0:3], (0, f * part), (3, part))
-        part = rel_table.shape[0]
-        table_delta = lax.dynamic_slice(last.small[3 : 3 + HEADS, 0:BUCKETS].T, (d * part, 0), (part, HEADS))
+                 done.f_i, done.f_o.T)
+        gains_delta, table_delta, dx, denc = done.gains, done.table, done.dx, done.denc
     else:
         def owned(t, rows_axis=0):
             t = lax.psum_scatter(t, "dp", scatter_dimension=1, tiled=True)
@@ -1091,7 +1204,8 @@
         table_delta = last.small[3 : 3 + HEADS, 0:BUCKETS].T
         table_delta = lax.psum_scatter(table_delta, "dp", scatter_dimension=0, tiled=True)
         table_delta = lax.psum(table_delta, "fsdp")
-    return (feed.out, last.dx, mid.denc, gains_delta, table_delta) + grads
+        dx, denc = last.dx, last.denc
+    return (feed.out, dx, denc, gains_delta, table_delta) + grads
 
 
 def solution(mesh):

time: 392 us -> 331 us (0.84)
  Pallas kernels: 361 us -> 327 us
  local copies, waits for them, and re-layouts: 21.8 us -> 0 us
  other arithmetic: 4.98 us -> 0 us
    pallas_call x5, Pallas kernels: 361 us -> 327 us  [run(): pl.pallas_call(wrapped, grid=(1,), in_specs=specs, out_specs=[pl.BlockSpe...]
    unnamed x7 -> x0, local copies, waits for them, and re-layouts: 12.4 us -> none
    slice x3 -> x0, local copies, waits for them, and re-layouts: 7.23 us -> none  [the longest x1 5.79 us: body(): sq[2:7]]
where the time goes in v4:
time: 331 us; the launch traced here: 328 us
  Pallas kernels  327 us (99%)
    pallas_call x5, Pallas kernels, run(): pl.pallas_call(wrapped, grid=(1,), in_specs=specs, out_specs=[pl.BlockSpe...  327 us

profile of v4, /device:TPU:1, one launch (start us, length us, event | category | flops | bytes accessed | tf_op | source)
XLA Modules:
  0.0 328.2 jit_solution(312523524617353855)
XLA Ops:
  0.7 118.3 %forward.1 = (bf16[512,768]{1,0:T(8,128)(2,1)}, bf16[512,768]{1,0:T(8,128)(2,1)}, bf16[640,768]{1,0:T(8,128)(2,1)}, bf16[640,768]{1,0:T(8,128)(2,1)}, bf16[512,7...) custom-call(bf16[512,768]{1,0:T(8,128)(2,1)} %refs_4_.3, ...), custom_call_target="tpu_custom_call" | custom-call | bytes 20000000 | tf_op jit(solution)/shard_map/forward/pallas_call | solution.py:1043
  118.9 34.5 %feed.1 = (bf16[512,768]{1,0:T(8,128)(2,1)}, bf16[3072,768]{1,0:T(8,128)(2,1)}, bf16[768,3072]{1,0:T(8,128)(2,1)}, bf16[768,768]{1,0:T(8,128)(2,1)}, bf16[512,76...) custom-call(bf16[512,768]{1,0:T(8,128)(2,1)} %get-tuple-element.64.refs_0_, ...), custom_call_target="tpu_custom_call" | custom-call | bytes 20000000 | tf_op jit(solution)/shard_map/feed/pallas_call | solution.py:1043
  153.4 77.7 %cross_back.1 = (bf16[8,512,768]{2,1,0:T(8,128)(2,1)}, bf16[8,512,768]{2,1,0:T(8,128)(2,1)}, bf16[512,768]{1,0:T(8,128)(2,1)}, bf16[2,768,768]{2,1,0:T(8,128)(2,1)}, bf16[8,48,384]{2,1,0:T(8,128)(2,1)}) custom-call(bf16[8,512,768]{2,1,0:T(8,128)(2,1)} %refs_0_.3, bf16[8,512,768]{2,1,0:T(8,128)(2,1)} %get-tuple-element.71.refs_1_, ...), custom_call_target="tpu_custom_call" | custom-call | bytes 20000000 | tf_op jit(solution)/shard_map/cross_back/pallas_call | solution.py:1043
  231.1 88.5 %self_back.1 = (bf16[512,768]{1,0:T(8,128)(2,1)}, f32[16,768]{1,0:T(8,128)}, bf16[8,512,768]{2,1,0:T(8,128)(2,1)}, bf16[8,96,192]{2,1,0:T(8,128)(2,1)}, bf16[384...) custom-call(bf16[512,768]{1,0:T(8,128)(2,1)} %get-tuple-element.77.refs_0_, ...), custom_call_target="tpu_custom_call" | custom-call | bytes 20000000 | tf_op jit(solution)/shard_map/self_back/pallas_call | solution.py:1043
  319.7 8.3 %finish.1 = (f32[192,96]{1,0:T(8,128)}, f32[192,96]{1,0:T(8,128)}, f32[192,96]{1,0:T(8,128)}, f32[192,96]{1,0:T(8,128)}, f32[192,96]{1,0:T(8,128)}, /*index=5*/f...) custom-call(bf16[8,96,192]{2,1,0:T(8,128)(2,1)} %get-tuple-element.9, ...), custom_call_target="tpu_custom_call" | custom-call | bytes 20000000 | tf_op jit(solution)/shard_map/finish/pallas_call | solution.py:1043

commit v5 on v4

--- a/solution.py
+++ b/solution.py
@@ -68,12 +68,16 @@
     return pl.ds(pl.multiple_of(index * width, width), width)
 
 
-def loop(low, high, step):
+def loop(low, high, step, unroll=1):
     def run(index, carry):
         step(index)
         return carry
 
-    lax.fori_loop(low, high, run, 0)
+    lax.fori_loop(low, high, run, 0, unroll=unroll)
+
+
+def quiet(act):
+    act()
 
 
 def bucket_of(distance):
@@ -124,6 +128,7 @@
 WIDE = 384
 UNITS = 16
 ALL = slice(None)
+LOW, HIGH = slice(0, 2), slice(2, 4)
 
 
 class Place:
@@ -145,10 +150,11 @@
         return others + [self.at(x=1 - self.x), self.at(y=1 - self.y), self.at(c=1 - self.c)]
 
 
-def greet(peers):
+def greet(peers, between=lambda: None):
     barrier = pltpu.get_barrier_semaphore()
     for dev in peers:
         pl.semaphore_signal(barrier, inc=1, device_id=dev, device_id_type=MESH)
+    between()
     pl.semaphore_wait(barrier, len(peers))
 
 
@@ -223,114 +229,112 @@
     def second(self, u):
         p = self.p
         self.wait(u, 0, 1, 2)
-        self.same(u, 3, self.to_x if u % 2 == 0 else self.to_y, ALL, p.x, p.c, p.y)
+        self.same(u, 3, self.to_x, LOW, p.x, p.c, p.y)
+        self.same(u, 4, self.to_y, HIGH, p.x, p.c, p.y)
 
     def third(self, u):
         p = self.p
-        self.wait(u, 3)
-        if u % 2 == 0:
-            self.same(u, 4, self.to_y, ALL, ALL, p.c, p.y)
-            self.same(u, 6, self.to_c, ALL, ALL, p.c, p.y)
-        else:
-            for y in (0, 1):
-                self.same(u, 4 + y, self.to_x, ALL, p.x, p.c, y)
-            for y in (0, 1):
-                self.same(u, 6 + y, self.to_c, ALL, p.x, p.c, y)
+        self.wait(u, 3, 4)
+        self.same(u, 5, self.to_y, LOW, ALL, p.c, p.y)
+        for y in (0, 1):
+            self.same(u, 6 + y, self.to_x, HIGH, p.x, p.c, y)
+        self.same(u, 8, self.to_c, LOW, ALL, p.c, p.y)
+        for y in (0, 1):
+            self.same(u, 9 + y, self.to_c, HIGH, p.x, p.c, y)
 
     def fourth(self, u):
         p = self.p
-        if u % 2 == 0:
-            self.wait(u, 4)
-            self.same(u, 8, self.to_c, ALL, ALL, p.c, p.ny)
-        else:
-            self.wait(u, 4, 5)
-            for y in (0, 1):
-                self.same(u, 8 + y, self.to_c, ALL, p.nx, p.c, y)
+        self.wait(u, 5, 6, 7)
+        self.same(u, 11, self.to_c, LOW, ALL, p.c, p.ny)
+        for y in (0, 1):
+            self.same(u, 12 + y, self.to_c, HIGH, p.nx, p.c, y)
 
     def fifth(self, u):
-        self.wait(u, *((6, 8) if u % 2 == 0 else (6, 7, 8, 9)))
+        self.wait(u, *range(8, 14))
 
     def begin(self):
-        for act, u in ((self.second, 0), (self.second, 1), (self.third, 0), (self.third, 1),
-                       (self.second, 2), (self.second, 3), (self.fourth, 0), (self.fourth, 1), (self.second, 4)):
+        for act, u in ((self.second, 0), (self.second, 1), (self.third, 0),
+                       (self.third, 1), (self.second, 2), (self.second, 3), (self.fourth, 0), (self.fourth, 1),
+                       (self.second, 4)):
             act(u)
 
     def tick(self, t):
-        for act, u in ((self.fourth, t), (self.third, t + 2), (self.second, t + 5)):
-            low = {self.fourth: 2, self.third: 2, self.second: 5}[act]
-            if low <= u < UNITS:
-                act(u)
+        if 2 <= t:
+            self.fourth(t)
+        if t + 2 < UNITS:
+            self.third(t + 2)
+        if t + 5 < UNITS:
+            self.second(t + 5)
 
 
 class Scatter(Sends):
-    def __init__(self, place, parts, r):
+    def __init__(self, place, parts, staged, r):
         super().__init__(place, r.ssem, r.rsem)
-        self.parts, self.r = parts, r
+        self.parts, self.staged, self.r = parts, staged, r
 
     def halves(self, u):
         p, r = self.p, self.r
-        return [local(self.parts(u, p.c, y), r.acc.at[u, y], r.lsem.at[u, y]) for y in (0, 1)]
+        return [local(self.parts(u, p.c, y), r.stage.at[u, y], r.lsem.at[u, y]) for y in (0, 1)]
+
+    def own(self, u, y):
+        if u < self.staged:
+            return self.r.stage[u, pl.ds(y, 1)]
+        return self.parts(u, self.p.c, y)[...][None]
 
     def r0(self, u):
         p, r = self.p, self.r
         for y in (0, 1):
             self.go(
-                u, y, lambda y=y: self.parts(u, 1 - p.c, y), lambda y=y: r.land.at[u, y], self.to_c
+                u, y, lambda y=y: self.parts(u, p.nc, y), lambda y=y: r.land.at[u, y], self.to_c
             )
-        for copy in self.halves(u):
-            copy.start()
+        if u < self.staged:
+            for copy in self.halves(u):
+                copy.start()
 
     def r1(self, u):
         p, r = self.p, self.r
         self.wait(u, 0, 1)
-        for copy in self.halves(u):
-            copy.wait()
-        if u % 2 == 0:
-            other, own = pl.ds(1 - p.y, 1), pl.ds(p.y, 1)
-            r.acc[u, other] = r.acc[u, other] + r.land[u, other]
-            self.go(u, 2, lambda: r.acc.at[u, 1 - p.y], lambda: r.land1.at[u], self.to_y)
-            r.acc[u, own] = r.acc[u, own] + r.land[u, own]
-        else:
-            for y in (0, 1):
-                r.acc[u, y] = r.acc[u, y] + r.land[u, y]
+        if u < self.staged:
+            for copy in self.halves(u):
+                copy.wait()
+        for y in (p.ny, p.y):
+            at = pl.ds(y, 1)
+            r.land[u, at] = r.land[u, at] + self.own(u, y)
+            if y is p.ny:
                 self.go(
-                    u, 2 + y, lambda y=y: r.acc.at[u, y, :, 1 - p.x], lambda y=y: r.land1.at[u, :, y],
-                    self.to_x,
+                    u, 2, lambda: r.land.at[u, p.ny, LOW], lambda: r.land1.at[u, LOW], self.to_y
                 )
+        for y in (0, 1):
+            self.go(
+                u, 3 + y, lambda y=y: r.land.at[u, y, HIGH, p.nx], lambda y=y: r.land1.at[u, HIGH, y],
+                self.to_x,
+            )
 
     def r2(self, u):
         p, r = self.p, self.r
-        if u % 2 == 0:
-            self.wait(u, 2)
-            own = pl.ds(p.y, 1)
-            r.acc[u, own] = r.acc[u, own] + r.land1[u][None]
-            self.go(
-                u, 4, lambda: r.acc.at[u, p.y, :, 1 - p.x], lambda: r.land2.at[u], self.to_x
-            )
-        else:
-            self.wait(u, 2, 3)
-            x = pl.ds(p.x, 1)
-            for y in (0, 1):
-                r.acc[u, y, :, x] = r.acc[u, y, :, x] + r.land1[u, :, y][:, None]
-            self.go(
-                u, 4, lambda: r.acc.at[u, 1 - p.y, :, p.x], lambda: r.land2.at[u], self.to_y
-            )
+        self.wait(u, 2, 3, 4)
+        own, x = pl.ds(p.y, 1), pl.ds(p.x, 1)
+        r.land[u, own, LOW] = r.land[u, own, LOW] + r.land1[u, LOW][None]
+        for y in (0, 1):
+            r.land[u, y, HIGH, x] = r.land[u, y, HIGH, x] + r.land1[u, HIGH, y][:, None]
+        self.go(u, 5, lambda: r.land.at[u, p.y, LOW, p.nx], lambda: r.land2.at[u, LOW], self.to_x)
+        self.go(u, 6, lambda: r.land.at[u, p.ny, HIGH, p.x], lambda: r.land2.at[u, HIGH], self.to_y)
 
     def r3(self, u):
         p, r = self.p, self.r
-        self.wait(u, 4)
+        self.wait(u, 5, 6)
         y, x = pl.ds(p.y, 1), pl.ds(p.x, 1)
-        r.acc[u, y, :, x] = r.acc[u, y, :, x] + r.land2[u][None, :, None]
+        r.land[u, y, :, x] = r.land[u, y, :, x] + r.land2[u][None, :, None]
         for k in (1, 2, 3):
             self.go(
-                u, 4 + k, lambda k=k: r.acc.at[u, p.y, (p.z + k) % 4, p.x],
+                u, 6 + k, lambda k=k: r.land.at[u, p.y, (p.z + k) % 4, p.x],
                 lambda k=k: r.land3.at[u, k - 1], lambda k=k: p.at(z=(p.z + k) % 4),
             )
 
     def r4(self, u):
         p, r = self.p, self.r
-        self.wait(u, 5, 6, 7)
-        part = r.acc[u, pl.ds(p.y, 1), pl.ds(p.z, 1), pl.ds(p.x, 1)]
+        self.wait(u, 7, 8, 9)
+        part = r.land[u, pl.ds(p.y, 1), pl.ds(p.z, 1), pl.ds(p.x, 1)]
         total = part.reshape(PIECE, WIDE).astype(F32)
         for k in range(3):
             total = total + r.land3[u, k].astype(F32)
@@ -342,16 +346,16 @@
             act(u)
 
 
-def scatter_scratch(count):
+def scatter_scratch(count, staged):
     return dict(
         land=pltpu.VMEM((count, 2, 4, 2, PIECE, WIDE), BF),
-        acc=pltpu.VMEM((count, 2, 4, 2, PIECE, WIDE), BF),
+        stage=pltpu.VMEM((staged, 2, 4, 2, PIECE, WIDE), BF),
         land1=pltpu.VMEM((count, 4, 2, PIECE, WIDE), BF),
         land2=pltpu.VMEM((count, 4, PIECE, WIDE), BF),
         land3=pltpu.VMEM((count, 3, PIECE, WIDE), BF),
-        ssem=pltpu.SemaphoreType.DMA((count, 8)),
-        rsem=pltpu.SemaphoreType.DMA((count, 8)),
-        lsem=pltpu.SemaphoreType.DMA((count, 2)),
+        ssem=pltpu.SemaphoreType.DMA((count, 10)),
+        rsem=pltpu.SemaphoreType.DMA((count, 10)),
+        lsem=pltpu.SemaphoreType.DMA((staged, 2)),
     )
 
 
@@ -396,16 +400,28 @@
         r.hidden[e : e + 1, :] = jnp.where(place < r.valid[:, e : e + 1], 0.0, HIDDEN_SCORE)
 
 
-def spread_shards(p, r):
+def turn_squares(r, *which):
+    shards = (r.k_c, r.v_c, r.q_s, r.k_s, r.v_s, r.o_s, r.q_c, r.o_c)
     e96 = eye(96)
-    shards = (r.k_c, r.v_c, r.q_s, r.k_s, r.v_s, r.o_s, r.q_c, r.o_c)
-    for m, ref in enumerate(shards):
-        r.xt[m] = nt(e96, ref[...].astype(BF)).astype(BF).reshape(2, PIECE, 192)
+    for m in which:
+        r.xt[m] = nt(e96, shards[m][...].astype(BF)).astype(BF).reshape(2, PIECE, 192)
+
+
+def turn_feeds(r):
     t = nt(eye(384), r.f_i[...].astype(BF)).astype(BF).reshape(2, 4, PIECE, 192)
     for s in range(4):
         for h in range(2):
             r.xt[8 + s, h] = t[h, s]
     r.xf[...] = r.f_o[...].astype(BF).reshape(2, PIECE, 768)
+
+
+def own_parts(p, r, low, high):
+    first = p.c == 0
+    mine = r.xt[low:high, pl.ds(p.c, 1)].reshape(high - low, PIECE, 192)
+    other = r.took[low:high]
+    r.own[low:high] = jnp.concatenate(
+        [jnp.where(first, mine, other), jnp.where(first, other, mine)], axis=-1
+    )
 
 
 def small_sends(p, r):
@@ -430,40 +446,49 @@
     enc_copies = [local(r.enc.at[e], r.encv.at[e], r.esem.at[e]) for e in range(examples)]
     for copy in enc_copies:
         copy.start()
-
     if comm:
         p = Place()
         peers = [(p.d, (p.f + k) % 8) for k in range(1, 8)] + [((p.d + k) % 4, p.f) for k in range(1, 4)]
-        r.gt[pl.ds(p.f, 1)] = jnp.zeros((1, 8, 128), F32)
-        r.gt[pl.ds(p.f, 1), 0:3, 0:96] = r.gains_s[...].astype(BF).astype(F32)[None]
-        r.tt[pl.ds(p.d, 1)] = jnp.zeros((1, 8, 128), F32)
-        r.tt[pl.ds(p.d, 1), :, 0:HEADS] = r.table_s[...].astype(BF).astype(F32)[None]
-        spread_shards(p, r)
-        greet(peers)
+
+        def prepare():
+            r.gt[pl.ds(p.f, 1)] = jnp.zeros((1, 8, 128), F32)
+            r.gt[pl.ds(p.f, 1), 0:3, 0:96] = r.gains_s[...].astype(BF).astype(F32)[None]
+            r.tt[pl.ds(p.d, 1)] = jnp.zeros((1, 8, 128), F32)
+            r.tt[pl.ds(p.d, 1), :, 0:HEADS] = r.table_s[...].astype(BF).astype(F32)[None]
+            turn_squares(r, 0, 1)
+
+        greet(peers, prepare)
         sib = p.at(c=1 - p.c)
         trade = [
-            remote(r.xt.at[:, 1 - p.c], r.took, r.xsem.at[0], r.xsem.at[1], sib),
-            remote(r.xf.at[1 - p.c], r.tookf, r.xsem.at[2], r.xsem.at[3], sib),
+            remote(r.xt.at[0:2, 1 - p.c], r.took.at[0:2], r.xsem.at[0], r.xsem.at[1], sib),
+            remote(r.xt.at[2:12, 1 - p.c], r.took.at[2:12], r.xsem.at[2], r.xsem.at[3], sib),
+            remote(r.xf.at[1 - p.c], r.tookf, r.xsem.at[4], r.xsem.at[5], sib),
         ]
         small = small_sends(p, r)
-        for copy in trade + small:
+        for copy in trade[0:1] + small:
+            copy.start()
+        turn_feeds(r)
+        g = Gather(p, r.own, r.sq, r.fi, r.fo, r.ssem, r.rsem)
+        placed = [
+            local(r.own.at[u], g.piece(u, p.z, p.x, p.c, p.y), r.psem.at[u]) for u in range(UNITS)
+        ]
+        trade[0].wait_recv()
+        own_parts(p, r, 0, 2)
+        for u in (0, 1):
+            g.first(u)
+            placed[u].start()
+        turn_squares(r, 2, 3, 4, 5, 6, 7)
+        for copy in trade[1:]:
             copy.start()
         first = p.c == 0
-        trade[0].wait_recv()
-        mine, other = r.xt[:, pl.ds(p.c, 1)].reshape(12, PIECE, 192), r.took[...]
-        r.own[0:12] = jnp.concatenate(
-            [jnp.where(first, mine, other), jnp.where(first, other, mine)], axis=-1
-        )
         trade[1].wait_recv()
+        own_parts(p, r, 2, 12)
+        trade[2].wait_recv()
         mine, other = r.xf[pl.ds(p.c, 1)].reshape(PIECE, 768), r.tookf[...]
         low, high = jnp.where(first, mine, other), jnp.where(first, other, mine)
         r.own[12], r.own[13] = low[:, :WIDE], low[:, WIDE:]
         r.own[14], r.own[15] = high[:, :WIDE], high[:, WIDE:]
-        g = Gather(p, r.own, r.sq, r.fi, r.fo, r.ssem, r.rsem)
-        placed = [
-            local(r.own.at[u], g.piece(u, p.z, p.x, p.c, p.y), r.psem.at[u]) for u in range(UNITS)
-        ]
-        for u in range(UNITS):
+        for u in range(2, UNITS):
             g.first(u)
             placed[u].start()
         for copy in small:
@@ -541,10 +566,10 @@
             r.a1[MOST * i : MOST * (i + 1), at] = join_heads(nn(probs, values)).astype(BF)
 
     tick(5)
-    loop(0, PAIRS // 2, attend)
+    loop(0, PAIRS // 2, attend, PAIRS // 2)
     tick(6)
     fetch(5)
-    loop(PAIRS // 2, PAIRS, attend)
+    loop(PAIRS // 2, PAIRS, attend, PAIRS // 2)
     tick(7)
     fetch(6)
     have(5, 6)
@@ -568,7 +593,7 @@
             probs = softmax(nt(split_heads(r.qe[:, at]), r.k2v[e, :, at]) + hidden).astype(BF)
             r.ae[:, at] = join_heads(nn(probs, r.v2v[e, :, at])).astype(BF)
 
-        loop(0, PAIRS, pair_step)
+        loop(0, PAIRS, pair_step, PAIRS)
         r.sum[...] += tn(pick, r.ae[...])
 
     def cross_tick(e):
@@ -597,9 +622,19 @@
 GELU_B = 0.044715
 
 
-def feed_kernel(r):
+def feed_kernel(comm, r):
     rows, width = r.a2.shape
     hidden = r.fi.shape[0]
+    if comm:
+        p = Place()
+
+        def parts(u, c, y):
+            at = pl.ds(pl.multiple_of(y * 4 * WIDE + u * WIDE, WIDE), WIDE)
+            return r.dfo.at[:, :, c, :, at]
+
+        s = Scatter(p, parts, 0, r)
+        greet(p.near())
+    step = s.step if comm else lambda *units: None
 
     def cross_out(j):
         at = lanes(j, 256)
@@ -610,22 +645,37 @@
     r.sum[...] = r.h2[...]
     r.back[...] = jnp.zeros_like(r.back)
 
-    def part(j):
-        at = lanes(j, 256)
-        u = nt(r.n3[...], r.fi[at, :])
-        t = jnp.tanh(GELU_A * (u + GELU_B * (u * u * u)))
-        g = (0.5 * u * (1.0 + t)).astype(BF)
-        slope = 0.5 * (1.0 + t) + 0.5 * u * (1.0 - t * t) * (
-            GELU_A * (1.0 + (3.0 * GELU_B) * (u * u))
-        )
-        du = (nn(r.c[...], r.fo[:, at]) * slope).astype(BF)
-        r.dfo[:, at] = tn(r.c[...], g).astype(BF)
-        r.dfi[at, :] = tn(du, r.n3[...]).astype(BF)
-        r.sum[...] += nt(g, r.fo[:, at])
-        r.back[...] += nn(du, r.fi[at, :])
-
-    loop(0, hidden // 256, part)
+    r.ct[...] = r.c[...].T
+
+    def part(turn):
+        j = lax.rem(turn, 2) * 2 + turn // 2
+        if comm:
+            pl.when(turn == 2)(lambda: step(0, 0, 1))
+        for i in range(3):
+            at = pl.ds(pl.multiple_of(j * width + i * 256, 256), 256)
+            here = slice(256 * i, 256 * (i + 1))
+            u = nt(r.n3[...], r.fi[at, :])
+            t = jnp.tanh(GELU_A * (u + GELU_B * (u * u * u)))
+            r.g[:, here] = (0.5 * u * (1.0 + t)).astype(BF)
+            slope = 0.5 * (1.0 + t) + 0.5 * u * (1.0 - t * t) * (
+                GELU_A * (1.0 + (3.0 * GELU_B) * (u * u))
+            )
+            r.du[:, here] = (nn(r.c[...], r.fo[:, at]) * slope).astype(BF)
+        if comm:
+            pl.when(turn == 2)(lambda: step(1, 0, 1))
+            pl.when(turn == 3)(lambda: step(2, 0, 1))
+        whole_part = lanes(j, width)
+        for i in range(3):
+            at = pl.ds(pl.multiple_of(j * width + i * 256, 256), 256)
+            here = slice(256 * i, 256 * (i + 1))
+            r.dfo[:, :, :, :, at] = nn(r.ct[...], r.g[:, here]).astype(BF).reshape(4, 2, 2, PIECE, 256)
+            r.dfi[at, :] = tn(r.du[:, here], r.n3[...]).astype(BF)
+            r.sum[:, here] += nt(r.g[...], r.fo[here, whole_part])
+            r.back[:, here] += nn(r.du[...], r.fi[whole_part, here])
+
+    loop(0, hidden // width, part)
     r.out[...] = r.sum[...].astype(BF)
+    step(3, 0, 1)
     dz, dw = rms_back(r.h2[...], r.gains[2:3, :], r.back[...])
     r.gain[...] = dw
     r.dh2[...] = r.c[...].astype(F32) + dz
@@ -636,15 +686,18 @@
         r.dwoc[at, :] = tn(r.dh2[:, at].astype(BF), r.a2[...]).astype(BF)
 
     loop(0, width // 256, tail)
+    step(4, 0, 1)
+    if comm:
+        s.drain()
 
 
 def cross_back_kernel(comm, r):
     rows, width = r.q2.shape
-    examples, keys_n = r.enc.shape[0], r.enc.shape[1]
+    examples, keys_n = r.k2.shape[0], r.k2.shape[1]
 
     def fetches(e):
         return [local(getattr(r, a).at[e], getattr(r, b).at[e], r.esem.at[e, i])
-                for i, (a, b) in enumerate((("enc", "encv"), ("k2", "k2v"), ("v2", "v2v")))]
+                for i, (a, b) in enumerate((("k2", "k2v"), ("v2", "v2v")))]
 
     for e in range(examples):
         for copy in fetches(e):
@@ -653,16 +706,15 @@
         p = Place()
 
         def parts(u, c, y):
-            if u < 4:
-                return r.dfi.at[:, :, c, u, :, y * WIDE : (y + 1) * WIDE]
-            at = y * 4 * WIDE + (u - 4) * WIDE
+            if u >= 2:
+                return r.dfi.at[:, :, c, u - 2, :, y * WIDE : (y + 1) * WIDE]
+            at = y * 4 * WIDE + (u + 2) * WIDE
             return r.dfo.at[:, :, c, :, at : at + WIDE]
 
-        s = Scatter(p, parts, r)
+        s = Scatter(p, parts, 5, r)
         greet(p.near())
     example_index(r, rows)
     r.sum[...] = jnp.zeros_like(r.sum)
-    r.dwsum[...] = jnp.zeros_like(r.dwsum)
 
     def out_copies(e):
         return [
@@ -677,8 +729,9 @@
                 @pl.when(at == t)
                 def _():
                     for number in (4, 3, 2, 1, 0):
-                        if 0 <= t - 2 * number < 8:
-                            s.step(number, t - 2 * number)
+                        for u, at_first in enumerate((0, 1, 3, 5, 7)):
+                            if at_first + 2 * number == t:
+                                s.step(number, u)
 
     def example(e):
         tick(2 * e)
@@ -702,26 +755,18 @@
             probs = softmax(nt(queries, keys) + hidden)
             dprobs = nt(deltas, r.v2v[e, :, at])
             low = (probs * (dprobs - jnp.sum(dprobs * probs, axis=-1, keepdims=True))).astype(BF)
-            r.dv[e % 2, :, at] = tn(probs.astype(BF), deltas).astype(BF)
-            r.dk[e % 2, :, at] = tn(low, queries).astype(BF)
+            r.dv[e % 2, at, :] = tn(deltas, probs.astype(BF)).astype(BF)
+            r.dk[e % 2, at, :] = tn(queries, low).astype(BF)
             r.dqe[:, at] = join_heads(nn(low, keys)).astype(BF)
 
-        loop(0, PAIRS, attend)
+        loop(0, PAIRS, attend, PAIRS)
         tick(2 * e + 1)
         for copy in out_copies(e):
             copy.start()
         r.sum[...] += tn(pick, r.dqe[...])
 
-        def dense(j):
-            at = lanes(j, 256)
-            r.dwsum[0, at, :] += tn(r.dk[e % 2, :, at], r.encv[e])
-            r.dwsum[1, at, :] += tn(r.dv[e % 2, :, at], r.encv[e])
-
-        loop(0, width // 256, dense)
-
     loop(0, examples, example)
     r.dq2[...] = r.sum[...].astype(BF)
-    r.dwkv[...] = r.dwsum[...].astype(BF)
     for e in (examples - 2, examples - 1):
         for copy in out_copies(e):
             copy.wait()
@@ -737,14 +782,14 @@
         p = Place()
 
         def parts(u, c, y):
-            at = slice(y * WIDE, (y + 1) * WIDE)
-            if u < 2:
-                return r.dwkv.at[u, :, :, c, :, at]
-            if u == 2:
+            at = pl.ds(pl.multiple_of(y * WIDE, WIDE), WIDE)
+            if u == 0:
+                return r.dfi.at[:, :, c, 3, :, at]
+            if u == 1:
                 return r.dwoc.at[:, :, c, :, at]
-            return r.dw.at[u - 3, :, :, c, :, at]
-
-        s = Scatter(p, parts, r)
+            return r.dw.at[u - 2, :, :, c, :, at]
+
+        s = Scatter(p, parts, 2, r)
         greet(p.near())
         step = s.step
     else:
@@ -758,33 +803,51 @@
 
     halves = width // WIDE
     examples = r.denc.shape[0]
-    loads = [local(r.sq.at[m], r.w.at[m], r.wsem.at[m]) for m in range(7)]
+    loads = [local(r.sq.at[2 + m], r.w.at[m], r.wsem.at[m]) for m in range(5)]
+    late = [local(r.sq.at[m], r.w.at[3 + m], r.wsem.at[5 + m]) for m in range(2)]
     for copy in loads:
         copy.start()
 
-    def fetches(e):
-        return [
-            local(r.dk2.at[e], r.dkv.at[e % 2, 0], r.esem.at[e % 2, 0]),
-            local(r.dv2.at[e], r.dkv.at[e % 2, 1], r.esem.at[e % 2, 1]),
-        ]
+    passes = ((r.dk2, r.enc), (r.dv2, r.enc), (r.dk2, r.dv2))
+
+    def fetches(number, e):
+        places = (r.one, r.three if number == 2 else r.two)
+        return [local(passes[number][i].at[e], places[i].at[e % 2], r.esem.at[e % 2, i]) for i in (0, 1)]
+
+    def pass_step(number, e, act):
+        for copy in fetches(number, e):
+            copy.wait()
+        act(e)
+
+        @pl.when(e + 2 < examples)
+        def _():
+            for copy in fetches(number, e + 2):
+                copy.start()
+
+        if number < 2:
+
+            @pl.when(e + 2 >= examples)
+            def _():
+                for copy in fetches(number + 1, e + 2 - examples):
+                    copy.start()
 
     def out_copy(e):
         return local(r.denv.at[e % 2], r.denc.at[e], r.dsem.at[e % 2])
 
     for e in (0, 1):
-        for copy in fetches(e):
+        for copy in fetches(0, e):
             copy.start()
-    step(0, 0, 1, 2)
+    step(0, 0, 1)
     for j in range(halves):
         at = slice(WIDE * j, WIDE * (j + 1))
         put(0, j, tn(r.dq2[:, at], r.n2[...]))
-    step(0, 3)
+    step(0, 2)
     for copy in loads:
         copy.wait()
 
     def query(j):
         at = lanes(j, 256)
-        r.back[:, at] = nn(r.dq2[...], w_lanes(r.w, 6, at))
+        r.back[:, at] = nn(r.dq2[...], w_lanes(r.w, 4, at))
 
     loop(0, thirds, query)
     step(1, 0, 1)
@@ -795,14 +858,16 @@
     for j in range(halves):
         at = slice(WIDE * j, WIDE * (j + 1))
         put(1, j, tn(r.b1[:, at], r.a1[...]))
-    step(0, 4)
-    step(1, 2, 3)
+    step(0, 3)
+    step(1, 2)
 
     def out(j):
         at = lanes(j, 256)
-        r.da1[:, at] = nn(r.b1[...], w_lanes(r.w, 5, at)).astype(BF)
+        r.da1[:, at] = nn(r.b1[...], w_lanes(r.w, 3, at)).astype(BF)
 
     loop(0, thirds, out)
+    for copy in late:
+        copy.start()
     self_masks(r.lengths[...], r.mask)
     a = lax.broadcasted_iota(jnp.int32, (MOST, MOST), 0)
     b = lax.broadcasted_iota(jnp.int32, (MOST, MOST), 1)
@@ -825,11 +890,11 @@
             dscores = probs * (dprobs - jnp.sum(dprobs * probs, axis=-1, keepdims=True))
             low = dscores.astype(BF)
             skewed = skewed + dscores
-            r.dvsum[band, :] += tn(probs.astype(BF), deltas)
-            r.dksum[band, :] += tn(low, queries)
+            r.dvsum[:, band] += tn(deltas, probs.astype(BF))
+            r.dksum[:, band] += tn(queries, low)
             r.dq[own, at] = join_heads(nn(low, keys)).astype(BF)
-        r.dk[:, at] = r.dksum[MOST:, :].astype(BF)
-        r.dv[:, at] = r.dvsum[MOST:, :].astype(BF)
+        r.dk[at, :] = r.dksum[:, MOST:].astype(BF)
+        r.dv[at, :] = r.dvsum[:, MOST:].astype(BF)
         for h in range(2):
             flipped = jnp.dot(
                 flip,
@@ -841,12 +906,12 @@
             r.distsum[pl.ds(2 * pair + h, 1), :] = jnp.sum(straight, axis=0, keepdims=True)
 
     plan = {
-        0: ((2, 0, 1), (1, 4)),
-        1: ((2, 2, 3),),
-        2: ((3, 0, 1), (2, 4)),
-        3: ((3, 2, 3),),
-        4: ((4, 0, 1), (3, 4)),
-        5: ((4, 2, 3),),
+        0: ((1, 3),),
+        1: ((2, 0, 1),),
+        2: ((2, 2),),
+        3: ((3, 0, 1), (2, 3)),
+        4: ((3, 2),),
+        5: ((4, 0, 1), (3, 3)),
     }
 
     def attend_tick(pair):
@@ -861,24 +926,28 @@
         attend(pair)
 
     loop(0, PAIRS, attend_tick)
-    step(4, 4)
+    step(4, 2)
     for m, ref in ((2, r.dq), (3, r.dk), (4, r.dv)):
         for j in range(halves):
             at = slice(WIDE * j, WIDE * (j + 1))
-            put(m, j, tn(ref[:, at], r.n1[...]))
-        step(0, 3 + m)
-    step(1, 5, 6)
+            put(m, j, tn(ref[:, at], r.n1[...]) if m == 2 else nn(ref[at, :], r.n1[...]))
+        step(0, 2 + m)
+    step(4, 3)
+    step(1, 4, 5)
+
+    r.b1[...] = r.dk[...].T
+    r.da1[...] = r.dv[...].T
 
     def qkv(j):
         at = lanes(j, 256)
         r.back[:, at] = (
-            nn(r.dq[...], w_lanes(r.w, 2, at))
-            + nn(r.dk[...], w_lanes(r.w, 3, at))
-            + nn(r.dv[...], w_lanes(r.w, 4, at))
+            nn(r.dq[...], w_lanes(r.w, 0, at))
+            + nn(r.b1[...], w_lanes(r.w, 1, at))
+            + nn(r.da1[...], w_lanes(r.w, 2, at))
         )
 
-    loop(0, thirds, qkv)
-    step(1, 7)
+    loop(0, thirds, qkv, thirds)
+    step(1, 6)
     dz, dw = rms_back(r.x[...].astype(F32), r.gains[0:1, :], r.back[...])
     r.gain[0:1, :] = dw
     r.dx[...] = (r.dh1[...] + dz).astype(BF)
@@ -890,68 +959,83 @@
     r.small[2:3, :] = r.gain3[...]
     r.small[3 : 3 + HEADS, 0:BUCKETS] = by_bucket
 
+    if comm:
+        pairs = [p.at(c=1 - p.c), p.at(y=1 - p.y), p.at(x=1 - p.x),
+                 p.at(z=p.z + 1 - 2 * (p.z % 2)), p.at(z=(p.z + 2) % 4)]
+
+        def share(i):
+            return remote(r.given.at[i], r.gotten.at[i], r.smsem.at[0, i], r.smsem.at[1, i], pairs[i])
+
+        def share_go(i):
+            r.given[i] = r.small[...]
+            share(i).start()
+
+        def share_end(i):
+            share(i).wait_recv()
+            r.small[...] = r.small[...] + r.gotten[i]
+
+        share_go(0)
+
+    def passing(number, act, events):
+        def one(e):
+            pass_step(number, e, act)
+            if comm:
+                for at, happens in events.items():
+                    pl.when(e == at)(functools.partial(quiet, happens))
+
+        loop(0, examples, one)
+
+    def weight_sum(e):
+        def dense(j):
+            at = lanes(j, 256)
+            r.dwsum[at, :] = nn(r.one[e % 2, at, :], r.two[e % 2]) + jnp.where(e == 0, 0.0, r.dwsum[at, :])
+
+        loop(0, thirds, dense, thirds)
+
+    def share_next(i):
+        share_end(i)
+        share_go(i + 1)
+
+    events = (
+        {0: lambda: share_next(0), 1: lambda: step(2, 4), 2: lambda: step(2, 5), 4: lambda: step(2, 6),
+         5: lambda: step(3, 4), 6: lambda: (step(3, 5), share_next(1)), 7: lambda: step(3, 6)},
+        {1: lambda: (step(1, 7), step(4, 4)), 2: lambda: step(4, 5), 3: lambda: share_next(2),
+         4: lambda: step(4, 6), 5: lambda: step(2, 7), 7: lambda: share_next(3)},
+        {0: lambda: step(3, 7), 1: lambda: step(1, 8), 3: lambda: step(4, 7), 4: lambda: share_end(4),
+         5: lambda: step(2, 8), 7: lambda: step(3, 8)},
+    )
+
+    r.dwsum[...] = jnp.zeros_like(r.dwsum)
+    passing(0, weight_sum, events[0])
+    for j in range(halves):
+        put(5, j, r.dwsum[WIDE * j : WIDE * (j + 1), :])
+    step(0, 7)
+    passing(1, weight_sum, events[1])
+    for j in range(halves):
+        put(6, j, r.dwsum[WIDE * j : WIDE * (j + 1), :])
+    step(0, 8)
+    for copy in late:
+        copy.wait()
+
     def encoder(e):
-        for copy in fetches(e):
-            copy.wait()
-
         @pl.when(e >= 2)
         def _():
             out_copy(e - 2).wait()
 
+        r.b1[...] = r.one[e % 2].T
+        r.da1[...] = r.three[e % 2].T
+
         def dense(j):
             at = lanes(j, 256)
             r.denv[e % 2, :, at] = (
-                nn(r.dkv[e % 2, 0], w_lanes(r.w, 0, at)) + nn(r.dkv[e % 2, 1], w_lanes(r.w, 1, at))
+                nn(r.b1[...], w_lanes(r.w, 3, at)) + nn(r.da1[...], w_lanes(r.w, 4, at))
             ).astype(BF)
 
-        loop(0, thirds, dense)
+        loop(0, thirds, dense, thirds)
         out_copy(e).start()
 
-        @pl.when(e + 2 < examples)
-        def _():
-            for copy in fetches(e + 2):
-                copy.start()
-
-    if comm:
-        pairs = [p.at(c=1 - p.c), p.at(y=1 - p.y), p.at(x=1 - p.x),
-                 p.at(z=p.z + 1 - 2 * (p.z % 2)), p.at(z=(p.z + 2) % 4)]
-
-        def share(i):
-            return remote(r.given.at[i], r.gotten.at[i], r.smsem.at[0, i], r.smsem.at[1, i], pairs[i])
-
-        def share_go(i):
-            r.given[i] = r.small[...]
-            share(i).start()
-
-        def share_end(i):
-            share(i).wait_recv()
-            r.small[...] = r.small[...] + r.gotten[i]
-
-        share_go(0)
-        loop(0, 2, encoder)
-        share_end(0)
-        share_go(1)
-        step(2, 6, 5)
-        loop(2, 3, encoder)
-        step(2, 7)
-        loop(3, 4, encoder)
-        share_end(1)
-        share_go(2)
-        step(3, 6, 5)
-        loop(4, 5, encoder)
-        share_end(2)
-        share_go(3)
-        loop(5, 6, encoder)
-        step(3, 7)
-        loop(6, 7, encoder)
-        share_end(3)
-        share_go(4)
-        step(4, 6, 5)
-        loop(7, examples, encoder)
-        share_end(4)
-        step(4, 7)
-    else:
-        loop(0, examples, encoder)
+    passing(2, encoder, events[2])
+    step(4, 8)
     for e in (examples - 2, examples - 1):
         out_copy(e).wait()
     if not comm:
@@ -963,9 +1047,11 @@
         low, high = ref[0:n, :, :192], ref[0:n, :, 192:]
         return jnp.where(first, low, high), jnp.where(first, high, low)
 
-    keep_sq, r.give[0:8] = split(r.fin, 8)
-    keep_fi, r.give[8:12] = split(r.finf, 4)
-    r.giveo[...] = r.finf[pl.ds(4 + 2 * (1 - p.c), 2)]
+    r.all[0:8] = r.fin[1:9]
+    r.all[8:11] = r.finf[2:5]
+    r.all[11] = r.fin[0]
+    keep, r.give[...] = split(r.all, 12)
+    r.giveo[...] = jnp.where(first, r.finf[0:2], r.fing[...])
     sib = p.at(c=1 - p.c)
     trade = [
         remote(r.give, r.take, r.xsem.at[0], r.xsem.at[1], sib),
@@ -979,9 +1065,9 @@
     def both(a, b, axis):
         return jnp.concatenate([jnp.where(first, a, b), jnp.where(first, b, a)], axis=axis)
 
-    r.tsq[...] = both(keep_sq, r.take[0:8], 1)
-    r.tfi[...] = both(keep_fi.reshape(192, 192), r.take[8:12].reshape(192, 192), 0)
-    own = r.finf[pl.ds(4 + 2 * p.c, 2)]
+    r.tsq[...] = both(keep[0:8], r.take[0:8], 1)
+    r.tfi[...] = both(keep[8:12].reshape(192, 192), r.take[8:12].reshape(192, 192), 0)
+    own = jnp.where(first, r.fing[...], r.finf[0:2])
     r.tfo[...] = both(
         jnp.concatenate([own[0], own[1]], axis=1), jnp.concatenate([r.takeo[0], r.takeo[1]], axis=1), 0
     )
@@ -1011,8 +1097,9 @@
     for copy in ins:
         copy.start()
     r.dx[...] = r.dx_in[...]
+    r.out[...] = r.out_in[...]
     e192 = eye(192)
-    for m, ref in enumerate((r.k_c, r.v_c, r.o_c, r.q_c, r.o_s, r.q_s, r.k_s, r.v_s)):
+    for m, ref in enumerate((r.o_c, r.q_c, r.o_s, r.q_s, r.k_s, r.v_s, r.k_c, r.v_c)):
         ref[...] = nt(e192, r.tsq[m])
     r.f_i[...] = nt(e192, r.tfi[...])
     r.f_o[...] = r.tfo[...].astype(F32)
@@ -1097,8 +1184,8 @@
             scratch | dict(
                 xt=VM((12, 2, PIECE, 192), BF), xf=VM((2, PIECE, 768), BF), took=VM((12, PIECE, 192), BF),
                 tookf=VM((PIECE, 768), BF), own=VM((UNITS, PIECE, WIDE), BF), gt=VM((8, 8, 128), F32),
-                tt=VM((4, 8, 128), F32), xsem=dma(4), psem=dma(UNITS), smsem=dma(2, 10),
-                ssem=dma(UNITS, 10), rsem=dma(UNITS, 10)),
+                tt=VM((4, 8, 128), F32), xsem=dma(6), psem=dma(UNITS), smsem=dma(2, 10),
+                ssem=dma(UNITS, 14), rsem=dma(UNITS, 14)),
             "forward", collective=0,
         )
         sq, fi, fo, gains, dist = fwd.sq, fwd.fi, fwd.fo, fwd.gains, fwd.dist
@@ -1120,60 +1207,65 @@
         )
 
     feed = run(
-        feed_kernel,
+        functools.partial(feed_kernel, comm),
         dict(a2=fwd.a2, h1=fwd.h1, c=upstream, gains=gains,
              w=(sq.reshape(8, width, width), pl.BlockSpec((1, width, width), lambda _: (7, 0, 0))),
              fi=fi.reshape(hidden, width), fo=fo.reshape(width, hidden)),
-        dict(out=(small, BF), dfi=((hidden, width), BF), dfo=((width, hidden), BF),
-             dwoc=((width, width), BF), da2=(small, BF), dh2=(small, F32), gain=((1, width), F32)),
-        dict(h2=VM(small, F32), n3=VM(small, BF), sum=VM(small, F32), back=VM(small, F32)),
-        "feed",
+        dict(out=(small, BF), dfi=((hidden, width), BF), dfo=((4, 2, 2, PIECE, hidden), BF),
+             dwoc=((width, width), BF), da2=(small, BF), dh2=(small, F32), gain=((1, width), F32))
+        | (dict(fin=((2, PIECE, WIDE), BF)) if comm else {}),
+        dict(h2=VM(small, F32), n3=VM(small, BF), sum=VM(small, F32), back=VM(small, F32),
+             ct=VM((width, rows), BF), g=VM(small, BF), du=VM(small, BF))
+        | (scatter_scratch(2, 1) if comm else {}),
+        "feed", collective=3 if comm else None,
     )
 
-    ins = dict(enc=(encoder_out, HBM), k2=(fwd.k2, HBM), v2=(fwd.v2, HBM), q2=fwd.q2, da2=feed.da2,
+    ins = dict(k2=(fwd.k2, HBM), v2=(fwd.v2, HBM), q2=fwd.q2, da2=feed.da2,
                **index)
-    outs = dict(dk2=(encoder_out.shape, BF, HBM), dv2=(encoder_out.shape, BF, HBM), dq2=(small, BF),
-                dwkv=((2, width, width), BF))
+    turned = (examples, width, keys_n)
+    outs = dict(dk2=(turned, BF, HBM), dv2=(turned, BF, HBM), dq2=(small, BF))
     scratch = dict(
-        encv=VM(encoder_out.shape, BF), k2v=VM(encoder_out.shape, BF), v2v=VM(encoder_out.shape, BF),
+        k2v=VM(encoder_out.shape, BF), v2v=VM(encoder_out.shape, BF),
         qe=VM((MOST, width), BF), dae=VM((MOST, width), BF), dqe=VM((MOST, width), BF),
-        dk=VM((2, keys_n, width), BF), dv=VM((2, keys_n, width), BF),
-        sum=VM(small, F32), dwsum=VM((2, width, width), F32), esem=dma(examples, 3), dsem=dma(2, 2),
+        dk=VM((2, width, keys_n), BF), dv=VM((2, width, keys_n), BF),
+        sum=VM(small, F32), esem=dma(examples, 2), dsem=dma(2, 2),
         **index_scratch,
     )
     fins = {}
     if comm:
-        ins |= dict(dfi=(feed.dfi.reshape(4, 2, 2, 4, PIECE, width), HBM),
-                    dfo=(feed.dfo.reshape(4, 2, 2, PIECE, hidden), HBM))
-        fins = dict(fin=((8, PIECE, WIDE), BF))
-        scratch |= scatter_scratch(8)
+        dfi = feed.dfi.reshape(4, 2, 2, 4, PIECE, width)
+        ins |= dict(dfi=(dfi, HBM),
+                    dfo=(feed.dfo, HBM))
+        fins = dict(fin=((5, PIECE, WIDE), BF))
+        scratch |= scatter_scratch(5, 5)
     mid = run(functools.partial(cross_back_kernel, comm), ins, outs | fins, scratch, "cross_back",
               collective=1 if comm else None)
 
-    five = (5,) + cut if comm else (5, width, width)
+    seven = (7,) + cut if comm else (7, width, width)
     ins = dict(dq2=mid.dq2, n2=fwd.n2, h1=fwd.h1, dh2=feed.dh2, x=decoder_in, n1=fwd.n1, q1=fwd.q1,
                k1=fwd.k1, v1=fwd.v1, a1=fwd.a1, gains=gains, dist=dist, gain3=feed.gain,
-               sq=(sq, HBM), dk2=(mid.dk2, HBM), dv2=(mid.dv2, HBM), lengths=decoder_lengths)
+               sq=(sq, HBM), enc=(encoder_out, HBM), dk2=(mid.dk2, HBM), dv2=(mid.dv2, HBM), lengths=decoder_lengths)
     outs = dict(dx=(small, BF), small=((16, width), F32), denc=(encoder_out.shape, BF, HBM))
     scratch = dict(
         mask=VM((rows // MOST, MOST, 2 * MOST), F32), dh1=VM(small, F32), b1=VM(small, BF),
-        da1=VM(small, BF), dq=VM(small, BF), dk=VM(small, BF), dv=VM(small, BF),
-        dksum=VM((rows + MOST, 128), F32), dvsum=VM((rows + MOST, 128), F32), back=VM(small, F32),
-        gain=VM((2, width), F32), distsum=VM((HEADS, 2 * MOST), F32), w=VM((7,) + cut, BF),
-        dkv=VM((2, 2, keys_n, width), BF), denv=VM((2, keys_n, width), BF), wsem=dma(7), esem=dma(2, 2),
+        da1=VM(small, BF), dq=VM(small, BF), dk=VM((width, rows), BF), dv=VM((width, rows), BF),
+        dksum=VM((128, rows + MOST), F32), dvsum=VM((128, rows + MOST), F32), back=VM(small, F32),
+        gain=VM((2, width), F32), distsum=VM((HEADS, 2 * MOST), F32), w=VM((5,) + cut, BF),
+        one=VM((2, width, keys_n), BF), two=VM((2, keys_n, width), BF), three=VM((2, width, keys_n), BF),
+        dwsum=VM((width, width), F32), denv=VM((2, keys_n, width), BF), wsem=dma(7), esem=dma(2, 2),
         dsem=dma(2),
     )
     if comm:
-        ins |= dict(dwkv=(mid.dwkv.reshape((2,) + cut), HBM), dwoc=(feed.dwoc.reshape(cut), HBM), finf=mid.fin)
+        ins |= dict(dfi=(dfi, HBM), dwoc=(feed.dwoc.reshape(cut), HBM), finf=mid.fin, fing=feed.fin)
         outs |= dict(tsq=((8, 96, 192), BF), tfi=((384, 192), BF), tfo=((96, 768), BF), gains_own=((8, 128), F32),
                      table_own=((8, HEADS), F32))
         scratch |= dict(
-            dw=VM(five, BF), fin=VM((8, PIECE, WIDE), BF), give=VM((12, PIECE, 192), BF),
+            dw=VM(seven, BF), fin=VM((9, PIECE, WIDE), BF), all=VM((12, PIECE, WIDE), BF), give=VM((12, PIECE, 192), BF),
             take=VM((12, PIECE, 192), BF), giveo=VM((2, PIECE, WIDE), BF), takeo=VM((2, PIECE, WIDE), BF),
             given=VM((5, 16, width), F32), gotten=VM((5, 16, width), F32), smsem=dma(2, 5), xsem=dma(4),
-        ) | scatter_scratch(8)
+        ) | scatter_scratch(9, 2)
     else:
-        outs |= dict(dw=(five, BF))
+        outs |= dict(dw=(seven, BF))
     last = run(functools.partial(self_back_kernel, comm), ins, outs, scratch, "self_back",
                collective=2 if comm else None)
 
@@ -1182,30 +1274,30 @@
         done = run(
             finish_kernel,
             dict(tsq=last.tsq, tfi=last.tfi, tfo=last.tfo, gains_in=last.gains_own, table_in=last.table_own,
-                 dx_in=last.dx, denc_in=(last.denc, HBM)),
+                 dx_in=last.dx, out_in=feed.out, denc_in=(last.denc, HBM)),
             {n: square for n in ("k_c", "v_c", "q_s", "k_s", "v_s", "o_s", "q_c", "o_c")}
             | dict(f_i=((192, 384), F32), f_o=((96, 768), F32), gains=((3, 96), F32), table=((8, HEADS), F32),
-                   dx=(small, BF), denc=(encoder_out.shape, BF, HBM)),
+                   dx=(small, BF), out=(small, BF), denc=(encoder_out.shape, BF, HBM)),
             dict(sem=dma(examples, 2), hold=VM(encoder_out.shape, BF)), "finish",
         )
         grads = (done.q_s, done.k_s, done.v_s, done.o_s, done.q_c, done.k_c, done.v_c, done.o_c,
                  done.f_i, done.f_o.T)
-        gains_delta, table_delta, dx, denc = done.gains, done.table, done.dx, done.denc
+        gains_delta, table_delta, dx, denc, out = done.gains, done.table, done.dx, done.denc, done.out
     else:
         def owned(t, rows_axis=0):
             t = lax.psum_scatter(t, "dp", scatter_dimension=1, tiled=True)
             return lax.psum_scatter(t, "fsdp", scatter_dimension=0, tiled=True).astype(F32).T
 
         dw = last.dw
-        grads = tuple(owned(t) for t in (dw[2], dw[3], dw[4], dw[1], dw[0], mid.dwkv[0], mid.dwkv[1],
-                                         feed.dwoc, feed.dfi, feed.dfo))
+        grads = tuple(owned(t) for t in (dw[2], dw[3], dw[4], dw[1], dw[0], dw[5], dw[6],
+                                         feed.dwoc, feed.dfi, feed.dfo.reshape(width, hidden)))
         gains_delta = lax.psum(last.small[0:3], "dp")
         gains_delta = lax.psum_scatter(gains_delta, "fsdp", scatter_dimension=1, tiled=True)
         table_delta = last.small[3 : 3 + HEADS, 0:BUCKETS].T
         table_delta = lax.psum_scatter(table_delta, "dp", scatter_dimension=0, tiled=True)
         table_delta = lax.psum(table_delta, "fsdp")
-        dx, denc = last.dx, last.denc
-    return (feed.out, dx, denc, gains_delta, table_delta) + grads
+        dx, denc, out = last.dx, last.denc, feed.out
+    return (out, dx, denc, gains_delta, table_delta) + grads
 
 
 def solution(mesh):

time: 331 us -> 315 us (0.952)
  Pallas kernels: 327 us -> 308 us
    pallas_call x5, Pallas kernels: 327 us -> 308 us  [run(): pl.pallas_call(wrapped, grid=(1,), in_specs=specs, out_specs=[pl.BlockSpe...]
where the time goes in v5:
time: 315 us; the launch traced here: 309 us
  Pallas kernels  308 us (98%)
    pallas_call x5, Pallas kernels, run(): pl.pallas_call(wrapped, grid=(1,), in_specs=specs, out_specs=[pl.BlockSpe...  308 us

profile of v5, /device:TPU:1, one launch (start us, length us, event | category | flops | bytes accessed | tf_op | source)
XLA Modules:
  0.0 309.2 jit_solution(250899582726523211)
XLA Ops:
  0.7 111.9 %forward.1 = (bf16[512,768]{1,0:T(8,128)(2,1)}, bf16[512,768]{1,0:T(8,128)(2,1)}, bf16[640,768]{1,0:T(8,128)(2,1)}, bf16[640,768]{1,0:T(8,128)(2,1)}, bf16[512,7...) custom-call(bf16[512,768]{1,0:T(8,128)(2,1)} %refs_4_.5, ...), custom_call_target="tpu_custom_call" | custom-call | bytes 20000000 | tf_op jit(solution)/shard_map/forward/pallas_call | solution.py:1130
  112.5 42.3 %feed.1 = (bf16[512,768]{1,0:T(8,128)(2,1)}, bf16[3072,768]{1,0:T(8,128)(2,1)}, bf16[4,2,2,48,3072]{4,3,2,1,0:T(8,128)(2,1)}, bf16[768,768]{1,0:T(8,128)(2,1)}, ...) custom-call(bf16[512,768]{1,0:T(8,128)(2,1)} %get-tuple-element.68.refs_0_, ...), custom_call_target="tpu_custom_call" | custom-call | bytes 20000000 | tf_op jit(solution)/shard_map/feed/pallas_call | solution.py:1130
  154.9 51.3 %cross_back.1 = (bf16[8,768,512]{2,1,0:T(8,128)(2,1)}, bf16[8,768,512]{2,1,0:T(8,128)(2,1)}, bf16[512,768]{1,0:T(8,128)(2,1)}, bf16[5,48,384]{2,1,0:T(8,128)(2,1)}) custom-call(bf16[8,512,768]{2,1,0:T(8,128)(2,1)} %get-tuple-element.65.refs_0_, bf16[8,512,768]{2,1,0:T(8,128)(2,1)} %get-tuple-element.66.refs_1_, bf16[512,768]{1,0:T(8,128)(2,1)} %get-tuple-element.67.refs_2_, ...), custom_call_target="tpu_custom_call" | custom-call | bytes 20000000 | tf_op jit(solution)/shard_map/cross_back/pallas_call | solution.py:1130
  206.2 93.8 %self_back.1 = (bf16[512,768]{1,0:T(8,128)(2,1)}, f32[16,768]{1,0:T(8,128)}, bf16[8,512,768]{2,1,0:T(8,128)(2,1)}, bf16[8,96,192]{2,1,0:T(8,128)(2,1)}, bf16[384...) custom-call(bf16[512,768]{1,0:T(8,128)(2,1)} %get-tuple-element.77.refs_0_, ...), custom_call_target="tpu_custom_call" | custom-call | bytes 20000000 | tf_op jit(solution)/shard_map/self_back/pallas_call | solution.py:1130
  299.9 8.8 %finish.1 = (f32[192,96]{1,0:T(8,128)}, f32[192,96]{1,0:T(8,128)}, f32[192,96]{1,0:T(8,128)}, f32[192,96]{1,0:T(8,128)}, f32[192,96]{1,0:T(8,128)}, /*index=5*/f...) custom-call(bf16[8,96,192]{2,1,0:T(8,128)(2,1)} %get-tuple-element.9, ...), custom_call_target="tpu_custom_call" | custom-call | bytes 20000000 | tf_op jit(solution)/shard_map/finish/pallas_call | solution.py:1130
